TPU v7x, 32 devices: a whole 2x2x4 slice. The times are simulated.
32 devices in a mesh: batch: 8 (over y, x, core), chan: 4 (over z).
Axes of the slice: x: 2, y: 2, z: 4, core: 2. Of those that a mesh axis runs over, the one named last changes fastest.
Arguments:
- input_long: float32 [16, 512, 768], P('batch', None, 'chan'), may hold values from -25 to 25, as said below
- input_short: float32 [32, 128, 768], P('batch', None, 'chan'), may hold values from -25 to 25, as said below
- length_long: int32 [16], P('batch'), may hold values from 128 to 512, as said below
- length_short: int32 [32], P('batch'), may hold values from 32 to 128, as said below
- gain_mixer: float32 [2, 768], P(None, 'chan'), may hold values from 0.5 to 1.5
- weight_in: bfloat16 [2, 768, 3, 768], P(None, None, None, 'chan'), may hold values from -0.21875 to 0.21875
- short_taps: float32 [2, 3, 3, 768], P(None, None, None, 'chan'), may hold values from -4 to 4
- cond_taps: float32 [2, 3, 768], P(None, None, 'chan'), may hold values from -4 to 4
- static_filter: float32 [2, 512, 768], P(None, None, 'chan'), may hold values from -0.25 to 0.25
- weight_out: bfloat16 [2, 768, 768], P(None, 'chan'), may hold values from -0.21875 to 0.21875
- gain_mlp: float32 [2, 768], P(None, 'chan'), may hold values from 0.5 to 1.5
- weight_up: bfloat16 [2, 768, 2, 3072], P(None, None, None, 'chan'), may hold values from -0.21875 to 0.21875
- weight_down: bfloat16 [2, 3072, 768], P(None, 'chan'), may hold values from -0.109375 to 0.109375
- grad_long: float32 [16, 512, 768], P('batch', None, 'chan'), may hold values from -6 to 6
- grad_short: float32 [32, 128, 768], P('batch', None, 'chan'), may hold values from -6 to 6
Outputs:
- output_long: float32 [16, 512, 768], P('batch', None, 'chan')
- output_short: float32 [32, 128, 768], P('batch', None, 'chan')
- input_grad_long: float32 [16, 512, 768], P('batch', None, 'chan')
- input_grad_short: float32 [32, 128, 768], P('batch', None, 'chan')
- gain_mixer_grad: float32 [2, 768], P(None, 'chan')
- weight_in_grad: float32 [2, 768, 3, 768], P(None, None, None, 'chan')
- short_taps_grad: float32 [2, 3, 3, 768], P(None, None, None, 'chan')
- cond_taps_grad: float32 [2, 3, 768], P(None, None, 'chan')
- static_filter_grad: float32 [2, 512, 768], P(None, None, 'chan')
- weight_out_grad: float32 [2, 768, 768], P(None, 'chan')
- gain_mlp_grad: float32 [2, 768], P(None, 'chan')
- weight_up_grad: float32 [2, 768, 2, 3072], P(None, None, None, 'chan')
- weight_down_grad: float32 [2, 3072, 768], P(None, 'chan')
Inputs may be any that keep to these rules, and one draw needn't show every extreme that they name: `input_long`: activations of each token, with feature scales that differ over the features. `input_short`: activations of each token, with feature scales that differ over the features. `length_long`: positions at and after a sequence's length are padding; in every draw some long sequence is full. `length_short`: positions at and after a sequence's length are padding; in every draw some short sequence is full.
All inputs are finite; a program needn't handle non-finite values.
Results may differ from a plain program's by a relative error of at most 0.03.
Values may be sent and summed in bfloat16 or wider, within the bound.
No kernel may reach another device: no remote copies, remote signals or barrier semaphores. Data moves between devices by JAX's collectives and lax.ppermute only.
A program may use at most 256 MiB of HBM per device.

v0:
```python
import math

import jax
import jax.numpy as jnp
from jax import lax
from jax.sharding import PartitionSpec as P

EPS = 1e-05
HIGH = lax.Precision.HIGHEST


def causal_taps(values, taps):
    length = values.shape[1]
    padded = jnp.pad(values, ((0, 0), (2, 0)) + ((0, 0),) * (values.ndim - 2))
    return (
        taps[0] * padded[:, 2:] + taps[1] * padded[:, 1 : length + 1] + taps[2] * padded[:, :length]
    )


def dft_tables(length):
    freqs = jnp.arange(length + 1, dtype=jnp.int32)[:, None]
    places = jnp.arange(length, dtype=jnp.int32)[None, :]
    phase = (freqs * places % (2 * length)).astype(jnp.float32) * (math.pi / length)
    return (jnp.cos(phase), jnp.sin(phase))


def forward_dft(cosines, sines, values):
    real_part = jnp.einsum("fn,bnc->bfc", cosines, values, precision=HIGH)
    imag_part = -jnp.einsum("fn,bnc->bfc", sines, values, precision=HIGH)
    return (real_part, imag_part)


def mix_shape(projected, lengths, short_taps, cond_taps, static_filter):
    length = projected.shape[1]
    conv = causal_taps(projected, short_taps)
    query = conv[:, :, 0]
    key_part = conv[:, :, 1]
    value_part = conv[:, :, 2]
    live = (jnp.arange(length)[None, :] < lengths[:, None]).astype(jnp.float32)
    gated = key_part * value_part * live[:, :, None]
    shaped = causal_taps(gated, cond_taps)
    cosines, sines = dft_tables(length)
    shaped_re, shaped_im = forward_dft(cosines, sines, shaped)
    magnitude = (
        jnp.sqrt(shaped_re * shaped_re + shaped_im * shaped_im + length) / math.sqrt(length) - 1.0
    )
    fixed_re = jnp.dot(cosines, static_filter[:length], precision=HIGH)
    fixed_im = -jnp.dot(sines, static_filter[:length], precision=HIGH)
    filter_re = fixed_re + magnitude
    signal_re, signal_im = forward_dft(cosines, sines, gated)
    product_re = filter_re * signal_re - fixed_im * signal_im
    product_im = filter_re * signal_im + fixed_im * signal_re
    freqs = jnp.arange(length + 1)
    edges = (freqs == 0) | (freqs == length)
    weight_re = jnp.where(edges, 1.0, 2.0).astype(jnp.float32) / (2.0 * length)
    weight_im = jnp.where(edges, 0.0, 2.0).astype(jnp.float32) / (2.0 * length)
    long_out = jnp.einsum("fn,bfc->bnc", cosines * weight_re[:, None], product_re, precision=HIGH)
    long_out = long_out - jnp.einsum(
        "fn,bfc->bnc", sines * weight_im[:, None], product_im, precision=HIGH
    )
    return query * long_out


def gated_unit(gate_up):
    halves = gate_up.reshape(gate_up.shape[0], 2, -1)
    return jax.nn.gelu(halves[:, 0], approximate=True) * halves[:, 1]


def project_in(values, gain, full_width):
    totals, squares = lax.psum(
        (jnp.sum(values, axis=1, keepdims=True), jnp.sum(values * values, axis=1, keepdims=True)),
        "chan",
    )
    average = totals / full_width
    inv_std = lax.rsqrt(squares / full_width - average * average + EPS)
    normal_rows = (values - average) * inv_std
    normed = lax.all_gather((normal_rows * gain).astype(jnp.bfloat16), "chan", axis=1, tiled=True)
    stored = (normal_rows, inv_std, gain)
    return (normed, stored)


def norm_back(partial_rows, stored, full_width):
    local = lax.psum_scatter(
        partial_rows.astype(jnp.bfloat16), "chan", scatter_dimension=1, tiled=True
    ).astype(jnp.float32)
    normal_rows, inv_std, gain = stored
    scaled = local * gain
    totals, crossed = lax.psum(
        (
            jnp.sum(scaled, axis=1, keepdims=True),
            jnp.sum(scaled * normal_rows, axis=1, keepdims=True),
        ),
        "chan",
    )
    grad_local = inv_std * (scaled - totals / full_width - normal_rows * crossed / full_width)
    gain_grad = jnp.sum(local * normal_rows, axis=0)
    return (grad_local, gain_grad)


def branch_out(values, weight):
    partial_rows = jnp.dot(values, weight, preferred_element_type=jnp.float32)
    return lax.psum_scatter(
        partial_rows.astype(jnp.bfloat16), "chan", scatter_dimension=1, tiled=True
    ).astype(jnp.float32)


def branch_back(grad_local):
    return lax.all_gather(grad_local.astype(jnp.bfloat16), "chan", axis=1, tiled=True)


def on_device(
    input_long,
    input_short,
    length_long,
    length_short,
    gain_mixer,
    weight_in,
    short_taps,
    cond_taps,
    static_filter,
    weight_out,
    gain_mlp,
    weight_up,
    weight_down,
    grad_long,
    grad_short,
):
    count_long, seq_long, chan_width = input_long.shape
    count_short, seq_short = (input_short.shape[0], input_short.shape[1])
    rows_long = count_long * seq_long
    layers = weight_in.shape[0]
    full_width = chan_width * lax.axis_size("chan")

    def mixer_all(proj_long, proj_short, taps_here, conds_here, static_here):
        return (
            mix_shape(proj_long, length_long, taps_here, conds_here, static_here),
            mix_shape(proj_short, length_short, taps_here, conds_here, static_here),
        )

    residual = jnp.concatenate(
        [input_long.reshape(rows_long, chan_width), input_short.reshape(-1, chan_width)], axis=0
    )
    stored_all = []
    for layer in range(layers):
        normed, norm_stored = project_in(residual, gain_mixer[layer], full_width)
        projected = jnp.dot(
            normed, weight_in[layer].reshape(full_width, -1), preferred_element_type=jnp.float32
        )
        proj_long = projected[:rows_long].reshape(count_long, seq_long, 3, chan_width)
        proj_short = projected[rows_long:].reshape(count_short, seq_short, 3, chan_width)
        mixed_long, mixed_short = mixer_all(
            proj_long, proj_short, short_taps[layer], cond_taps[layer], static_filter[layer]
        )
        mixed_rows = jnp.concatenate(
            [mixed_long.reshape(rows_long, chan_width), mixed_short.reshape(-1, chan_width)], axis=0
        ).astype(jnp.bfloat16)
        middle = residual + branch_out(mixed_rows, weight_out[layer])
        normed_mlp, mlp_stored = project_in(middle, gain_mlp[layer], full_width)
        gate_up = jnp.dot(
            normed_mlp, weight_up[layer].reshape(full_width, -1), preferred_element_type=jnp.float32
        )
        activated = gated_unit(gate_up).astype(jnp.bfloat16)
        residual = middle + branch_out(activated, weight_down[layer])
        stored_all.append(
            (
                normed,
                norm_stored,
                proj_long,
                proj_short,
                mixed_rows,
                normed_mlp,
                mlp_stored,
                gate_up,
                activated,
            )
        )
    upstream = jnp.concatenate(
        [grad_long.reshape(rows_long, chan_width), grad_short.reshape(-1, chan_width)], axis=0
    )
    layer_records = []
    for layer in reversed(range(layers)):
        (
            normed,
            norm_stored,
            proj_long,
            proj_short,
            mixed_rows,
            normed_mlp,
            mlp_stored,
            gate_up,
            activated,
        ) = stored_all[layer]
        coming = branch_back(upstream)
        grad_down = jnp.einsum("rf,rd->fd", activated, coming, preferred_element_type=jnp.float32)
        grad_act = jnp.einsum(
            "rd,fd->rf", coming, weight_down[layer], preferred_element_type=jnp.float32
        )
        unused, pull_unit = jax.vjp(gated_unit, gate_up)
        grad_gate_up = pull_unit(grad_act)[0].astype(jnp.bfloat16)
        grad_up_w = jnp.einsum(
            "rd,re->de", normed_mlp, grad_gate_up, preferred_element_type=jnp.float32
        ).reshape(weight_up.shape[1:])
        partial_mlp = jnp.einsum(
            "re,de->rd",
            grad_gate_up,
            weight_up[layer].reshape(full_width, -1),
            preferred_element_type=jnp.float32,
        )
        grad_in_mlp, grad_gain_mlp = norm_back(partial_mlp, mlp_stored, full_width)
        upstream = upstream + grad_in_mlp
        coming = branch_back(upstream)
        grad_out_w = jnp.einsum("rc,rd->cd", mixed_rows, coming, preferred_element_type=jnp.float32)
        grad_mixed = jnp.einsum(
            "rd,cd->rc", coming, weight_out[layer], preferred_element_type=jnp.float32
        )
        unused, pull_mix = jax.vjp(
            mixer_all,
            proj_long,
            proj_short,
            short_taps[layer],
            cond_taps[layer],
            static_filter[layer],
        )
        grad_proj_long, grad_proj_short, grad_taps, grad_cond, grad_static = pull_mix(
            (
                grad_mixed[:rows_long].reshape(count_long, seq_long, chan_width),
                grad_mixed[rows_long:].reshape(count_short, seq_short, chan_width),
            )
        )
        grad_proj = jnp.concatenate(
            [grad_proj_long.reshape(rows_long, -1), grad_proj_short.reshape(-1, 3 * chan_width)],
            axis=0,
        ).astype(jnp.bfloat16)
        grad_in_w = jnp.einsum(
            "rd,re->de", normed, grad_proj, preferred_element_type=jnp.float32
        ).reshape(weight_in.shape[1:])
        partial_mix = jnp.einsum(
            "re,de->rd",
            grad_proj,
            weight_in[layer].reshape(full_width, -1),
            preferred_element_type=jnp.float32,
        )
        grad_in_mix, grad_gain_mix = norm_back(partial_mix, norm_stored, full_width)
        upstream = upstream + grad_in_mix
        record = (
            grad_gain_mix,
            grad_in_w,
            grad_taps,
            grad_cond,
            grad_static,
            grad_out_w,
            grad_gain_mlp,
            grad_up_w,
            grad_down,
        )
        layer_records.insert(0, record)
    stacked = tuple(
        (jnp.stack([record[member] for record in layer_records]) for member in range(9))
    )
    stacked = (
        lax.psum(stacked[0].astype(jnp.bfloat16), "batch").astype(jnp.float32),
        lax.psum(stacked[1].astype(jnp.bfloat16), "batch").astype(jnp.float32),
        lax.psum(stacked[2].astype(jnp.bfloat16), "batch").astype(jnp.float32),
        lax.psum(stacked[3].astype(jnp.bfloat16), "batch").astype(jnp.float32),
        lax.psum(stacked[4].astype(jnp.bfloat16), "batch").astype(jnp.float32),
        lax.psum(stacked[5].astype(jnp.bfloat16), "batch").astype(jnp.float32),
        lax.psum(stacked[6].astype(jnp.bfloat16), "batch").astype(jnp.float32),
        lax.psum(stacked[7].astype(jnp.bfloat16), "batch").astype(jnp.float32),
        lax.psum(stacked[8].astype(jnp.bfloat16), "batch").astype(jnp.float32),
    )
    output_long = residual[:rows_long].reshape(count_long, seq_long, chan_width)
    output_short = residual[rows_long:].reshape(count_short, seq_short, chan_width)
    back_long = upstream[:rows_long].reshape(count_long, seq_long, chan_width)
    back_short = upstream[rows_long:].reshape(count_short, seq_short, chan_width)
    return (
        output_long,
        output_short,
        back_long,
        back_short,
        stacked[0],
        stacked[1],
        stacked[2],
        stacked[3],
        stacked[4],
        stacked[5],
        stacked[6],
        stacked[7],
        stacked[8],
    )


def solution(mesh):
    placed = (
        P("batch", None, "chan"),
        P("batch", None, "chan"),
        P("batch"),
        P("batch"),
        P(None, "chan"),
        P(None, None, None, "chan"),
        P(None, None, None, "chan"),
        P(None, None, "chan"),
        P(None, None, "chan"),
        P(None, "chan", None),
        P(None, "chan"),
        P(None, None, None, "chan"),
        P(None, "chan", None),
        P("batch", None, "chan"),
        P("batch", None, "chan"),
    )
    return jax.shard_map(
        on_device,
        mesh=mesh,
        in_specs=placed,
        out_specs=(
            P("batch", None, "chan"),
            P("batch", None, "chan"),
            P("batch", None, "chan"),
            P("batch", None, "chan"),
            P(None, "chan"),
            P(None, None, None, "chan"),
            P(None, None, None, "chan"),
            P(None, None, "chan"),
            P(None, None, "chan"),
            P(None, "chan", None),
            P(None, "chan"),
            P(None, None, None, "chan"),
            P(None, "chan", None),
        ),
        check_vma=False,
    )
```

profile of v0, /device:TPU:0, one launch (start us, length us, event | category | flops | bytes accessed | tf_op | source)
XLA Modules:
  0.0 1443.5 jit_solution(14924395118208514849)
XLA Ops:
  10.1 20.4 %all-reduce.83 = (f32[1536,1]{0,1:T(1,128)S(1)}, f32[1536,1]{0,1:T(1,128)S(1)}) all-reduce(f32[1536,1]{0,1:T(1,128)S(1)} %broadcast_in_dim.296, f32[1536,1]{0,1:T(1,128)S(1)} %broadcast_in_dim.297), channel_id=1, replica_groups=mesh['batch'=8,'chan'=4] {'chan'}, use_global_device_ids=true, to_apply=%region_1.0 | all-reduce | flops 3072 | bytes 24576 | tf_op jit(solution)/shard_map/psum | solution.py:70
  52.7 27.8 %all-gather.9.cloned.1.call-done = bf16[1536,768]{0,1:T(8,128)(2,1)} async-done(((bf16[1536,192]{0,1:T(8,128)(2,1)}), bf16[1536,768]{0,1:T(8,128)(2,1)}) %all-gather.9.cloned.1.call-update) | async-done | bytes 2359312 | tf_op jit(solution)/shard_map/all_gather | solution.py:77
  155.0 45.8 %reduce-scatter.9.cloned.1.call-done = bf16[1536,192]{0,1:T(8,128)(2,1)} async-done(((bf16[1536,768]{0,1:T(8,128)(2,1)}), bf16[1536,192]{0,1:T(8,128)(2,1)}) %reduce-scatter.9.cloned.1.call-update) | async-done | bytes 589840 | tf_op jit(solution)/shard_map/reduce_scatter | solution.py:102
  231.1 38.6 %all-gather.11.cloned.1.call-done = bf16[1536,768]{0,1:T(8,128)(2,1)} async-done(((bf16[1536,192]{0,1:T(8,128)(2,1)}), bf16[1536,768]{0,1:T(8,128)(2,1)}) %all-gather.11.cloned.1.call-update) | async-done | bytes 2359312 | tf_op jit(solution)/shard_map/all_gather | solution.py:77
  284.1 46.9 %reduce-scatter.11.cloned.1.call-done = bf16[1536,192]{0,1:T(8,128)(2,1)} async-done(((bf16[1536,768]{0,1:T(8,128)(2,1)}), bf16[1536,192]{0,1:T(8,128)(2,1)}) %reduce-scatter.11.cloned.1.call-update) | async-done | bytes 589840 | tf_op jit(solution)/shard_map/reduce_scatter | solution.py:102
  332.3 16.9 %all-reduce.81 = (f32[1536,1]{0,1:T(1,128)S(1)}, f32[1536,1]{0,1:T(1,128)S(1)}) all-reduce(f32[1536,1]{0,1:T(1,128)S(1)} %broadcast_in_dim.306, f32[1536,1]{0,1:T(1,128)S(1)} %broadcast_in_dim.307), channel_id=1, replica_groups=mesh['batch'=8,'chan'=4] {'chan'}, use_global_device_ids=true, to_apply=%region_11.12 | all-reduce | flops 3072 | bytes 24576 | tf_op jit(solution)/shard_map/psum | solution.py:70
  366.1 33.9 %all-gather.13.cloned.1.call-done = bf16[1536,768]{0,1:T(8,128)(2,1)} async-done(((bf16[1536,192]{0,1:T(8,128)(2,1)}), bf16[1536,768]{0,1:T(8,128)(2,1)}) %all-gather.13.cloned.1.call-update) | async-done | bytes 2359312 | tf_op jit(solution)/shard_map/all_gather | solution.py:77
  475.3 46.9 %reduce-scatter.13.cloned.1.call-done = bf16[1536,192]{0,1:T(8,128)(2,1)} async-done(((bf16[1536,768]{0,1:T(8,128)(2,1)}), bf16[1536,192]{0,1:T(8,128)(2,1)}) %reduce-scatter.13.cloned.1.call-update) | async-done | bytes 589840 | tf_op jit(solution)/shard_map/reduce_scatter | solution.py:102
  523.6 17.5 %all-reduce.80 = (f32[1536,1]{0,1:T(1,128)}, f32[1536,1]{0,1:T(1,128)}) all-reduce(f32[1536,1]{0,1:T(1,128)S(1)} %broadcast_in_dim.308, f32[1536,1]{0,1:T(1,128)S(1)} %broadcast_in_dim.309), channel_id=1, replica_groups=mesh['batch'=8,'chan'=4] {'chan'}, use_global_device_ids=true, to_apply=%region_16.17 | all-reduce | flops 3072 | bytes 24576 | tf_op jit(solution)/shard_map/psum | solution.py:70
  556.1 36.4 %all-gather.15.cloned.1.call-done = bf16[1536,768]{0,1:T(8,128)(2,1)} async-done(((bf16[1536,192]{0,1:T(8,128)(2,1)}), bf16[1536,768]{0,1:T(8,128)(2,1)}) %all-gather.15.cloned.1.call-update) | async-done | bytes 2359312 | tf_op jit(solution)/shard_map/all_gather | solution.py:77
  602.4 41.0 %all-gather.17.cloned.1.call-done = bf16[1536,768]{0,1:T(8,128)(2,1)} async-done(((bf16[1536,192]{0,1:T(8,128)(2,1)}), bf16[1536,768]{0,1:T(8,128)(2,1)}) %all-gather.17.cloned.1.call-update) | async-done | bytes 2359312 | tf_op jit(solution)/shard_map/all_gather | solution.py:108
  663.6 46.9 %reduce-scatter.17.cloned.1.call-done = bf16[1536,192]{0,1:T(8,128)(2,1)} async-done(((bf16[1536,768]{0,1:T(8,128)(2,1)}), bf16[1536,192]{0,1:T(8,128)(2,1)}) %reduce-scatter.17.cloned.1.call-update) | async-done | bytes 589840 | tf_op jit(solution)/shard_map/reduce_scatter | solution.py:83
  713.3 18.2 %all-reduce.79 = (f32[1536]{0:T(1024)}, f32[1536,1]{0,1:T(1,128)}) all-reduce(f32[1536]{0:T(1024)} %get-tuple-element.71, f32[1536,1]{0,1:T(1,128)} %broadcast_in_dim.312), channel_id=1, replica_groups=mesh['batch'=8,'chan'=4] {'chan'}, use_global_device_ids=true, to_apply=%region_24.25 | all-reduce | flops 3072 | bytes 24576 | tf_op jit(solution)/shard_map/psum | solution.py:88
  735.7 48.8 %all-gather.19.cloned.1.call-done = bf16[1536,768]{0,1:T(8,128)(2,1)} async-done(((bf16[1536,192]{0,1:T(8,128)(2,1)}), bf16[1536,768]{0,1:T(8,128)(2,1)}) %all-gather.19.cloned.1.call-update) | async-done | bytes 2359312 | tf_op jit(solution)/shard_map/all_gather | solution.py:108
  864.7 39.0 %reduce-scatter.19.cloned.1.call-done = bf16[1536,192]{0,1:T(8,128)(2,1)} async-done(((bf16[1536,768]{0,1:T(8,128)(2,1)}), bf16[1536,192]{0,1:T(8,128)(2,1)}) %reduce-scatter.19.cloned.1.call-update) | async-done | bytes 589840 | tf_op jit(solution)/shard_map/reduce_scatter | solution.py:83
  906.5 18.5 %all-reduce.78 = (f32[1536]{0:T(1024)}, f32[1536,1]{0,1:T(1,128)}) all-reduce(f32[1536]{0:T(1024)} %get-tuple-element.75, f32[1536,1]{0,1:T(1,128)} %broadcast_in_dim.320), channel_id=1, replica_groups=mesh['batch'=8,'chan'=4] {'chan'}, use_global_device_ids=true, to_apply=%region_29.30 | all-reduce | flops 3072 | bytes 24576 | tf_op jit(solution)/shard_map/psum | solution.py:88
  926.2 27.5 %reduce-scatter.15.cloned.1.call-done = bf16[1536,192]{0,1:T(8,128)(2,1)} async-done(((bf16[1536,768]{0,1:T(8,128)(2,1)}), bf16[1536,192]{0,1:T(8,128)(2,1)}) %reduce-scatter.15.cloned.1.call-update) | async-done | bytes 589840 | tf_op jit(solution)/shard_map/reduce_scatter | solution.py:102
  958.2 50.0 %all-gather.21.cloned.1.call-done = bf16[1536,768]{0,1:T(8,128)(2,1)} async-done(((bf16[1536,192]{0,1:T(8,128)(2,1)}), bf16[1536,768]{0,1:T(8,128)(2,1)}) %all-gather.21.cloned.1.call-update) | async-done | bytes 2359312 | tf_op jit(solution)/shard_map/all_gather | solution.py:108
  1024.6 47.0 %reduce-scatter.21.cloned.1.call-done = bf16[1536,192]{0,1:T(8,128)(2,1)} async-done(((bf16[1536,768]{0,1:T(8,128)(2,1)}), bf16[1536,192]{0,1:T(8,128)(2,1)}) %reduce-scatter.21.cloned.1.call-update) | async-done | bytes 589840 | tf_op jit(solution)/shard_map/reduce_scatter | solution.py:83
  1073.7 17.3 %all-reduce.77 = (f32[1536]{0:T(1024)S(1)}, f32[1536,1]{0,1:T(1,128)S(1)}) all-reduce(f32[1536]{0:T(1024)S(1)} %get-tuple-element.69, f32[1536,1]{0,1:T(1,128)S(1)} %broadcast_in_dim.324), channel_id=1, replica_groups=mesh['batch'=8,'chan'=4] {'chan'}, use_global_device_ids=true, to_apply=%region_34.35 | all-reduce | flops 3072 | bytes 24576 | tf_op jit(solution)/shard_map/psum | solution.py:88
  1262.8 26.7 %all-reduce.84 = (bf16[2,3,3,192]{3,2,1,0:T(4,128)(2,1)}, bf16[2,3,192]{2,1,0:T(4,128)(2,1)}, bf16[2,192]{1,0:T(2,128)(2,1)}, bf16[2,192]{1,0:T(2,128)(2,1)}) all-reduce(bf16[2,3,3,192]{3,2,1,0:T(4,128)(2,1)} %pad_maximum_fusion.5, bf16[2,3,192]{2,1,0:T(4,128)(2,1)} %pad_maximum_fusion.6, ...), channel_id=1, replica_groups=mesh['batch'=8,'chan'=4] {'batch'}, use_global_device_ids=true, to_apply=%region_56.57 | all-reduce | flops 5376 | bytes 21504 | tf_op jit(solution)/shard_map/psum | solution.py:263
  1295.8 18.6 %all-reduce.76 = (f32[1536]{0:T(1024)}, f32[1536,1]{0,1:T(1,128)}) all-reduce(f32[1536]{0:T(1024)} %get-tuple-element.73, f32[1536,1]{0,1:T(1,128)} %broadcast_in_dim.332), channel_id=1, replica_groups=mesh['batch'=8,'chan'=4] {'chan'}, use_global_device_ids=true, to_apply=%region_39.40 | all-reduce | flops 3072 | bytes 24576 | tf_op jit(solution)/shard_map/psum | solution.py:88
  1319.1 89.3 %all-reduce.88.cloned.1.call-done = (bf16[2,768,2,768]{3,1,2,0:T(8,128)(2,1)}, bf16[2,768,3,192]{1,3,2,0:T(8,128)(2,1)}, bf16[2,512,192]{1,2,0:T(8,128)(2,1)}, b...) async-done(((bf16[2,768,2,768]{3,1,2,0:T(8,128)(2,1)}, bf16[2,768,3,192]{1,3,2,0:T(8,128)(2,1)}, bf16[2,512,192]{1,2,0:T(8,128)(2,1)}, bf16[2,192,768]{2,1,0:T(8,128)(2,1)}, ...) | async-done | bytes 9830416 | tf_op jit(solution)/shard_map/psum | solution.py:268
  1415.9 18.1 %copy.126 = f32[2,768,2,768]{3,2,1,0:T(2,128)} copy(bf16[2,768,2,768]{3,1,2,0:T(8,128)(2,1)S(1)} %copy-done.65) | data formatting | bytes 14155776
  (800 shorter events, 587.6 us)
Async XLA Ops:
  7.2 73.3 %all-gather.9.cloned.1.call-start = ((), (), s32[]{:S(2)}) async-start(), calls=%async_computation.8 | async-start | bytes 2949120 | tf_op jit(solution)/shard_map/all_gather | solution.py:77
  9.9 190.9 %copy-start.2 = (f32[1536,192]{0,1:T(8,128)}, f32[1536,192]{0,1:T(8,128)S(1)}, u32[]{:S(2)}) copy-start(f32[1536,192]{0,1:T(8,128)S(1)} %bitcast_dynamic-update-slice_fusion.3) | copy-start | bytes 3538948
  31.7 169.2 %reduce-scatter.9.cloned.1.call-start = ((), (), s32[]{:S(2)}) async-start(), calls=%async_computation.9 | async-start | bytes 2949120 | tf_op jit(solution)/shard_map/reduce_scatter | solution.py:102
  34.8 386.4 %copy-start.153 = (f32[2,512]{1,0:T(2,128)}, f32[2,512]{1,0:T(2,128)S(1)}, u32[]{:S(2)}) copy-start(f32[2,512]{1,0:T(2,128)S(1)} %compare_convert_fusion) | copy-start | bytes 12292
  153.8 115.9 %all-gather.11.cloned.1.call-start = ((), (), s32[]{:S(2)}) async-start(), calls=%async_computation.10 | async-start | bytes 2949120 | tf_op jit(solution)/shard_map/all_gather | solution.py:77
  155.0 64.1 %copy-start.178 = (f32[1,192]{1,0:T(1,128)}, f32[1,192]{1,0:T(1,128)S(1)}, u32[]{:S(2)}) copy-start(f32[1,192]{1,0:T(1,128)S(1)} %get-tuple-element.200) | copy-start | bytes 2308
  220.7 110.3 %reduce-scatter.11.cloned.1.call-start = ((), (), s32[]{:S(2)}) async-start(), calls=%async_computation.11 | async-start | bytes 2949120 | tf_op jit(solution)/shard_map/reduce_scatter | solution.py:102
  284.0 65.9 %copy-start.189 = (f32[1,192]{1,0:T(1,128)S(1)}, f32[1,192]{1,0:T(1,128)}, u32[]{:S(2)}) copy-start(f32[1,192]{1,0:T(1,128)} %get-tuple-element.201) | copy-start | bytes 2308
  284.0 115.9 %all-gather.13.cloned.1.call-start = ((), (), s32[]{:S(2)}) async-start(), calls=%async_computation.12 | async-start | bytes 2949120 | tf_op jit(solution)/shard_map/all_gather | solution.py:77
  350.9 171.3 %reduce-scatter.13.cloned.1.call-start = ((), (), s32[]{:S(2)}) async-start(), calls=%async_computation.13 | async-start | bytes 2949120 | tf_op jit(solution)/shard_map/reduce_scatter | solution.py:102
  351.4 68.1 %copy-start.165 = (f32[3,192]{1,0:T(4,128)}, f32[3,192]{1,0:T(4,128)S(1)}, u32[]{:S(2)}) copy-start(f32[3,192]{1,0:T(4,128)S(1)} %get-tuple-element.219) | copy-start | bytes 6916
  351.4 68.1 %copy-start.168 = (f32[3,192]{1,0:T(4,128)}, f32[3,192]{1,0:T(4,128)S(1)}, u32[]{:S(2)}) copy-start(f32[3,192]{1,0:T(4,128)S(1)} %get-tuple-element.220) | copy-start | bytes 6916
  475.3 117.2 %all-gather.15.cloned.1.call-start = ((), (), s32[]{:S(2)}) async-start(), calls=%async_computation.14 | async-start | bytes 2949120 | tf_op jit(solution)/shard_map/all_gather | solution.py:77
  543.4 99.9 %all-gather.17.cloned.1.call-start = ((), (), s32[]{:S(2)}) async-start(), calls=%async_computation.16 | async-start | bytes 2949120 | tf_op jit(solution)/shard_map/all_gather | solution.py:108
  547.7 162.8 %reduce-scatter.17.cloned.1.call-start = ((), (), s32[]{:S(2)}) async-start(), calls=%async_computation.17 | async-start | bytes 2949120 | tf_op jit(solution)/shard_map/reduce_scatter | solution.py:83
  663.5 121.0 %all-gather.19.cloned.1.call-start = ((), (), s32[]{:S(2)}) async-start(), calls=%async_computation.18 | async-start | bytes 2949120 | tf_op jit(solution)/shard_map/all_gather | solution.py:108
  735.5 168.2 %reduce-scatter.19.cloned.1.call-start = ((), (), s32[]{:S(2)}) async-start(), calls=%async_computation.19 | async-start | bytes 2949120 | tf_op jit(solution)/shard_map/reduce_scatter | solution.py:83
  856.7 97.0 %reduce-scatter.15.cloned.1.call-start = ((), (), s32[]{:S(2)}) async-start(), calls=%async_computation.15 | async-start | bytes 2949120 | tf_op jit(solution)/shard_map/reduce_scatter | solution.py:102
  864.6 143.6 %all-gather.21.cloned.1.call-start = ((), (), s32[]{:S(2)}) async-start(), calls=%async_computation.20 | async-start | bytes 2949120 | tf_op jit(solution)/shard_map/all_gather | solution.py:108
  958.2 113.4 %reduce-scatter.21.cloned.1.call-start = ((), (), s32[]{:S(2)}) async-start(), calls=%async_computation.21 | async-start | bytes 2949120 | tf_op jit(solution)/shard_map/reduce_scatter | solution.py:83
  1024.6 66.5 %copy-start.33 = (f32[1536,192]{0,1:T(8,128)S(1)}, f32[1536,192]{0,1:T(8,128)}, u32[]{:S(2)}) copy-start(f32[1536,192]{0,1:T(8,128)} %get-tuple-element.142) | copy-start | bytes 3538948
  1024.6 116.8 %all-gather.23.cloned.1.call-start = ((), (), s32[]{:S(2)}) async-start(), calls=%async_computation.22 | async-start | bytes 2949120 | tf_op jit(solution)/shard_map/all_gather | solution.py:108
  1092.3 167.7 %reduce-scatter.23.cloned.1.call-start = ((), (), s32[]{:S(2)}) async-start(), calls=%async_computation.23 | async-start | bytes 2949120 | tf_op jit(solution)/shard_map/reduce_scatter | solution.py:83
  1213.0 195.4 %all-reduce.88.cloned.1.call-start = ((), (), s32[]{:S(2)}) async-start(), calls=%async_computation.24 | async-start | bytes 19660800 | tf_op jit(solution)/shard_map/psum | solution.py:268
  (253 other events, 1832.0 us)
Sparse Core Ops, SparseCore 0:
  31.8 48.6 all-gather.8
  153.9 46.8 reduce-scatter.8
  220.8 48.8 all-gather.10
  284.1 46.8 reduce-scatter.10
  351.1 48.8 all-gather.12
  475.4 46.8 reduce-scatter.12
  543.6 48.8 all-gather.14
  594.0 49.2 all-gather.16
  663.6 46.8 reduce-scatter.16
  735.6 48.8 all-gather.18
  856.8 46.8 reduce-scatter.18
  905.9 47.8 reduce-scatter.14
  958.3 49.9 all-gather.20
  1024.7 46.8 reduce-scatter.20
  1092.4 48.8 all-gather.22
  1213.1 46.8 reduce-scatter.22
  1264.8 143.4 all-reduce.87
where the time goes:
time: 1460 us; the launch traced here: 1440 us
  waiting for transfers between devices  684 us (47%)
  matrix products  368 us (25%)
  blocking collectives  171 us (12%)
  local copies, waits for them, and re-layouts  117 us (8%)
  other arithmetic  83.8 us (6%)
  between operations  18 us (1%)
    reduce_scatter x4, waiting for transfers between devices, branch_out(): lax.psum_scatter(partial_rows.astype(jnp.bfloat16), 'chan', scatter_dimen...  167 us
    all_gather x4, waiting for transfers between devices, branch_back(): lax.all_gather(grad_local.astype(jnp.bfloat16), 'chan', axis=1, tiled=True)  154 us
    all_gather x4, waiting for transfers between devices, project_in(): lax.all_gather((normal_rows * gain).astype(jnp.bfloat16), 'chan', axis=1,...  137 us
    reduce_scatter x4, waiting for transfers between devices, norm_back(): lax.psum_scatter(partial_rows.astype(jnp.bfloat16), 'chan', scatter_dimen...  136 us
    psum x1, waiting for transfers between devices, on_device(): lax.psum(stacked[7].astype(jnp.bfloat16), 'batch').astype(jnp.float32)  89.3 us
    psum x4, blocking collectives, norm_back(): lax.psum((jnp.sum(scaled, axis=1, keepdims=True), jnp.sum(scaled * normal...  72.5 us
    psum x4, blocking collectives, project_in(): lax.psum((jnp.sum(values, axis=1, keepdims=True), jnp.sum(values * values...  71.8 us
    unnamed x538, local copies, waits for them, and re-layouts  67.8 us
  transfers between devices with their start and end apart: 17, of which 17 were waited for; matrix products, arithmetic and copies ran while one was open for 12% of the time, Pallas kernels for 0%

commit v1 on v0

v1 whole, which is shorter than its diff:
```python
import functools
import math

import jax
import jax.numpy as jnp
import numpy as np
from jax import lax
from jax.experimental import pallas as pl
from jax.experimental.pallas import tpu as pltpu
from jax.sharding import PartitionSpec as P

EPS = 1e-05
BF16 = jnp.bfloat16
F32 = jnp.float32
VMEM_BYTES = 52 * 2**20
FAR, NEAR = (3, 1)


def nn(left, right):
    return lax.dot_general(left, right, (((1,), (0,)), ((), ())), preferred_element_type=F32)


def nt(left, right):
    return lax.dot_general(left, right, (((1,), (1,)), ((), ())), preferred_element_type=F32)


def tn(left, right):
    return lax.dot_general(left, right, (((0,), (0,)), ((), ())), preferred_element_type=F32)


def table(length):
    places = np.arange(length)[:, None]
    phase = (places * np.arange(length + 1)[None, :] % (2 * length)) * (np.pi / length)
    packed = np.concatenate(
        [np.cos(phase[:, :length]), np.cos(phase[:, length:]), -np.sin(phase[:, 1:length])], axis=1
    )
    return jnp.asarray(packed.astype(np.float32)).astype(BF16)


def swap(values, step):
    axis, mask = step
    return lax.ppermute(values, axis, [(i, i ^ mask) for i in range(lax.axis_size(axis))])


def pick(values, index):
    return lax.dynamic_index_in_dim(values, index, 0, keepdims=False)


def by_xor(values, index):
    return jnp.stack([pick(values, place ^ index) for place in range(values.shape[0])])


def copy_all(copies):
    for copy in copies:
        copy.start()
    for copy in copies:
        copy.wait()


def assemble_kernel(plan, ranks, place_ref, own_ref, *refs):
    *buffers, flat_ref, sems = refs
    pair = place_ref[1]
    step = pl.program_id(0)

    for other in range(ranks):

        @pl.when(step == other)
        def fill():
            copies = []
            if other == 0:
                copies.append(pltpu.make_async_copy(own_ref, flat_ref.at[0], sems.at[0]))
            for buffer, (half, blocks, start, count) in zip(buffers, plan):
                for at, (offset, owner) in enumerate(blocks):
                    if owner != other:
                        continue
                    row = pl.multiple_of(((pair ^ offset) * 2 + half) * count, 16)
                    copies.append(
                        pltpu.make_async_copy(
                            buffer.at[at, pl.ds(start, count)],
                            flat_ref.at[0, pl.ds(row, count)],
                            sems.at[len(copies)],
                        )
                    )
            copy_all(copies)


def assemble(place, own, buffers, plan, ranks):
    rows, width = own.shape
    return pl.pallas_call(
        functools.partial(assemble_kernel, plan, ranks),
        grid=(ranks,),
        out_shape=jax.ShapeDtypeStruct((ranks, rows, width), own.dtype),
        in_specs=[pl.BlockSpec(memory_space=pltpu.SMEM)]
        + [pl.BlockSpec(memory_space=pl.ANY)] * (1 + len(buffers)),
        out_specs=pl.BlockSpec((1, rows, width), lambda r: (r, 0, 0)),
        scratch_shapes=[pltpu.SemaphoreType.DMA((sum(len(p[1]) for p in plan),))],
        compiler_params=pltpu.CompilerParams(vmem_limit_bytes=VMEM_BYTES),
        cost_estimate=pl.CostEstimate(
            flops=0, bytes_accessed=4 * ranks * rows * width, transcendentals=0
        ),
        name="assemble",
    )(place, own, *buffers)


def cut_kernel(plans, orders, place_ref, *refs):
    sources, outs, sems = (refs[: len(plans)], refs[len(plans) : -1], refs[-1])
    pair = place_ref[1]
    step = pl.program_id(0)
    for owner in sorted({other for _, other in orders[0]}):

        @pl.when(step == owner)
        def spill():
            copies = []
            for half, blocks in enumerate(orders):
                for at, (offset, other) in enumerate(blocks):
                    if other != owner:
                        continue
                    middle = len(blocks) // 2
                    target = outs[2 * half + (1 if at >= middle else 0)].at[at % middle]
                    for source, (start, count) in zip(sources, plans):
                        row = pl.multiple_of(((pair ^ offset) * 2 + half) * count, 16)
                        copies.append(
                            pltpu.make_async_copy(
                                source.at[0, pl.ds(row, count)],
                                target.at[pl.ds(start, count)],
                                sems.at[len(copies)],
                            )
                        )
            copy_all(copies)


def cut(place, sources, plans, orders):
    ranks, _, width = sources[0].shape
    rows = sum(count for _, count in plans)
    shape = jax.ShapeDtypeStruct((len(orders[0]) // 2, rows, width), sources[0].dtype)
    kept0, sent0, kept1, sent1 = pl.pallas_call(
        functools.partial(cut_kernel, plans, orders),
        grid=(ranks,),
        out_shape=[shape] * 4,
        in_specs=[pl.BlockSpec(memory_space=pltpu.SMEM)]
        + [pl.BlockSpec((1,) + source.shape[1:], lambda r: (r, 0, 0)) for source in sources],
        out_specs=[pl.BlockSpec(memory_space=pl.ANY)] * 4,
        scratch_shapes=[
            pltpu.SemaphoreType.DMA((len(sources) * sum(len(blocks) for blocks in orders),))
        ],
        compiler_params=pltpu.CompilerParams(vmem_limit_bytes=VMEM_BYTES),
        cost_estimate=pl.CostEstimate(
            flops=0, bytes_accessed=8 * shape.size * 2, transcendentals=0
        ),
        name="cut",
    )(place, *sources)
    return ((kept0, sent0), (kept1, sent1))


def gelu_parts(gate):
    slope = math.sqrt(2.0 / math.pi)
    square = gate * gate
    bent = jnp.tanh(slope * (gate + 0.044715 * square * gate))
    gelu = 0.5 * gate * (1.0 + bent)
    grad = 0.5 * (1.0 + bent) + 0.5 * gate * (1.0 - bent * bent) * slope * (
        1.0 + 0.134145 * square
    )
    return (gelu, grad)


def mlp_forward_kernel(flat_ref, normed_ref, gate_up_ref, kept_ref, sent_ref, total):
    step = pl.program_id(0)
    width = normed_ref.shape[0]
    hidden = flat_ref.shape[1] - width
    gate_up = tn(flat_ref[0, :width], normed_ref[...])
    gate_up_ref[0] = gate_up.astype(BF16)
    activated = (gelu_parts(gate_up[:hidden])[0] * gate_up[hidden:]).astype(BF16)
    part = tn(flat_ref[0, width:], activated)

    @pl.when(step == 0)
    def start():
        total[...] = part

    @pl.when(step > 0)
    def add():
        total[...] += part

    @pl.when(step == pl.num_programs(0) - 1)
    def finish():
        own = kept_ref.shape[1]
        kept_ref[...] = total[:, :own]
        sent_ref[...] = total[:, own:].astype(BF16)


def mlp_forward(flat, normed):
    ranks, rows, width = flat.shape
    tokens = normed.shape[1]
    hidden = rows - width
    half = tokens // 2
    return pl.pallas_call(
        mlp_forward_kernel,
        grid=(ranks,),
        out_shape=[
            jax.ShapeDtypeStruct((ranks, 2 * hidden, tokens), BF16),
            jax.ShapeDtypeStruct((width, half), F32),
            jax.ShapeDtypeStruct((width, half), BF16),
        ],
        in_specs=[
            pl.BlockSpec((1, rows, width), lambda r: (r, 0, 0)),
            pl.BlockSpec((width, tokens), lambda r: (0, 0)),
        ],
        out_specs=[
            pl.BlockSpec((1, 2 * hidden, tokens), lambda r: (r, 0, 0)),
            pl.BlockSpec((width, half), lambda r: (0, 0)),
            pl.BlockSpec((width, half), lambda r: (0, 0)),
        ],
        scratch_shapes=[pltpu.VMEM((width, tokens), F32)],
        compiler_params=pltpu.CompilerParams(vmem_limit_bytes=VMEM_BYTES),
        cost_estimate=pl.CostEstimate(
            flops=6 * ranks * hidden * width * tokens,
            bytes_accessed=2 * flat.size + 4 * ranks * hidden * tokens,
            transcendentals=ranks * hidden * tokens,
        ),
        name="mlp_forward",
    )(flat, normed)


def mlp_back_kernel(
    flat_ref, normed_ref, gate_up_ref, coming_ref, grads_ref, kept_ref, sent_ref, total
):
    step = pl.program_id(0)
    width = normed_ref.shape[0]
    hidden = flat_ref.shape[1] - width
    gate = gate_up_ref[0, :hidden].astype(F32)
    up = gate_up_ref[0, hidden:].astype(F32)
    grad_act = nn(flat_ref[0, width:], coming_ref[...])
    gelu, slope = gelu_parts(gate)
    activated = (gelu * up).astype(BF16)
    grad_gate = (grad_act * up * slope).astype(BF16)
    grad_up = (grad_act * gelu).astype(BF16)
    grads_ref[0, width:] = nt(activated, coming_ref[...]).astype(BF16)
    grads_ref[0, :width, :hidden] = nt(normed_ref[...], grad_gate).astype(BF16)
    grads_ref[0, :width, hidden:] = nt(normed_ref[...], grad_up).astype(BF16)
    part = nn(flat_ref[0, :width, :hidden], grad_gate) + nn(flat_ref[0, :width, hidden:], grad_up)

    @pl.when(step == 0)
    def start():
        total[...] = part

    @pl.when(step > 0)
    def add():
        total[...] += part

    @pl.when(step == pl.num_programs(0) - 1)
    def finish():
        own = kept_ref.shape[1]
        kept_ref[...] = total[:, :own]
        sent_ref[...] = total[:, own:].astype(BF16)


def mlp_back(flat, normed, gate_up, coming):
    ranks, rows, width = flat.shape
    tokens = normed.shape[1]
    hidden = rows - width
    half = tokens // 2
    return pl.pallas_call(
        mlp_back_kernel,
        grid=(ranks,),
        out_shape=[
            jax.ShapeDtypeStruct(flat.shape, BF16),
            jax.ShapeDtypeStruct((width, half), F32),
            jax.ShapeDtypeStruct((width, half), BF16),
        ],
        in_specs=[
            pl.BlockSpec((1, rows, width), lambda r: (r, 0, 0)),
            pl.BlockSpec((width, tokens), lambda r: (0, 0)),
            pl.BlockSpec((1, 2 * hidden, tokens), lambda r: (r, 0, 0)),
            pl.BlockSpec((width, tokens), lambda r: (0, 0)),
        ],
        out_specs=[
            pl.BlockSpec((1, rows, width), lambda r: (r, 0, 0)),
            pl.BlockSpec((width, half), lambda r: (0, 0)),
            pl.BlockSpec((width, half), lambda r: (0, 0)),
        ],
        scratch_shapes=[pltpu.VMEM((width, tokens), F32)],
        compiler_params=pltpu.CompilerParams(vmem_limit_bytes=VMEM_BYTES),
        cost_estimate=pl.CostEstimate(
            flops=12 * ranks * hidden * width * tokens,
            bytes_accessed=4 * flat.size + 4 * ranks * hidden * tokens,
            transcendentals=ranks * hidden * tokens,
        ),
        name="mlp_back",
    )(flat, normed, gate_up, coming)


def delay(values, by):
    return jnp.pad(values, ((0, 0),) * (values.ndim - 1) + ((by, 0),))[..., : values.shape[-1]]


def advance(values, by):
    return jnp.pad(values, ((0, 0),) * (values.ndim - 1) + ((0, by),))[..., by:]


def taps_forward(values, taps):
    return taps[0] * values + taps[1] * delay(values, 1) + taps[2] * delay(values, 2)


def taps_back(values, taps):
    return taps[0] * values + taps[1] * advance(values, 1) + taps[2] * advance(values, 2)


def taps_grad(grads, values):
    return [
        jnp.sum(grads * (delay(values, k) if k else values), axis=(0, 2)) for k in range(3)
    ]


def transform(values, cosines):
    return lax.dot_general(
        values.astype(BF16),
        cosines,
        (((values.ndim - 1,), (0,)), ((), ())),
        preferred_element_type=F32,
    )


def transform_back(real_part, imag_part, cosines):
    packed = jnp.concatenate([real_part.astype(BF16), imag_part.astype(BF16)], axis=-1)
    return lax.dot_general(
        packed, cosines, (((packed.ndim - 1,), (1,)), ((), ())), preferred_element_type=F32
    )


def mix_forward(projected, live, short_taps, cond_taps, static_rows):
    count, width, length = projected[0].shape
    cosines = table(length)
    query, key_part, value_part = (
        taps_forward(values, short_taps[group]) for group, values in enumerate(projected)
    )
    gated = key_part * value_part * live
    shaped = taps_forward(gated, cond_taps)
    spectra = transform(jnp.concatenate([gated, shaped], axis=0), cosines)
    signal_re, signal_im = (spectra[:count, :, :length], spectra[:count, :, length:])
    shaped_re, shaped_im = (spectra[count:, :, :length], spectra[count:, :, length:])
    fixed = transform(static_rows[:, :length], cosines)
    fixed_re, fixed_im = (fixed[:, :length], fixed[:, length:])
    edge = (jnp.arange(length) == 0)[None, None, :]
    square_im = shaped_im * shaped_im
    root = jnp.sqrt(shaped_re * shaped_re + jnp.where(edge, 0.0, square_im) + length)
    root_last = jnp.sqrt(square_im + length)
    scale = 1.0 / math.sqrt(length)
    filter_re = fixed_re + (root * scale - 1.0)
    filter_last = fixed_im + (root_last * scale - 1.0)
    weight = jnp.where(edge, 0.5 / length, 1.0 / length)
    product_re = filter_re * signal_re - jnp.where(edge, 0.0, fixed_im * signal_im)
    product_im = jnp.where(
        edge, filter_last * signal_im, filter_re * signal_im + fixed_im * signal_re
    )
    long_out = transform_back(product_re * weight, product_im * weight, cosines)
    stored = (
        projected, query, key_part, value_part, gated, signal_re, signal_im, shaped_re, shaped_im,
        fixed_im, root, root_last, filter_re, filter_last, long_out, edge, weight, cosines,
    )
    return (query * long_out, stored)


def mix_back(grad_mixed, live, short_taps, cond_taps, stored):
    (
        projected, query, key_part, value_part, gated, signal_re, signal_im, shaped_re, shaped_im,
        fixed_im, root, root_last, filter_re, filter_last, long_out, edge, weight, cosines,
    ) = stored
    count, width, length = gated.shape
    scale = 1.0 / math.sqrt(length)
    grad_query = grad_mixed * long_out
    grad_product = transform(grad_mixed * query, cosines)
    product_re = grad_product[..., :length] * weight
    product_im = grad_product[..., length:] * weight
    grad_signal_re = filter_re * product_re + jnp.where(edge, 0.0, fixed_im * product_im)
    grad_signal_im = jnp.where(
        edge, filter_last * product_im, filter_re * product_im - fixed_im * product_re
    )
    crossed = signal_im * product_im
    grad_filter = signal_re * product_re + jnp.where(edge, 0.0, crossed)
    grad_fixed_im = jnp.where(edge, crossed, signal_re * product_im - signal_im * product_re)
    slope = grad_filter * scale / root
    grad_shaped_re = slope * shaped_re
    grad_shaped_im = jnp.where(edge, crossed * scale / root_last, slope) * shaped_im
    grad_static = transform_back(
        jnp.sum(grad_filter, axis=0), jnp.sum(grad_fixed_im, axis=0), cosines
    )
    back = transform_back(
        jnp.concatenate([grad_signal_re, grad_shaped_re], axis=0),
        jnp.concatenate([grad_signal_im, grad_shaped_im], axis=0),
        cosines,
    )
    grad_shaped = back[count:]
    grad_gated = (back[:count] + taps_back(grad_shaped, cond_taps)) * live
    grad_cond = taps_grad(grad_shaped, gated)
    grads = (grad_query, grad_gated * value_part, grad_gated * key_part)
    grad_projected = [taps_back(grad, short_taps[group]) for group, grad in enumerate(grads)]
    grad_taps = [taps_grad(grad, projected[group]) for group, grad in enumerate(grads)]
    return (grad_projected, grad_taps, grad_cond, grad_static)


def norm_forward(values, gain):
    average = jnp.mean(values, axis=0, keepdims=True)
    centered = values - average
    inv_std = lax.rsqrt(jnp.mean(centered * centered, axis=0, keepdims=True) + EPS)
    normal_rows = centered * inv_std
    return ((normal_rows * gain).astype(BF16), (normal_rows, inv_std, gain))


def norm_back(grads, stored):
    normal_rows, inv_std, gain = stored
    scaled = grads * gain
    total = jnp.mean(scaled, axis=0, keepdims=True)
    crossed = jnp.mean(scaled * normal_rows, axis=0, keepdims=True)
    gain_grad = jnp.sum(grads * normal_rows, axis=1)
    return (inv_std * (scaled - total - normal_rows * crossed), gain_grad)


def on_device(
    input_long,
    input_short,
    length_long,
    length_short,
    gain_mixer,
    weight_in,
    short_taps,
    cond_taps,
    static_filter,
    weight_out,
    gain_mlp,
    weight_up,
    weight_down,
    grad_long,
    grad_short,
):
    count_long, seq_long, chan_width = input_long.shape
    count_short, seq_short = (input_short.shape[0], input_short.shape[1])
    layers = weight_in.shape[0]
    ranks = lax.axis_size("chan")
    pairs = lax.axis_size("batch") // 2
    place = lax.axis_index("chan")
    core = lax.axis_index("batch") % 2
    pair = lax.axis_index("batch") // 2
    width = chan_width * ranks
    hidden = weight_down.shape[1] // 2
    chans = chan_width // 2
    half_long = seq_long // 2
    tokens = half_long + seq_short
    mate = ("batch", 1)
    first = core == 0
    pieces = 4
    piece = pair % pieces
    plane = {1: ("batch", 2), 2: ("batch", 4)}
    extra_steps = []
    mask = 2 * pieces
    while mask < 2 * pairs:
        extra_steps.append(("batch", mask))
        mask *= 2
    spot = jnp.stack([core, piece]).astype(jnp.int32)
    plane_orders = ((1, 2), (2, 1))

    def exchange(blocks):
        came = [pick(blocks, place)]
        came += [swap(pick(blocks, place ^ r), ("chan", r)) for r in range(1, ranks)]
        return by_xor(jnp.stack(came), place)

    def to_tokens(long_rows, short_rows, extra=None):
        turned = jnp.swapaxes(long_rows, 1, 2).astype(BF16)
        halves = jnp.stack([turned[:, :, :half_long], turned[:, :, half_long:]])
        kept = pick(halves, core)
        came = swap(pick(halves, 1 - core), mate)
        ordered = jnp.where(first, jnp.concatenate([kept, came]), jnp.concatenate([came, kept]))
        parts = [ordered, jnp.swapaxes(short_rows, 1, 2).astype(BF16)]
        if extra is not None:
            parts.append(jnp.broadcast_to(extra[None], (ranks,) + extra.shape))
        gathered = exchange(jnp.concatenate(parts, axis=2))
        return gathered.reshape(width, -1)

    def from_tokens(values):
        gathered = exchange(values.reshape(ranks, chan_width, tokens))
        halves = gathered[:, :, :half_long].reshape(2, count_long, chan_width, half_long)
        kept = pick(halves, core)
        came = swap(pick(halves, 1 - core), mate)
        ordered = jnp.where(
            first, jnp.concatenate([kept, came], axis=2), jnp.concatenate([came, kept], axis=2)
        )
        return (jnp.swapaxes(ordered, 1, 2), jnp.swapaxes(gathered[:, :, half_long:], 1, 2))

    def both_cores(values):
        return jnp.concatenate([values, swap(values, mate)], axis=1)

    def both_ordered(values):
        came = swap(values, mate)
        low, high = (jnp.where(first, values, came), jnp.where(first, came, values))
        return jnp.concatenate(
            [low[:, :half_long], high[:, :half_long], low[:, half_long:], high[:, half_long:]],
            axis=1,
        )

    def core_part(values, which):
        long_part = lax.dynamic_slice_in_dim(values, which * half_long, half_long, 1)
        short_part = lax.dynamic_slice_in_dim(values, seq_long + which * seq_short, seq_short, 1)
        return jnp.concatenate([long_part, short_part], axis=1)

    def own_sum(sent, kept):
        return kept + swap(sent, mate).astype(F32)

    def mlp_rows(layer):
        up = lax.dynamic_slice_in_dim(weight_up[layer], core * hidden, hidden, 2)
        down = lax.dynamic_slice_in_dim(weight_down[layer], core * hidden, hidden, 0)
        return jnp.concatenate([up.reshape(width, 2 * hidden), down])

    def mixer_rows(layer):
        into = jnp.transpose(weight_in[layer], (1, 2, 0))
        into = lax.dynamic_slice_in_dim(into, core * chans, chans, 1)
        out = lax.dynamic_slice_in_dim(weight_out[layer], core * chans, chans, 0)
        taps = jnp.concatenate([short_taps[layer].reshape(9, chan_width), cond_taps[layer]]).T
        coarse = lax.reduce_precision(taps, 8, 7)
        static = jnp.concatenate([static_filter[layer].T, coarse, taps - coarse], axis=1)
        static = jnp.pad(static.astype(BF16), ((0, 0), (0, width - static.shape[1])))
        static = lax.dynamic_slice_in_dim(static, core * chans, chans, 0)
        spare = jnp.zeros((mixer_count - 5 * chans, width), BF16)
        return jnp.concatenate([into.reshape(3 * chans, width), out, static, spare])

    mixer_count = -(-5 * chans // (32 * pieces)) * 32 * pieces
    mlp_count = width + hidden
    own_rows = [
        {"mixer": mixer_rows(layer), "mlp": mlp_rows(layer)} for layer in range(layers)
    ]

    def half_rows(kind):
        return (mixer_count if kind == "mixer" else mlp_count) // (2 * pieces)

    def own_block(layer, kind, half):
        count = half_rows(kind)
        return lax.dynamic_slice_in_dim(
            own_rows[layer][kind], (piece * 2 + half) * count, count, 0
        )

    def gather_weights(wanted):
        parts = [own_block(layer, kind, half) for half in range(2) for layer, kind in wanted]
        block = jnp.concatenate(parts)[None]
        rows = block.shape[1] // 2
        far = swap(block, ("chan", FAR))
        near = swap(jnp.concatenate([block, far]), ("chan", NEAR))
        others = (FAR, NEAR, FAR ^ NEAR)
        foreign = jnp.concatenate([far, near])
        buffers, blocks = ([], [])
        for half in range(2):
            held = foreign[:, half * rows : (half + 1) * rows]
            held_blocks = [(0, other) for other in others]
            one, two = plane_orders[half]
            held = jnp.concatenate([held, swap(held, plane[one])])
            held_blocks = held_blocks + [(one, other) for other in others]
            buffers += [held, swap(held, plane[two])]
            blocks += [held_blocks, [(offset ^ two, other) for offset, other in held_blocks]]
        start = 0
        found = {}
        for layer, kind in wanted:
            count = half_rows(kind)
            plan = tuple((at // 2, tuple(blocks[at]), start, count) for at in range(4))
            found[layer, kind] = assemble(spot, own_rows[layer][kind], buffers, plan, ranks)
            start += count
        return found

    weights = gather_weights([(0, "mixer")])
    gains = jnp.stack([gain_mixer, gain_mlp], axis=1).reshape(2 * layers, chan_width)
    gains_coarse = lax.reduce_precision(gains, 8, 7)
    extra = jnp.concatenate([gains_coarse, gains - gains_coarse]).astype(BF16).T
    extra = jnp.pad(extra, ((0, 0), (0, 128 - extra.shape[1])))
    arrived = to_tokens(input_long, input_short, extra)
    gains = arrived[:, tokens:].astype(F32)
    gains = gains[:, : 2 * layers] + gains[:, 2 * layers : 4 * layers]
    gains = [[gains[:, 2 * layer + which][:, None] for which in range(2)] for layer in range(layers)]
    weights.update(gather_weights([(0, "mlp")]))
    for layer in range(1, layers):
        weights.update(gather_weights([(layer, "mlp"), (layer, "mixer")]))
    upstream = to_tokens(grad_long, grad_short).astype(F32)

    own_lengths = jnp.concatenate([length_long, length_short])
    other_lengths = swap(own_lengths, mate)
    low, high = (
        jnp.where(first, own_lengths, other_lengths),
        jnp.where(first, other_lengths, own_lengths),
    )
    live_long = jnp.arange(seq_long) < pick(
        jnp.concatenate([low[:count_long], high[:count_long]]), place
    )
    live_short = jnp.arange(seq_short) < jnp.stack(
        [pick(low[count_long:], place), pick(high[count_long:], place)]
    )[:, None]
    live_long = live_long.astype(F32)[None, None, :]
    live_short = live_short.astype(F32)[:, None, :]

    def by_sequence(values):
        shorts = [
            values[:, seq_long + i * seq_short : seq_long + (i + 1) * seq_short] for i in range(2)
        ]
        return (values[:, :seq_long][None], jnp.stack(shorts))

    def by_token(whole, shorts):
        return jnp.concatenate([whole[0], shorts[0], shorts[1]], axis=1)

    def mixer_part(flat, index, count=1):
        return flat[:, index * chans : (index + count) * chans]

    residual_start = arrived[:, :tokens].astype(F32)
    residual = residual_start
    stored_all = []
    for layer in range(layers):
        flat = weights[layer, "mixer"]
        normed, norm_stored = norm_forward(residual, gains[layer][0])
        normed = both_ordered(normed)
        into = jnp.concatenate([mixer_part(flat, g).reshape(-1, width) for g in range(3)])
        out_rows = mixer_part(flat, 3).reshape(-1, width)
        filters = mixer_part(flat, 4).reshape(-1, width)
        taps = filters[:, seq_long : seq_long + 24].astype(F32)
        taps = taps[:, :12] + taps[:, 12:]
        shorts = [[taps[:, 3 * k + group][:, None] for k in range(3)] for group in range(3)]
        conds = [taps[:, 9 + k][:, None] for k in range(3)]
        static_rows = filters[:, :seq_long]
        projected = nn(into, normed)
        count = out_rows.shape[0]
        sequences = [by_sequence(projected[g * count : (g + 1) * count]) for g in range(3)]
        mixed_long, stored_long = mix_forward(
            [s[0] for s in sequences], live_long, shorts, conds, static_rows
        )
        mixed_short, stored_short = mix_forward(
            [s[1] for s in sequences], live_short, shorts, conds, static_rows
        )
        mixed = by_token(mixed_long, mixed_short).astype(BF16)
        sent = tn(out_rows, core_part(mixed, 1 - core)).astype(BF16)
        kept = tn(out_rows, core_part(mixed, core))
        middle = residual + own_sum(sent, kept)
        normed_mlp, mlp_stored = norm_forward(middle, gains[layer][1])
        normed_mlp = both_cores(normed_mlp)
        gate_up, kept, sent = mlp_forward(weights[layer, "mlp"], normed_mlp)
        residual = middle + own_sum(sent, kept)
        stored_all.append(
            (
                normed, norm_stored, into, out_rows, shorts, conds, stored_long, stored_short,
                mixed, normed_mlp, mlp_stored, gate_up,
            )
        )

    gone_long, gone_short = from_tokens((residual - residual_start).astype(BF16))
    output_long = input_long + gone_long.astype(F32)
    output_short = input_short + gone_short.astype(F32)

    orders = []
    for one, two in plane_orders:
        orders.append(
            tuple(
                (a * one + c * two, (b * NEAR) ^ (d * FAR))
                for a in range(2) for b in range(2) for c in range(2) for d in range(2)
            )
        )

    def scatter_grads(sources, kinds):
        plans, start = ([], 0)
        for kind in kinds:
            plans.append((start, half_rows(kind)))
            start += half_rows(kind)
        done = []
        for half, (kept, sent) in enumerate(cut(spot, sources, tuple(plans), tuple(orders))):
            one, two = plane_orders[half]
            steps = [plane[one], ("chan", NEAR), plane[two], ("chan", FAR)]
            for at, step in enumerate(steps):
                came = swap(sent, step)
                middle = kept.shape[0] // 2
                if at + 1 < len(steps):
                    sent = (kept[middle:].astype(F32) + came[middle:].astype(F32)).astype(BF16)
                    kept = (kept[:middle].astype(F32) + came[:middle].astype(F32)).astype(BF16)
                else:
                    kept = (kept.astype(F32) + came.astype(F32)).astype(BF16)
            for step in extra_steps:
                kept = (kept.astype(F32) + swap(kept, step).astype(F32)).astype(BF16)
            done.append({kind: kept[0, a : a + n] for kind, (a, n) in zip(kinds, plans)})
        return {kind: [done[0][kind], done[1][kind]] for kind in kinds}

    upstream_start = upstream
    reduced = {}
    waiting = None
    for layer in reversed(range(layers)):
        (
            normed, norm_stored, into, out_rows, shorts, conds, stored_long, stored_short,
            mixed, normed_mlp, mlp_stored, gate_up,
        ) = stored_all[layer]
        coming = both_cores(upstream.astype(BF16))
        grads, kept, sent = mlp_back(weights[layer, "mlp"], normed_mlp, gate_up, coming)
        if waiting is None:
            reduced[layer, "mlp"] = scatter_grads([grads], ["mlp"])["mlp"]
        else:
            done = scatter_grads([grads, waiting], ["mlp", "mixer"])
            reduced[layer, "mlp"] = done["mlp"]
            reduced[layer + 1, "mixer"] = done["mixer"]
        change, grad_gain_mlp = norm_back(own_sum(sent, kept), mlp_stored)
        upstream = upstream + change
        coming = both_ordered(upstream.astype(BF16))
        grad_out = nt(mixed, coming).astype(BF16)
        grad_mixed_long, grad_mixed_short = by_sequence(nn(out_rows, coming))
        back_long = mix_back(grad_mixed_long, live_long, shorts, conds, stored_long)
        back_short = mix_back(grad_mixed_short, live_short, shorts, conds, stored_short)
        grad_proj = jnp.concatenate(
            [by_token(back_long[0][group], back_short[0][group]) for group in range(3)]
        ).astype(BF16)
        grad_into = nt(grad_proj, normed).astype(BF16)
        sent = tn(into, core_part(grad_proj, 1 - core)).astype(BF16)
        kept = tn(into, core_part(grad_proj, core))
        change, grad_gain_mixer = norm_back(own_sum(sent, kept), norm_stored)
        upstream = upstream + change
        grad_static = back_long[3]
        grad_static = jnp.concatenate(
            [grad_static[:, :seq_short] + back_short[3], grad_static[:, seq_short:]], axis=1
        )
        grad_taps = [
            back_long[1][group][k] + back_short[1][group][k] for k in range(3) for group in range(3)
        ]
        grad_taps += [back_long[2][k] + back_short[2][k] for k in range(3)]
        lanes = jnp.concatenate([grad_static, jnp.stack(grad_taps, axis=1)], axis=1)
        lanes = jnp.pad(lanes, ((0, 0), (0, width - lanes.shape[1]))).astype(BF16)
        gain_rows = jnp.concatenate(
            [values.reshape(ranks, chan_width) for values in (grad_gain_mixer, grad_gain_mlp)],
            axis=1,
        )
        gain_rows = by_xor(gain_rows, place).astype(BF16)[:, None]
        gain_rows = jnp.pad(
            gain_rows,
            ((0, 0), (0, mixer_count - 5 * chans - 1), (0, width - 2 * chan_width)),
        )
        waiting = jnp.concatenate(
            [
                grad_into.reshape(3, ranks, chans, width).swapaxes(0, 1).reshape(ranks, -1, width),
                grad_out.reshape(ranks, chans, width),
                lanes.reshape(ranks, chans, width),
                gain_rows,
            ],
            axis=1,
        )
    reduced[0, "mixer"] = scatter_grads([waiting], ["mixer"])["mixer"]

    gone_long, gone_short = from_tokens((upstream - upstream_start).astype(BF16))
    back_long = grad_long + gone_long.astype(F32)
    back_short = grad_short + gone_short.astype(F32)

    def gather_grads(wanted):
        packed = []
        for half in range(2):
            one, two = plane_orders[half]
            block = jnp.concatenate([reduced[key][half] for key in wanted])[None]
            block = jnp.concatenate([block, swap(block, plane[one])])
            block = jnp.concatenate([block, swap(block, plane[two])])
            offsets = [0, one, two, one ^ two]
            packed.append(jnp.stack([block[offsets.index(p)] for p in range(pieces)]))
        packed = jnp.concatenate(packed, axis=1)
        came = swap(packed, mate)
        rows = packed.shape[1] // 2
        result = {}
        at = 0
        for layer, kind in wanted:
            count = half_rows(kind)
            sides = []
            for values in (packed, came):
                mine = jnp.concatenate(
                    [values[:, at : at + count], values[:, rows + at : rows + at + count]], axis=1
                )
                sides.append(by_xor(mine, piece).reshape(-1, width))
            result[layer, kind] = jnp.where(first, jnp.stack(sides), jnp.stack(sides[::-1]))
            at += count
        return result

    final = gather_grads(
        [(layer, kind) for layer in range(layers) for kind in ("mlp", "mixer") if (layer, kind) != (0, "mixer")]
    )
    final.update(gather_grads([(0, "mixer")]))

    def stacked(function, kind):
        return jnp.stack([function(final[layer, kind].astype(F32)) for layer in range(layers)])

    def part_of(values, index, count=1):
        rows = values[:, index * chans : (index + count) * chans]
        return rows.reshape(2, count, chans, width).swapaxes(0, 1).reshape(count, 2 * chans, width)

    def lanes_of(values, start, stop):
        return part_of(values, 4)[0][:, start:stop].T

    def gain_of(values, which):
        rows = values[:, 5 * chans, which * chan_width : (which + 1) * chan_width]
        return rows[0] + rows[1]

    def up_of(values):
        both = values[:, :width].reshape(2, width, 2, hidden)
        return jnp.moveaxis(both, 0, 2).reshape(width, 2, 2 * hidden)

    return (
        output_long,
        output_short,
        back_long,
        back_short,
        stacked(lambda values: gain_of(values, 0), "mixer"),
        stacked(lambda values: jnp.transpose(part_of(values, 0, 3), (2, 0, 1)), "mixer"),
        stacked(
            lambda values: lanes_of(values, seq_long, seq_long + 9).reshape(3, 3, chan_width),
            "mixer",
        ),
        stacked(lambda values: lanes_of(values, seq_long + 9, seq_long + 12), "mixer"),
        stacked(lambda values: lanes_of(values, 0, seq_long), "mixer"),
        stacked(lambda values: part_of(values, 3)[0], "mixer"),
        stacked(lambda values: gain_of(values, 1), "mixer"),
        stacked(up_of, "mlp"),
        stacked(lambda values: values[:, width:].reshape(2 * hidden, width), "mlp"),
    )


def solution(mesh):
    tokens = P("batch", None, "chan")
    placed = (
        tokens,
        tokens,
        P("batch"),
        P("batch"),
        P(None, "chan"),
        P(None, None, None, "chan"),
        P(None, None, None, "chan"),
        P(None, None, "chan"),
        P(None, None, "chan"),
        P(None, "chan", None),
        P(None, "chan"),
        P(None, None, None, "chan"),
        P(None, "chan", None),
        tokens,
        tokens,
    )
    return jax.shard_map(
        on_device,
        mesh=mesh,
        in_specs=placed,
        out_specs=(tokens,) * 4 + placed[4:13],
        check_vma=False,
    )
```

time: 1460 us -> 921 us (0.63)
  the two profiles are of different devices: /device:TPU:0 before, /device:TPU:9 now
where the time goes in v1:
time: 921 us; the launch traced here: 909 us
  waiting for transfers between devices  302 us (33%)
  local copies, waits for them, and re-layouts  179 us (19%)
  other arithmetic  169 us (18%)
  Pallas kernels  122 us (13%)
  starting transfers between devices  79.7 us (9%)
  matrix products  50.4 us (5%)
    ppermute x85, waiting for transfers between devices, swap(): lax.ppermute(values, axis, [(i, i ^ mask) for i in range(lax.axis_size(ax...  302 us
    ppermute x85, starting transfers between devices, swap(): lax.ppermute(values, axis, [(i, i ^ mask) for i in range(lax.axis_size(ax...  79.7 us
    unnamed x801, local copies, waits for them, and re-layouts  45.4 us
    pallas_call x2, Pallas kernels, mlp_back(): pl.pallas_call(mlp_back_kernel, grid=(ranks,), out_shape=[jax.ShapeDtypeS...  41.9 us
    pallas_call x4, Pallas kernels, assemble(): pl.pallas_call(functools.partial(assemble_kernel, plan, ranks), grid=(ran...  33.1 us
    reshape x4, local copies, waits for them, and re-layouts, up_of(): both = values[:, :width].reshape(2, width, 2, hidden)  29.9 us
    pallas_call x3, Pallas kernels, cut(): pl.pallas_call(functools.partial(cut_kernel, plans, orders), grid=(ranks,...  24.8 us
    pallas_call x2, Pallas kernels, mlp_forward(): pl.pallas_call(mlp_forward_kernel, grid=(ranks,), out_shape=[jax.ShapeDty...  22.1 us
  transfers between devices with their start and end apart: 85, of which 34 were waited for; matrix products, arithmetic and copies ran while one was open for 23% of the time, Pallas kernels for 8%

profile of v1, /device:TPU:9, one launch (start us, length us, event | category | flops | bytes accessed | tf_op | source)
XLA Modules:
  0.0 908.5 jit_solution(1526242248542205275)
XLA Ops:
  48.7 13.6 %collective-permute-done.1 = bf16[192,512]{1,0:T(8,128)(2,1)S(1)} collective-permute-done((bf16[192,512]{1,0:T(8,128)(2,1)S(1)}, bf16[192,512]{1,0:T(8,128)(2,1)S(1)}, u32[]{:S(2)}, u32[]{:S(2)}) %collective-permute-start.1) | collective-permute-done | bytes 196640 | tf_op jit(solution)/shard_map/ppermute | solution.py:42
  64.6 25.0 %collective-permute-done.2 = bf16[192,512]{1,0:T(8,128)(2,1)S(1)} collective-permute-done((bf16[192,512]{1,0:T(8,128)(2,1)S(1)}, bf16[192,512]{1,0:T(8,128)(2,1)S(1)}, u32[]{:S(2)}, u32[]{:S(2)}) %collective-permute-start.2) | collective-permute-done | bytes 196640 | tf_op jit(solution)/shard_map/ppermute | solution.py:42
  112.9 9.2 %collective-permute-done.14 = bf16[2,288,768]{2,1,0:T(8,128)(2,1)S(1)} collective-permute-done((bf16[2,288,768]{2,1,0:T(8,128)(2,1)S(1)}, bf16[2,288,768]{2,1,0:T(8,128)(2,1)S(1)}, u32[]{:S(2)}, u32[]{:S(2)}) %collective-permute-start.14) | collective-permute-done | bytes 884768 | tf_op jit(solution)/shard_map/ppermute | solution.py:42
  185.0 22.0 %collective-permute-done.18.refs_3_ = bf16[6,144,768]{2,1,0:T(8,128)(2,1)S(1)} collective-permute-done((bf16[6,144,768]{2,1,0:T(8,128)(2,1)S(1)}, bf16[6,144,768]{2,1,0:T(8,128)(2,1)S(1)}, u32[]{:S(2)}, u32[]{:S(2)}) %collective-permute-start.18) | collective-permute-done | bytes 1327136 | tf_op jit(solution)/shard_map/ppermute | solution.py:42
  209.4 9.6 %assemble.5.flat_ref = bf16[4,1152,768]{2,1,0:T(8,128)(2,1)} custom-call(s32[2]{0:T(128)S(1)} %pad_add_fusion.place_ref, bf16[1152,768]{1,0:T(8,128)(2,1)} %pad_maximum_fusion.5.own_ref, bf16[6,144,768]{2,1,0:T(8,128)(2,1)S(1)} %pad_maximum_fusion.18.refs_0_, bf16[6,144,768]{2,1,0:T(8,128)(2,1)} %collective-permute-done.16.refs_1_, ...), custom_call_target="tpu_custom_call" | custom-call | bytes 14155776 | tf_op jit(solution)/shard_map/assemble/pallas_call | solution.py:89
  219.0 11.1 %mlp_forward.2 = (bf16[4,768,768]{2,1,0:T(8,128)(2,1)}, f32[768,384]{1,0:T(8,128)S(1)}, bf16[768,384]{1,0:T(8,128)(2,1)S(1)}) custom-call(bf16[4,1152,768]{2,1,0:T(8,128)(2,1)} %assemble.5.flat_ref, bf16[768,768]{1,0:T(8,128)(2,1)} %pad_maximum_fusion.22.normed_ref), custom_call_target="tpu_custom_call" | custom-call | flops 5435817984 | bytes 11796480 | tf_op jit(solution)/shard_map/mlp_forward/pallas_call | solution.py:195
  240.1 35.7 %collective-permute-done.26.refs_3_ = bf16[6,208,768]{2,1,0:T(8,128)(2,1)S(1)} collective-permute-done((bf16[6,208,768]{2,1,0:T(8,128)(2,1)S(1)}, bf16[6,208,768]{2,1,0:T(8,128)(2,1)S(1)}, u32[]{:S(2)}, u32[]{:S(2)}) %collective-permute-start.26) | collective-permute-done | bytes 1916960 | tf_op jit(solution)/shard_map/ppermute | solution.py:42
  341.4 9.2 %assemble.7.flat_ref = bf16[4,1152,768]{2,1,0:T(8,128)(2,1)} custom-call(s32[2]{0:T(128)S(1)} %pad_add_fusion.place_ref, bf16[1152,768]{1,0:T(8,128)(2,1)S(1)} %pad_maximum_fusion.6.own_ref, bf16[6,208,768]{2,1,0:T(8,128)(2,1)} %copy-done.20, bf16[6,208,768]{2,1,0:T(8,128)(2,1)} %collective-permute-done.24.refs_1_, bf16[6,208,768]{2,1,0:T(8,128)(2,1)} %copy-done.19, ...), custom_call_target="tpu_custom_call" | custom-call | bytes 14155776 | tf_op jit(solution)/shard_map/assemble/pallas_call | solution.py:89
  351.8 11.0 %mlp_forward.3 = (bf16[4,768,768]{2,1,0:T(8,128)(2,1)}, f32[768,384]{1,0:T(8,128)S(1)}, bf16[768,384]{1,0:T(8,128)(2,1)S(1)}) custom-call(bf16[4,1152,768]{2,1,0:T(8,128)(2,1)} %assemble.7.flat_ref, bf16[768,768]{1,0:T(8,128)(2,1)} %pad_maximum_fusion.24.normed_ref), custom_call_target="tpu_custom_call" | custom-call | flops 5435817984 | bytes 11796480 | tf_op jit(solution)/shard_map/mlp_forward/pallas_call | solution.py:195
  362.8 20.7 %mlp_back.2 = (bf16[4,1152,768]{2,1,0:T(8,128)(2,1)}, f32[768,384]{1,0:T(8,128)S(1)}, bf16[768,384]{1,0:T(8,128)(2,1)S(1)}) custom-call(bf16[4,1152,768]{2,1,0:T(8,128)(2,1)} %assemble.7.flat_ref, bf16[768,768]{1,0:T(8,128)(2,1)} %pad_maximum_fusion.24.normed_ref, bf16[4,768,768]{2,1,0:T(8,128)(2,1)} %get-tuple-element.41.gate_up_ref, ...), custom_call_target="tpu_custom_call" | custom-call | flops 10871635968 | bytes 18874368 | tf_op jit(solution)/shard_map/mlp_back/pallas_call | solution.py:261
  392.6 8.9 cut.5
  432.0 10.5 %maximum_maximum_fusion.1 = bf16[1152,768]{0,1:T(8,128)(2,1)S(1)} fusion(bf16[384,128]{0,1:T(8,128)(2,1)S(1)} %get-tuple-element.524, bf16[384,128]{0,1:T(8,128)(2,1)S(1)} %get-tuple-element.523, bf16[384,512]{0,1:T(8,128)(2,1)S(1)} %fusion.265, bf16[384,128]{0,1:T(8,128)(2,1)S(1)} %get-tuple-element.522, bf16[384,128]{0,1:T(8,128)(2,1)S(1)} %get-tuple-element.521, ...), kind=kLoop, calls=%fused_computation.76 | loop fusion | flops 15925248 | bytes 3538944 | tf_op jit(solution)/shard_map/concatenate | solution.py:702
  474.3 21.2 %mlp_back.3 = (bf16[4,1152,768]{2,1,0:T(8,128)(2,1)}, f32[768,384]{1,0:T(8,128)S(1)}, bf16[768,384]{1,0:T(8,128)(2,1)S(1)}) custom-call(bf16[4,1152,768]{2,1,0:T(8,128)(2,1)} %assemble.5.flat_ref, bf16[768,768]{1,0:T(8,128)(2,1)} %pad_maximum_fusion.22.normed_ref, bf16[4,768,768]{2,1,0:T(8,128)(2,1)} %get-tuple-element.44.gate_up_ref, ...), custom_call_target="tpu_custom_call" | custom-call | flops 10871635968 | bytes 18874368 | tf_op jit(solution)/shard_map/mlp_back/pallas_call | solution.py:261
  521.3 9.8 %collective-permute-done.71 = bf16[1,144,768]{2,1,0:T(8,128)(2,1)S(1)} collective-permute-done((bf16[1,144,768]{2,1,0:T(8,128)(2,1)S(1)}, bf16[1,144,768]{2,1,0:T(8,128)(2,1)S(1)}, u32[]{:S(2)}, u32[]{:S(2)}) %collective-permute-start.71) | collective-permute-done | bytes 221216 | tf_op jit(solution)/shard_map/ppermute | solution.py:42
  563.3 10.3 %maximum_maximum_fusion.2 = bf16[1152,768]{0,1:T(8,128)(2,1)S(1)} fusion(bf16[384,128]{0,1:T(8,128)(2,1)S(1)} %get-tuple-element.518, bf16[384,128]{0,1:T(8,128)(2,1)S(1)} %get-tuple-element.517, bf16[384,512]{0,1:T(8,128)(2,1)S(1)} %fusion.262, bf16[384,128]{0,1:T(8,128)(2,1)S(1)} %get-tuple-element.516, bf16[384,128]{0,1:T(8,128)(2,1)S(1)} %get-tuple-element.515, ...), kind=kLoop, calls=%fused_computation.77 | loop fusion | flops 15925248 | bytes 3538944 | tf_op jit(solution)/shard_map/concatenate | solution.py:702
  584.4 9.3 %cut.4 = (bf16[8,208,768]{2,1,0:T(8,128)(2,1)}, bf16[8,208,768]{2,1,0:T(8,128)(2,1)}, bf16[8,208,768]{2,1,0:T(8,128)(2,1)}, bf16[8,208,768]{2,1,0:T(8,128)(2,1)}) custom-call(s32[2]{0:T(128)S(1)} %pad_add_fusion.place_ref, bf16[4,1152,768]{2,1,0:T(8,128)(2,1)} %get-tuple-element.51.refs_0_, bf16[4,512,768]{2,1,0:T(8,128)(2,1)} %pad_maximum_fusion.4.refs_1_), custom_call_target="tpu_custom_call" | custom-call | bytes 20447232 | tf_op jit(solution)/shard_map/cut/pallas_call | solution.py:136
  635.3 15.0 %collective-permute-done.64 = bf16[8,208,768]{2,1,0:T(8,128)(2,1)} collective-permute-done((bf16[8,208,768]{2,1,0:T(8,128)(2,1)}, bf16[8,208,768]{2,1,0:T(8,128)(2,1)}, u32[]{:S(2)}, u32[]{:S(2)}) %collective-permute-start.64) | collective-permute-done | bytes 2555936 | tf_op jit(solution)/shard_map/ppermute | solution.py:42
  657.9 9.1 %collective-permute-done.51 = bf16[8,64,768]{2,1,0:T(8,128)(2,1)S(1)} collective-permute-done((bf16[8,64,768]{2,1,0:T(8,128)(2,1)S(1)}, bf16[8,64,768]{2,1,0:T(8,128)(2,1)S(1)}, u32[]{:S(2)}, u32[]{:S(2)}) %collective-permute-start.51) | collective-permute-done | bytes 786464 | tf_op jit(solution)/shard_map/ppermute | solution.py:42
  669.0 10.4 %collective-permute-done.65 = bf16[4,208,768]{2,1,0:T(8,128)(2,1)S(1)} collective-permute-done((bf16[4,208,768]{2,1,0:T(8,128)(2,1)S(1)}, bf16[4,208,768]{2,1,0:T(8,128)(2,1)S(1)}, u32[]{:S(2)}, u32[]{:S(2)}) %collective-permute-start.65) | collective-permute-done | bytes 1277984 | tf_op jit(solution)/shard_map/ppermute | solution.py:42
  680.2 35.1 %collective-permute-done.52 = bf16[4,64,768]{2,1,0:T(8,128)(2,1)S(1)} collective-permute-done((bf16[4,64,768]{2,1,0:T(8,128)(2,1)S(1)}, bf16[4,64,768]{2,1,0:T(8,128)(2,1)S(1)}, u32[]{:S(2)}, u32[]{:S(2)}) %collective-permute-start.52) | collective-permute-done | bytes 393248 | tf_op jit(solution)/shard_map/ppermute | solution.py:42
  732.2 18.0 %collective-permute-done.67 = bf16[1,208,768]{2,1,0:T(8,128)(2,1)S(1)} collective-permute-done((bf16[1,208,768]{2,1,0:T(8,128)(2,1)S(1)}, bf16[1,208,768]{2,1,0:T(8,128)(2,1)S(1)}, u32[]{:S(2)}, u32[]{:S(2)}) %collective-permute-start.67) | collective-permute-done | bytes 319520 | tf_op jit(solution)/shard_map/ppermute | solution.py:42
  750.4 9.8 %collective-permute-done.77 = bf16[1,208,768]{2,1,0:T(8,128)(2,1)S(1)} collective-permute-done((bf16[1,208,768]{2,1,0:T(8,128)(2,1)S(1)}, bf16[1,208,768]{2,1,0:T(8,128)(2,1)S(1)}, u32[]{:S(2)}, u32[]{:S(2)}) %collective-permute-start.77) | collective-permute-done | bytes 319520 | tf_op jit(solution)/shard_map/ppermute | solution.py:42
  762.9 9.6 %collective-permute-done.82 = bf16[1,352,768]{2,1,0:T(8,128)(2,1)S(1)} collective-permute-done((bf16[1,352,768]{2,1,0:T(8,128)(2,1)S(1)}, bf16[1,352,768]{2,1,0:T(8,128)(2,1)S(1)}, u32[]{:S(2)}, u32[]{:S(2)}) %collective-permute-start.82) | collective-permute-done | bytes 540704 | tf_op jit(solution)/shard_map/ppermute | solution.py:42
  780.3 16.2 %collective-permute-done.55 = bf16[1,64,768]{2,1,0:T(8,128)(2,1)S(1)} collective-permute-done((bf16[1,64,768]{2,1,0:T(8,128)(2,1)S(1)}, bf16[1,64,768]{2,1,0:T(8,128)(2,1)S(1)}, u32[]{:S(2)}, u32[]{:S(2)}) %collective-permute-start.55) | collective-permute-done | bytes 98336 | tf_op jit(solution)/shard_map/ppermute | solution.py:42
  (1442 shorter events, 541.9 us)
Async XLA Ops:
  2.9 37.2 %collective-permute-start = (bf16[2,192,256]{2,1,0:T(8,128)(2,1)}, bf16[2,192,256]{2,1,0:T(8,128)(2,1)}, u32[]{:S(2)}, u32[]{:S(2)}) collective-permute-start(bf16[2,192,256]{2,1,0:T(8,128)(2,1)} %get-tuple-element.508), channel_id=1, source_target_pairs={{0,4},{4,0},{8,12},{12,8},{16,20},{20,16},{24,28},{28,24},{1,5},{5... | collective-permute-start | bytes 589832 | tf_op jit(solution)/shard_map/ppermute | solution.py:42
  30.3 68.8 %collective-permute-start.13 = (bf16[1,288,768]{2,1,0:T(8,128)(2,1)}, bf16[1,288,768]{2,1,0:T(8,128)(2,1)}, u32[]{:S(2)}, u32[]{:S(2)}) collective-permute-start(bf16[1,288,768]{2,1,0:T(8,128)(2,1)} %maximum_bitcast_fusion.7), channel_id=1, source_target_pairs={{0,3},{1,2},{2,1},{3,0},{4,7},{5,6},{6,5},{7,4},{8,11},{9,10},{10,... | collective-permute-start | bytes 1327112 | tf_op jit(solution)/shard_map/ppermute | solution.py:42
  32.2 73.5 %collective-permute-start.21 = (bf16[1,416,768]{2,1,0:T(8,128)(2,1)}, bf16[1,416,768]{2,1,0:T(8,128)(2,1)S(1)}, u32[]{:S(2)}, u32[]{:S(2)}) collective-permute-start(bf16[1,416,768]{2,1,0:T(8,128)(2,1)} %maximum_bitcast_fusion.4), channel_id=1, source_target_pairs={{0,3},{1,2},{2,1},{3,0},{4,7},{5,6},{6,5},{7,4},{8,11},{9,10},{10,... | collective-permute-start | bytes 1916936 | tf_op jit(solution)/shard_map/ppermute | solution.py:42
  45.5 44.1 %collective-permute-start.2 = (bf16[192,512]{1,0:T(8,128)(2,1)S(1)}, bf16[192,512]{1,0:T(8,128)(2,1)S(1)}, u32[]{:S(2)}, u32[]{:S(2)}) collective-permute-start(bf16[192,512]{1,0:T(8,128)(2,1)S(1)} %get-tuple-element.453), channel_id=1, source_target_pairs={{0,2},{1,3},{2,0},{3,1},{4,6},{5,7},{6,4},{7,5},{8,10},{9,11},{10,... | collective-permute-start | bytes 589832 | tf_op jit(solution)/shard_map/ppermute | solution.py:42
  45.5 50.3 %collective-permute-start.3 = (bf16[192,512]{1,0:T(8,128)(2,1)S(1)}, bf16[192,512]{1,0:T(8,128)(2,1)S(1)}, u32[]{:S(2)}, u32[]{:S(2)}) collective-permute-start(bf16[192,512]{1,0:T(8,128)(2,1)S(1)} %get-tuple-element.452), channel_id=1, source_target_pairs={{0,3},{1,2},{2,1},{3,0},{4,7},{5,6},{6,5},{7,4},{8,11},{9,10},{10,... | collective-permute-start | bytes 589832 | tf_op jit(solution)/shard_map/ppermute | solution.py:42
  62.4 38.5 %collective-permute-start.5 = (bf16[2,128,768]{2,1,0:T(8,128)(2,1)S(1)}, bf16[2,128,768]{2,1,0:T(8,128)(2,1)S(1)}, u32[]{:S(2)}, u32[]{:S(2)}) collective-permute-start(bf16[2,128,768]{2,1,0:T(8,128)(2,1)S(1)} %pad_maximum_fusion.53), channel_id=1, source_target_pairs={{0,1},{1,0},{2,3},{3,2},{4,5},{5,4},{6,7},{7,6},{8,9},{9,8},{10,11... | collective-permute-start | bytes 1179656 | tf_op jit(solution)/shard_map/ppermute | solution.py:42
  108.2 65.1 %collective-permute-start.22 = (bf16[2,416,768]{2,1,0:T(8,128)(2,1)}, bf16[2,416,768]{2,1,0:T(8,128)(2,1)}, u32[]{:S(2)}, u32[]{:S(2)}) collective-permute-start(bf16[2,416,768]{2,1,0:T(8,128)(2,1)} %pad_maximum_fusion.20), channel_id=1, source_target_pairs={{0,1},{1,0},{2,3},{3,2},{4,5},{5,4},{6,7},{7,6},{8,9},{9,8},{10,11... | collective-permute-start | bytes 3833864 | tf_op jit(solution)/shard_map/ppermute | solution.py:42
  123.3 51.4 %collective-permute-start.17 = (bf16[3,144,768]{2,1,0:T(8,128)(2,1)}, bf16[3,144,768]{2,1,0:T(8,128)(2,1)}, u32[]{:S(2)}, u32[]{:S(2)}) collective-permute-start(bf16[3,144,768]{2,1,0:T(8,128)(2,1)} %get-tuple-element.406), channel_id=1, source_target_pairs={{0,16},{4,20},{8,24},{12,28},{16,0},{20,4},{24,8},{28,12},{1,17},{... | collective-permute-start | bytes 1990664 | tf_op jit(solution)/shard_map/ppermute | solution.py:42
  124.5 52.8 %collective-permute-start.15 = (bf16[3,144,768]{2,1,0:T(8,128)(2,1)}, bf16[3,144,768]{2,1,0:T(8,128)(2,1)}, u32[]{:S(2)}, u32[]{:S(2)}) collective-permute-start(bf16[3,144,768]{2,1,0:T(8,128)(2,1)} %get-tuple-element.407), channel_id=1, source_target_pairs={{0,8},{4,12},{8,0},{12,4},{16,24},{20,28},{24,16},{28,20},{1,9},{5... | collective-permute-start | bytes 1990664 | tf_op jit(solution)/shard_map/ppermute | solution.py:42
  180.5 51.5 %collective-permute-start.25 = (bf16[3,208,768]{2,1,0:T(8,128)(2,1)S(1)}, bf16[3,208,768]{2,1,0:T(8,128)(2,1)S(1)}, u32[]{:S(2)}, u32[]{:S(2)}) collective-permute-start(bf16[3,208,768]{2,1,0:T(8,128)(2,1)S(1)} %get-tuple-element.360), channel_id=1, source_target_pairs={{0,16},{4,20},{8,24},{12,28},{16,0},{20,4},{24,8},{28,12},{1,17},{... | collective-permute-start | bytes 2875400 | tf_op jit(solution)/shard_map/ppermute | solution.py:42
  183.6 48.9 %collective-permute-start.23 = (bf16[3,208,768]{2,1,0:T(8,128)(2,1)S(1)}, bf16[3,208,768]{2,1,0:T(8,128)(2,1)}, u32[]{:S(2)}, u32[]{:S(2)}) collective-permute-start(bf16[3,208,768]{2,1,0:T(8,128)(2,1)S(1)} %get-tuple-element.361), channel_id=1, source_target_pairs={{0,8},{4,12},{8,0},{12,4},{16,24},{20,28},{24,16},{28,20},{1,9},{5... | collective-permute-start | bytes 2875400 | tf_op jit(solution)/shard_map/ppermute | solution.py:42
  232.2 43.6 %collective-permute-start.26 = (bf16[6,208,768]{2,1,0:T(8,128)(2,1)S(1)}, bf16[6,208,768]{2,1,0:T(8,128)(2,1)S(1)}, u32[]{:S(2)}, u32[]{:S(2)}) collective-permute-start(bf16[6,208,768]{2,1,0:T(8,128)(2,1)S(1)} %pad_maximum_fusion.8.refs_2_), channel_id=1, source_target_pairs={{0,8},{4,12},{8,0},{12,4},{16,24},{20,28},{24,16},{28,20},{1,9},{5... | collective-permute-start | bytes 5750792 | tf_op jit(solution)/shard_map/ppermute | solution.py:42
  234.8 43.6 %collective-permute-start.24 = (bf16[6,208,768]{2,1,0:T(8,128)(2,1)S(1)}, bf16[6,208,768]{2,1,0:T(8,128)(2,1)}, u32[]{:S(2)}, u32[]{:S(2)}) collective-permute-start(bf16[6,208,768]{2,1,0:T(8,128)(2,1)S(1)} %pad_maximum_fusion.7.refs_0_), channel_id=1, source_target_pairs={{0,16},{4,20},{8,24},{12,28},{16,0},{20,4},{24,8},{28,12},{1,17},{... | collective-permute-start | bytes 5750792 | tf_op jit(solution)/shard_map/ppermute | solution.py:42
  401.5 63.3 %collective-permute-start.68 = (bf16[8,144,768]{2,1,0:T(8,128)(2,1)}, bf16[8,144,768]{2,1,0:T(8,128)(2,1)}, u32[]{:S(2)}, u32[]{:S(2)}) collective-permute-start(bf16[8,144,768]{2,1,0:T(8,128)(2,1)} %get-tuple-element.56), channel_id=1, source_target_pairs={{0,8},{4,12},{8,0},{12,4},{16,24},{20,28},{24,16},{28,20},{1,9},{5... | collective-permute-start | bytes 5308424 | tf_op jit(solution)/shard_map/ppermute | solution.py:42
  401.9 66.0 %collective-permute-start.78 = (bf16[8,144,768]{2,1,0:T(8,128)(2,1)}, bf16[8,144,768]{2,1,0:T(8,128)(2,1)}, u32[]{:S(2)}, u32[]{:S(2)}) collective-permute-start(bf16[8,144,768]{2,1,0:T(8,128)(2,1)} %get-tuple-element.60), channel_id=1, source_target_pairs={{0,16},{4,20},{8,24},{12,28},{16,0},{20,4},{24,8},{28,12},{1,17},{... | collective-permute-start | bytes 5308424 | tf_op jit(solution)/shard_map/ppermute | solution.py:42
  470.3 37.6 %collective-permute-start.79 = (bf16[4,144,768]{2,1,0:T(8,128)(2,1)S(1)}, bf16[4,144,768]{2,1,0:T(8,128)(2,1)S(1)}, u32[]{:S(2)}, u32[]{:S(2)}) collective-permute-start(bf16[4,144,768]{2,1,0:T(8,128)(2,1)S(1)} %get-tuple-element.309), channel_id=1, source_target_pairs={{0,1},{1,0},{2,3},{3,2},{4,5},{5,4},{6,7},{7,6},{8,9},{9,8},{10,11... | collective-permute-start | bytes 2654216 | tf_op jit(solution)/shard_map/ppermute | solution.py:42
  593.7 56.6 %collective-permute-start.64 = (bf16[8,208,768]{2,1,0:T(8,128)(2,1)}, bf16[8,208,768]{2,1,0:T(8,128)(2,1)}, u32[]{:S(2)}, u32[]{:S(2)}) collective-permute-start(bf16[8,208,768]{2,1,0:T(8,128)(2,1)} %get-tuple-element.53), channel_id=1, source_target_pairs={{0,8},{4,12},{8,0},{12,4},{16,24},{20,28},{24,16},{28,20},{1,9},{5... | collective-permute-start | bytes 7667720 | tf_op jit(solution)/shard_map/ppermute | solution.py:42
  594.9 58.1 %collective-permute-start.74 = (bf16[8,208,768]{2,1,0:T(8,128)(2,1)}, bf16[8,208,768]{2,1,0:T(8,128)(2,1)}, u32[]{:S(2)}, u32[]{:S(2)}) collective-permute-start(bf16[8,208,768]{2,1,0:T(8,128)(2,1)} %get-tuple-element.58), channel_id=1, source_target_pairs={{0,16},{4,20},{8,24},{12,28},{16,0},{20,4},{24,8},{28,12},{1,17},{... | collective-permute-start | bytes 7667720 | tf_op jit(solution)/shard_map/ppermute | solution.py:42
  630.5 36.5 %collective-permute-start.51 = (bf16[8,64,768]{2,1,0:T(8,128)(2,1)S(1)}, bf16[8,64,768]{2,1,0:T(8,128)(2,1)S(1)}, u32[]{:S(2)}, u32[]{:S(2)}) collective-permute-start(bf16[8,64,768]{2,1,0:T(8,128)(2,1)S(1)} %get-tuple-element.48), channel_id=1, source_target_pairs={{0,8},{4,12},{8,0},{12,4},{16,24},{20,28},{24,16},{28,20},{1,9},{5... | collective-permute-start | bytes 2359304 | tf_op jit(solution)/shard_map/ppermute | solution.py:42
  657.0 58.7 %collective-permute-start.75 = (bf16[4,208,768]{2,1,0:T(8,128)(2,1)S(1)}, bf16[4,208,768]{2,1,0:T(8,128)(2,1)S(1)}, u32[]{:S(2)}, u32[]{:S(2)}) collective-permute-start(bf16[4,208,768]{2,1,0:T(8,128)(2,1)S(1)} %get-tuple-element.293), channel_id=1, source_target_pairs={{0,1},{1,0},{2,3},{3,2},{4,5},{5,4},{6,7},{7,6},{8,9},{9,8},{10,11... | collective-permute-start | bytes 3833864 | tf_op jit(solution)/shard_map/ppermute | solution.py:42
  667.3 48.0 %collective-permute-start.52 = (bf16[4,64,768]{2,1,0:T(8,128)(2,1)S(1)}, bf16[4,64,768]{2,1,0:T(8,128)(2,1)S(1)}, u32[]{:S(2)}, u32[]{:S(2)}) collective-permute-start(bf16[4,64,768]{2,1,0:T(8,128)(2,1)S(1)} %get-tuple-element.401), channel_id=1, source_target_pairs={{0,1},{1,0},{2,3},{3,2},{4,5},{5,4},{6,7},{7,6},{8,9},{9,8},{10,11... | collective-permute-start | bytes 1179656 | tf_op jit(solution)/shard_map/ppermute | solution.py:42
  668.0 55.6 %collective-permute-start.58 = (bf16[4,64,768]{2,1,0:T(8,128)(2,1)S(1)}, bf16[4,64,768]{2,1,0:T(8,128)(2,1)S(1)}, u32[]{:S(2)}, u32[]{:S(2)}) collective-permute-start(bf16[4,64,768]{2,1,0:T(8,128)(2,1)S(1)} %get-tuple-element.403), channel_id=1, source_target_pairs={{0,1},{1,0},{2,3},{3,2},{4,5},{5,4},{6,7},{7,6},{8,9},{9,8},{10,11... | collective-permute-start | bytes 1179656 | tf_op jit(solution)/shard_map/ppermute | solution.py:42
  679.7 45.2 %collective-permute-start.66 = (bf16[2,208,768]{2,1,0:T(8,128)(2,1)S(1)}, bf16[2,208,768]{2,1,0:T(8,128)(2,1)S(1)}, u32[]{:S(2)}, u32[]{:S(2)}) collective-permute-start(bf16[2,208,768]{2,1,0:T(8,128)(2,1)S(1)} %get-tuple-element.351), channel_id=1, source_target_pairs={{0,16},{4,20},{8,24},{12,28},{16,0},{20,4},{24,8},{28,12},{1,17},{... | collective-permute-start | bytes 1916936 | tf_op jit(solution)/shard_map/ppermute | solution.py:42
  715.3 46.1 %collective-permute-start.53 = (bf16[2,64,768]{2,1,0:T(8,128)(2,1)S(1)}, bf16[2,64,768]{2,1,0:T(8,128)(2,1)S(1)}, u32[]{:S(2)}, u32[]{:S(2)}) collective-permute-start(bf16[2,64,768]{2,1,0:T(8,128)(2,1)S(1)} %get-tuple-element.432), channel_id=1, source_target_pairs={{0,16},{4,20},{8,24},{12,28},{16,0},{20,4},{24,8},{28,12},{1,17},{... | collective-permute-start | bytes 589832 | tf_op jit(solution)/shard_map/ppermute | solution.py:42
  (458 other events, 2769.8 us)

commit v2 on v1

v2 whole, which is shorter than its diff:
```python
import functools
import math

import jax
import jax.numpy as jnp
import numpy as np
from jax import lax
from jax.experimental import pallas as pl
from jax.experimental.pallas import tpu as pltpu
from jax.sharding import PartitionSpec as P

EPS = 1e-05
BF16 = jnp.bfloat16
F32 = jnp.float32
VMEM_BYTES = 52 * 2**20
FAR, NEAR = (3, 1)


def nn(left, right):
    return lax.dot_general(left, right, (((1,), (0,)), ((), ())), preferred_element_type=F32)


def nt(left, right):
    return lax.dot_general(left, right, (((1,), (1,)), ((), ())), preferred_element_type=F32)


def tn(left, right):
    return lax.dot_general(left, right, (((0,), (0,)), ((), ())), preferred_element_type=F32)


def table(length):
    places = np.arange(length)[:, None]
    phase = (places * np.arange(length + 1)[None, :] % (2 * length)) * (np.pi / length)
    packed = np.concatenate(
        [np.cos(phase[:, :length]), np.cos(phase[:, length:]), -np.sin(phase[:, 1:length])], axis=1
    )
    return jnp.asarray(packed.astype(np.float32)).astype(BF16)


def swap(values, step):
    axis, mask = step
    return lax.ppermute(values, axis, [(i, i ^ mask) for i in range(lax.axis_size(axis))])


def pick(values, index):
    return lax.dynamic_index_in_dim(values, index, 0, keepdims=False)


def by_xor(values, index):
    return jnp.stack([pick(values, place ^ index) for place in range(values.shape[0])])


def block_copies(plan, place_ref, own_ref, buffers, flat_ref, sems, wanted):
    if wanted == 0:
        return [pltpu.make_async_copy(own_ref, flat_ref.at[0], sems.at[0, 0])]
    copies = []
    for buffer, (half, blocks, start, count) in zip(buffers, plan):
        for at, (offset, other) in enumerate(blocks):
            if other == wanted:
                row = pl.multiple_of(((place_ref[1] ^ offset) * 2 + half) * count, 16)
                copies.append(
                    pltpu.make_async_copy(
                        buffer.at[at, pl.ds(start, count)],
                        flat_ref.at[wanted, pl.ds(row, count)],
                        sems.at[wanted, len(copies)],
                    )
                )
    return copies


def fill(plan, place_ref, own_ref, buffers, flat_ref, sems, per_step):
    step = pl.program_id(0)
    ranks = flat_ref.shape[0]
    args = (plan, place_ref, own_ref, buffers, flat_ref, sems)

    @pl.when(step == 0)
    def begin():
        for wanted in range(ranks):
            for copy in block_copies(*args, wanted):
                copy.start()

    for wanted in range(ranks):

        @pl.when(step == wanted // per_step)
        def arrive():
            for copy in block_copies(*args, wanted):
                copy.wait()


def spill_copies(orders, count, start, place_ref, rows_ref, outs, sems, slot, wanted):
    copies = []
    for half, blocks in enumerate(orders):
        for at, (offset, other) in enumerate(blocks):
            if other != wanted:
                continue
            middle = len(blocks) // 2
            target = outs[2 * half + (1 if at >= middle else 0)].at[at % middle]
            row = pl.multiple_of(((place_ref[1] ^ offset) * 2 + half) * count, 16)
            copies.append(
                pltpu.make_async_copy(
                    rows_ref.at[slot, pl.ds(row, count)],
                    target.at[pl.ds(start, count)],
                    sems.at[slot, len(copies)],
                )
            )
    return copies


def grouped(refs, *counts):
    groups, at = ([], 0)
    for count in counts:
        groups.append(refs[at : at + count])
        at += count
    return groups


def whole(shape):
    return pl.BlockSpec(shape, lambda i: (0,) * len(shape))


SMEM = pl.BlockSpec(memory_space=pltpu.SMEM)
ANY = pl.BlockSpec(memory_space=pl.ANY)
PARAMS = pltpu.CompilerParams(vmem_limit_bytes=VMEM_BYTES)


def gelu_parts(gate):
    slope = math.sqrt(2.0 / math.pi)
    square = gate * gate
    bent = jnp.tanh(slope * (gate + 0.044715 * square * gate))
    gelu = 0.5 * gate * (1.0 + bent)
    grad = 0.5 * (1.0 + bent) + 0.5 * gate * (1.0 - bent * bent) * slope * (
        1.0 + 0.134145 * square
    )
    return (gelu, grad)


def add_total(total, part):
    step = pl.program_id(0)

    @pl.when(step == 0)
    def start():
        total[...] = part

    @pl.when(step > 0)
    def add():
        total[...] += part


def split_total(total, kept_ref, sent_ref):
    @pl.when(pl.program_id(0) == pl.num_programs(0) - 1)
    def finish():
        own = kept_ref.shape[1]
        kept_ref[...] = total[:, :own]
        sent_ref[...] = total[:, own:].astype(BF16)


def mlp_forward_kernel(plan, *refs):
    (place_ref, normed_ref, own_ref), buffers, outs, scratch = grouped(refs, 3, len(plan), 3, 3)
    gate_up_ref, kept_ref, sent_ref = outs
    flat_ref, total, sems = scratch
    fill(plan, place_ref, own_ref, buffers, flat_ref, sems, 1)
    step = pl.program_id(0)
    width = normed_ref.shape[0]
    hidden = flat_ref.shape[1] - width
    gate_up = tn(flat_ref[step, :width], normed_ref[...])
    gate_up_ref[0] = gate_up.astype(BF16)
    activated = (gelu_parts(gate_up[:hidden])[0] * gate_up[hidden:]).astype(BF16)
    add_total(total, tn(flat_ref[step, width:], activated))
    split_total(total, kept_ref, sent_ref)


def mlp_forward(place, rows, normed):
    own, buffers, plan, ranks = rows
    count, width = own.shape
    tokens = normed.shape[1]
    hidden = count - width
    half = tokens // 2
    return pl.pallas_call(
        functools.partial(mlp_forward_kernel, plan),
        grid=(ranks,),
        out_shape=[
            jax.ShapeDtypeStruct((ranks, 2 * hidden, tokens), BF16),
            jax.ShapeDtypeStruct((width, half), F32),
            jax.ShapeDtypeStruct((width, half), BF16),
        ],
        in_specs=[SMEM, whole((width, tokens)), ANY] + [ANY] * len(buffers),
        out_specs=[
            pl.BlockSpec((1, 2 * hidden, tokens), lambda r: (r, 0, 0)),
            whole((width, half)),
            whole((width, half)),
        ],
        scratch_shapes=[
            pltpu.VMEM((ranks, count, width), BF16),
            pltpu.VMEM((width, tokens), F32),
            pltpu.SemaphoreType.DMA((ranks, 8)),
        ],
        compiler_params=PARAMS,
        cost_estimate=pl.CostEstimate(
            flops=6 * ranks * hidden * width * tokens,
            bytes_accessed=2 * ranks * own.size + 4 * ranks * hidden * tokens,
            transcendentals=ranks * hidden * tokens,
        ),
        name="mlp_forward",
    )(place, normed, own, *buffers)


def spill(orders, count, start, place_ref, grads_ref, outs, sems, per_step):
    step = pl.program_id(0)
    ranks = per_step * pl.num_programs(0)
    for wanted in range(ranks):
        at = wanted // per_step
        slot = (at % 2) * per_step + wanted % per_step

        @pl.when(step == at)
        def leave():
            for copy in spill_copies(
                orders, count, start, place_ref, grads_ref, outs, sems, slot, wanted
            ):
                copy.start()


def spill_wait(orders, count, start, place_ref, grads_ref, outs, sems, per_step, last):
    step = pl.program_id(0)
    steps = 4 // per_step
    for wanted in range(4):
        at = wanted // per_step
        slot = (at % 2) * per_step + wanted % per_step
        due = steps - 1 if last else at + 2
        if last and at + 2 < steps:
            continue
        if not last and at + 2 >= steps:
            continue

        @pl.when(step == due)
        def gone():
            for copy in spill_copies(
                orders, count, start, place_ref, grads_ref, outs, sems, slot, wanted
            ):
                copy.wait()


def mlp_back_kernel(plan, orders, start, aliased, *refs):
    (place_ref, normed_ref, coming_ref, gate_up_ref, own_ref), buffers, _, outs, scratch = grouped(
        refs, 5, len(plan), 4 if aliased else 0, 6, 5
    )
    kept_ref, sent_ref = outs[:2]
    flat_ref, grads_ref, total, sems, out_sems = scratch
    fill(plan, place_ref, own_ref, buffers, flat_ref, sems, 1)
    step = pl.program_id(0)
    width = normed_ref.shape[0]
    hidden = flat_ref.shape[1] - width
    count = flat_ref.shape[1] // (2 * len(orders[0]) // flat_ref.shape[0])
    spilled = (orders, count, start, place_ref, grads_ref, outs[2:], out_sems, 1)
    spill_wait(*spilled, False)
    slot = step % 2
    gate = gate_up_ref[0, :hidden].astype(F32)
    up = gate_up_ref[0, hidden:].astype(F32)
    grad_act = nn(flat_ref[step, width:], coming_ref[...])
    gelu, slope = gelu_parts(gate)
    activated = (gelu * up).astype(BF16)
    grad_gate = (grad_act * up * slope).astype(BF16)
    grad_up = (grad_act * gelu).astype(BF16)
    grads_ref[slot, width:] = nt(activated, coming_ref[...]).astype(BF16)
    grads_ref[slot, :width, :hidden] = nt(normed_ref[...], grad_gate).astype(BF16)
    grads_ref[slot, :width, hidden:] = nt(normed_ref[...], grad_up).astype(BF16)
    spill(*spilled)
    add_total(
        total,
        nn(flat_ref[step, :width, :hidden], grad_gate)
        + nn(flat_ref[step, :width, hidden:], grad_up),
    )
    split_total(total, kept_ref, sent_ref)
    spill_wait(*spilled, True)


def mlp_back(place, rows, normed, gate_up, coming, orders, start, into):
    own, buffers, plan, ranks = rows
    count, width = own.shape
    tokens = normed.shape[1]
    hidden = count - width
    half = tokens // 2
    aliased = not isinstance(into, int)
    blocks = jax.ShapeDtypeStruct(
        (len(orders[0]) // 2, into[0].shape[1] if aliased else into, width), BF16
    )
    first_alias = 5 + len(buffers)
    results = pl.pallas_call(
        functools.partial(mlp_back_kernel, plan, orders, start, aliased),
        grid=(ranks,),
        out_shape=[
            jax.ShapeDtypeStruct((width, half), F32),
            jax.ShapeDtypeStruct((width, half), BF16),
        ]
        + [blocks] * 4,
        in_specs=[
            SMEM,
            whole((width, tokens)),
            whole((width, tokens)),
            pl.BlockSpec((1, 2 * hidden, tokens), lambda r: (r, 0, 0)),
            ANY,
        ]
        + [ANY] * (len(buffers) + (4 if aliased else 0)),
        out_specs=[whole((width, half)), whole((width, half))] + [ANY] * 4,
        input_output_aliases={first_alias + i: 2 + i for i in range(4)} if aliased else {},
        scratch_shapes=[
            pltpu.VMEM((ranks, count, width), BF16),
            pltpu.VMEM((2, count, width), BF16),
            pltpu.VMEM((width, tokens), F32),
            pltpu.SemaphoreType.DMA((ranks, 8)),
            pltpu.SemaphoreType.DMA((2, 8)),
        ],
        compiler_params=PARAMS,
        cost_estimate=pl.CostEstimate(
            flops=12 * ranks * hidden * width * tokens,
            bytes_accessed=4 * ranks * own.size + 4 * ranks * hidden * tokens,
            transcendentals=ranks * hidden * tokens,
        ),
        name="mlp_back",
    )(place, normed, coming, gate_up, own, *buffers, *(into if aliased else ()))
    return (results[0], results[1], results[2:])


def delayed(layout, values, by):
    return jnp.where(layout["inside"] >= by, pltpu.roll(values, by, 1), 0.0)


def advanced(layout, values, by):
    moved = pltpu.roll(values, layout["tokens"] - by, 1)
    return jnp.where(layout["inside"] < layout["length"] - by, moved, 0.0)


def layout_of(long, short, tokens):
    lane = lax.broadcasted_iota(jnp.int32, (1, tokens), 1)
    return {
        "long": long,
        "short": short,
        "tokens": tokens,
        "inside": jnp.where(lane < long, lane, (lane - long) % short),
        "length": jnp.where(lane < long, long, short),
    }


def taps_forward(layout, values, taps):
    return (
        taps[0] * values
        + taps[1] * delayed(layout, values, 1)
        + taps[2] * delayed(layout, values, 2)
    )


def taps_back(layout, values, taps):
    return (
        taps[0] * values
        + taps[1] * advanced(layout, values, 1)
        + taps[2] * advanced(layout, values, 2)
    )


def taps_grad(layout, grads, values):
    moved = [values, delayed(layout, values, 1), delayed(layout, values, 2)]
    return [jnp.sum(grads * value, axis=1, keepdims=True) for value in moved]


def sequences(layout, values):
    long, short = (layout["long"], layout["short"])
    shorts = [values[:, at : at + short] for at in range(long, layout["tokens"], short)]
    return (values[:, :long], jnp.concatenate(shorts, axis=0))


def rejoined(long_part, short_part):
    rows = long_part.shape[0]
    shorts = [short_part[at * rows : (at + 1) * rows] for at in range(short_part.shape[0] // rows)]
    return jnp.concatenate([long_part] + shorts, axis=1)


def repeated(values, times):
    return jnp.concatenate([values] * times, axis=0) if times > 1 else values


def at_edge(edge, edge_values, others):
    head = jnp.where(edge[:, :128], edge_values, others[:, :128])
    return jnp.concatenate([head, others[:, 128:]], axis=1) if others.shape[1] > 128 else head


def turned_back(real_part, imag_part, cosines):
    return nt(jnp.concatenate([real_part.astype(BF16), imag_part.astype(BF16)], axis=1), cosines)


def filter_of(gated, shaped, static_rows, cosines):
    rows, length = gated.shape
    times = rows // static_rows.shape[0]
    edge = lax.broadcasted_iota(jnp.int32, (1, length), 1) == 0
    spectra = nn(jnp.concatenate([gated, shaped], axis=0).astype(BF16), cosines)
    shaped_re, shaped_im = (spectra[rows:, :length], spectra[rows:, length:])
    fixed = nn(static_rows, cosines)
    fixed_re = repeated(fixed[:, :length], times)
    fixed_im = repeated(fixed[:, length:], times)
    square = shaped_im * shaped_im
    power = shaped_re * shaped_re + jnp.where(edge, 0.0, square) + length
    inv_root = lax.rsqrt(power)
    power_last = square[:, :128] + length
    inv_root_last = lax.rsqrt(power_last)
    scale = 1.0 / math.sqrt(length)
    return {
        "length": length,
        "times": times,
        "edge": edge,
        "weight": jnp.where(edge, 0.5 / length, 1.0 / length),
        "signal_re": spectra[:rows, :length],
        "signal_im": spectra[:rows, length:],
        "shaped_re": shaped_re,
        "shaped_im": shaped_im,
        "fixed_im": fixed_im,
        "fixed_sine": jnp.where(edge, 0.0, fixed_im),
        "slope": scale * inv_root,
        "slope_last": scale * inv_root_last,
        "filter_re": fixed_re + (power * inv_root * scale - 1.0),
        "filter_last": fixed_im[:, :128] + (power_last * inv_root_last * scale - 1.0),
    }


def filtered(parts, cosines):
    signal_re, signal_im = (parts["signal_re"], parts["signal_im"])
    product_re = parts["filter_re"] * signal_re - parts["fixed_sine"] * signal_im
    product_im = at_edge(
        parts["edge"],
        parts["filter_last"] * signal_im[:, :128],
        parts["filter_re"] * signal_im + parts["fixed_im"] * signal_re,
    )
    return turned_back(product_re * parts["weight"], product_im * parts["weight"], cosines)


def filter_back(parts, grad_out, cosines):
    length, times, edge = (parts["length"], parts["times"], parts["edge"])
    signal_re, signal_im = (parts["signal_re"], parts["signal_im"])
    filter_re, fixed_im = (parts["filter_re"], parts["fixed_im"])
    turned = nn(grad_out.astype(BF16), cosines)
    product_re = turned[:, :length] * parts["weight"]
    product_im = turned[:, length:] * parts["weight"]
    grad_signal_re = filter_re * product_re + parts["fixed_sine"] * product_im
    grad_signal_im = at_edge(
        edge,
        parts["filter_last"] * product_im[:, :128],
        filter_re * product_im - fixed_im * product_re,
    )
    crossed = signal_im * product_im
    grad_filter = signal_re * product_re + jnp.where(edge, 0.0, crossed)
    grad_fixed_im = at_edge(
        edge, crossed[:, :128], signal_re * product_im - signal_im * product_re
    )
    slope = grad_filter * parts["slope"]
    grad_shaped_re = slope * parts["shaped_re"]
    grad_shaped_im = (
        at_edge(edge, crossed[:, :128] * parts["slope_last"], slope) * parts["shaped_im"]
    )
    count = grad_out.shape[0]
    rows = count // times
    grad_static = turned_back(
        sum(grad_filter[i * rows : (i + 1) * rows] for i in range(times)),
        sum(grad_fixed_im[i * rows : (i + 1) * rows] for i in range(times)),
        cosines,
    )
    back = turned_back(
        jnp.concatenate([grad_signal_re, grad_shaped_re], axis=0),
        jnp.concatenate([grad_signal_im, grad_shaped_im], axis=0),
        cosines,
    )
    return (back[:count], back[count:], grad_static)


def mixer_rows_of(flat_ref, step, per_step, chans):
    def rows(index):
        return [
            flat_ref[step * per_step + i, index * chans : (index + 1) * chans]
            for i in range(per_step)
        ]

    into = jnp.concatenate(rows(0) + rows(1) + rows(2), axis=0)
    filters = jnp.concatenate(rows(4), axis=0)
    return (into, jnp.concatenate(rows(3), axis=0), filters)


def mixer_taps(filters, start):
    lanes = filters[:, start : start + 128].astype(F32)
    taps = [lanes[:, k : k + 1] + lanes[:, 12 + k : 13 + k] for k in range(12)]
    return ([[taps[3 * k + group] for k in range(3)] for group in range(3)], taps[9:])


def own_lanes(ref, which, layout):
    half_long, short = (layout["long"] // 2, layout["short"])
    at = pl.multiple_of(which * half_long, 128)
    after = pl.multiple_of(layout["long"] + which * short, 128)
    return jnp.concatenate([ref[:, pl.ds(at, half_long)], ref[:, pl.ds(after, short)]], axis=1)


def mixer_forward_kernel(plan, sizes, *refs):
    inputs, buffers, outs, scratch = grouped(refs, 6, len(plan), 4, 4)
    place_ref, live_ref, long_ref, short_ref, normed_ref, own_ref = inputs
    proj_ref, long_out_ref, kept_ref, sent_ref = outs
    flat_ref, mixed_ref, total, sems = scratch
    long, short, chans, per_step = sizes
    fill(plan, place_ref, own_ref, buffers, flat_ref, sems, per_step)
    step = pl.program_id(0)
    layout = layout_of(long, short, normed_ref.shape[1])
    into, out_rows, filters = mixer_rows_of(flat_ref, step, per_step, chans)
    short_taps, cond_taps = mixer_taps(filters, long)
    rows = per_step * chans
    proj = nn(into, normed_ref[...])
    proj_ref[0] = proj.astype(BF16)
    query, key_part, value_part = (
        taps_forward(layout, proj[g * rows : (g + 1) * rows], short_taps[g]) for g in range(3)
    )
    gated = key_part * value_part * live_ref[:1]
    shaped = taps_forward(layout, gated, cond_taps)
    gated_parts, shaped_parts = (sequences(layout, gated), sequences(layout, shaped))
    results = [
        filtered(
            filter_of(gated_parts[i], shaped_parts[i], filters[:, :length], ref[...]), ref[...]
        )
        for i, (length, ref) in enumerate(((long, long_ref), (short, short_ref)))
    ]
    long_out = rejoined(*results)
    long_out_ref[0] = long_out.astype(BF16)
    mixed_ref[...] = (query * long_out).astype(BF16)
    core = place_ref[0]
    half = kept_ref.shape[1]
    part_kept = tn(out_rows, own_lanes(mixed_ref, core, layout))
    part_sent = tn(out_rows, own_lanes(mixed_ref, 1 - core, layout))
    add_total(total, jnp.concatenate([part_kept, part_sent], axis=1))
    split_total(total, kept_ref, sent_ref)


def mixer_forward(place, rows, normed, live, tables, sizes):
    own, buffers, plan, ranks = rows
    count, width = own.shape
    tokens = normed.shape[1]
    half = tokens // 2
    chans, per_step = sizes[2:]
    steps = ranks // per_step
    group = per_step * chans
    return pl.pallas_call(
        functools.partial(mixer_forward_kernel, plan, sizes),
        grid=(steps,),
        out_shape=[
            jax.ShapeDtypeStruct((steps, 3 * group, tokens), BF16),
            jax.ShapeDtypeStruct((steps, group, tokens), BF16),
            jax.ShapeDtypeStruct((width, half), F32),
            jax.ShapeDtypeStruct((width, half), BF16),
        ],
        in_specs=[SMEM, whole(live.shape)]
        + [whole(t.shape) for t in tables]
        + [whole((width, tokens)), ANY]
        + [ANY] * len(buffers),
        out_specs=[
            pl.BlockSpec((1, 3 * group, tokens), lambda r: (r, 0, 0)),
            pl.BlockSpec((1, group, tokens), lambda r: (r, 0, 0)),
            whole((width, half)),
            whole((width, half)),
        ],
        scratch_shapes=[
            pltpu.VMEM((ranks, count, width), BF16),
            pltpu.VMEM((group, tokens), BF16),
            pltpu.VMEM((width, tokens), F32),
            pltpu.SemaphoreType.DMA((ranks, 8)),
        ],
        compiler_params=PARAMS,
        cost_estimate=pl.CostEstimate(
            flops=2 * ranks * chans * (4 * width * tokens + 8 * sizes[0] * sizes[0]),
            bytes_accessed=2 * ranks * own.size,
            transcendentals=ranks * chans * 2 * tokens,
        ),
        name="mixer_forward",
    )(place, live, *tables, normed, own, *buffers)


def mixer_back_kernel(plan, orders, start, sizes, *refs):
    inputs, buffers, outs, scratch = grouped(refs, 9, len(plan), 6, 6)
    place_ref, live_ref, long_ref, short_ref, normed_ref, coming_ref = inputs[:6]
    proj_ref, long_out_ref, own_ref = inputs[6:]
    kept_ref, sent_ref = outs[:2]
    flat_ref, grads_ref, total, rows_ref, sems, out_sems = scratch
    long, short, chans, per_step = sizes
    fill(plan, place_ref, own_ref, buffers, flat_ref, sems, per_step)
    step = pl.program_id(0)
    layout = layout_of(long, short, normed_ref.shape[1])
    into, out_rows, filters = mixer_rows_of(flat_ref, step, per_step, chans)
    short_taps, cond_taps = mixer_taps(filters, long)
    rows = per_step * chans
    grad_mixed = nn(out_rows, coming_ref[...])
    proj = [proj_ref[0, g * rows : (g + 1) * rows].astype(F32) for g in range(3)]
    query, key_part, value_part = (taps_forward(layout, proj[g], short_taps[g]) for g in range(3))
    live = live_ref[:1]
    gated = key_part * value_part * live
    shaped = taps_forward(layout, gated, cond_taps)
    long_out = long_out_ref[0].astype(F32)
    mixed = (query * long_out).astype(BF16)
    grad_query = grad_mixed * long_out
    grad_long_out = sequences(layout, grad_mixed * query)
    gated_parts, shaped_parts = (sequences(layout, gated), sequences(layout, shaped))
    backs = [
        filter_back(
            filter_of(gated_parts[i], shaped_parts[i], filters[:, :length], ref[...]),
            grad_long_out[i],
            ref[...],
        )
        for i, (length, ref) in enumerate(((long, long_ref), (short, short_ref)))
    ]
    grad_gated = rejoined(backs[0][0], backs[1][0])
    grad_shaped = rejoined(backs[0][1], backs[1][1])
    grad_static = jnp.concatenate(
        [backs[0][2][:, :short] + backs[1][2], backs[0][2][:, short:]], axis=1
    )
    grad_cond = taps_grad(layout, grad_shaped, gated)
    grad_gated = (grad_gated + taps_back(layout, grad_shaped, cond_taps)) * live
    grads = (grad_query, grad_gated * value_part, grad_gated * key_part)
    grad_taps = [taps_grad(layout, grads[g], proj[g]) for g in range(3)]
    grad_proj = jnp.concatenate(
        [taps_back(layout, grads[g], short_taps[g]) for g in range(3)], axis=0
    ).astype(BF16)
    lane = lax.broadcasted_iota(jnp.int32, (1, flat_ref.shape[2] - long), 1)
    lanes = sum(
        jnp.where(lane == 3 * k + group, grad_taps[group][k], 0.0)
        for k in range(3)
        for group in range(3)
    )
    lanes += sum(jnp.where(lane == 9 + k, grad_cond[k], 0.0) for k in range(3))
    grad_into = nt(grad_proj, normed_ref[...]).astype(BF16)
    grad_out = nt(mixed, coming_ref[...]).astype(BF16)
    grad_filters = jnp.concatenate([grad_static, lanes], axis=1).astype(BF16)
    for i in range(per_step):
        part = slice(i * chans, (i + 1) * chans)
        at = step * per_step + i
        for g in range(3):
            grads_ref[at, g * chans : (g + 1) * chans] = grad_into[g * rows : (g + 1) * rows][part]
        grads_ref[at, 3 * chans : 4 * chans] = grad_out[part]
        grads_ref[at, 4 * chans : 5 * chans] = grad_filters[part]
        spare = flat_ref.shape[1] - 5 * chans
        if spare:
            grads_ref[at, 5 * chans :] = jnp.zeros((spare, flat_ref.shape[2]), BF16)
    count = flat_ref.shape[1] // (2 * len(orders[0]) // flat_ref.shape[0])
    spilled = (orders, count, start, place_ref, grads_ref, outs[2:], out_sems, per_step)
    spill(*spilled)
    add_total(total, tn(into, grad_proj))

    @pl.when(step == pl.num_programs(0) - 1)
    def finish():
        core = place_ref[0]
        kept_ref[...] = own_lanes(total, core, layout)
        sent_ref[...] = own_lanes(total, 1 - core, layout).astype(BF16)

    spill_wait(*spilled, True)


def mixer_back(place, rows, normed, coming, proj, long_out, live, tables, sizes, orders, start, into):
    own, buffers, plan, ranks = rows
    count, width = own.shape
    tokens = normed.shape[1]
    half = tokens // 2
    chans, per_step = sizes[2:]
    steps = ranks // per_step
    group = per_step * chans
    blocks = jax.ShapeDtypeStruct((len(orders[0]) // 2, into, width), BF16)
    results = pl.pallas_call(
        functools.partial(mixer_back_kernel, plan, orders, start, sizes),
        grid=(steps,),
        out_shape=[
            jax.ShapeDtypeStruct((width, half), F32),
            jax.ShapeDtypeStruct((width, half), BF16),
        ]
        + [blocks] * 4,
        in_specs=[SMEM, whole(live.shape)]
        + [whole(t.shape) for t in tables]
        + [
            whole((width, tokens)),
            whole((width, tokens)),
            pl.BlockSpec((1, 3 * group, tokens), lambda r: (r, 0, 0)),
            pl.BlockSpec((1, group, tokens), lambda r: (r, 0, 0)),
            ANY,
        ]
        + [ANY] * len(buffers),
        out_specs=[whole((width, half)), whole((width, half))] + [ANY] * 4,
        scratch_shapes=[
            pltpu.VMEM((ranks, count, width), BF16),
            pltpu.VMEM((ranks, count, width), BF16),
            pltpu.VMEM((width, tokens), F32),
            pltpu.VMEM((8, 128), F32),
            pltpu.SemaphoreType.DMA((ranks, 8)),
            pltpu.SemaphoreType.DMA((ranks, 8)),
        ],
        compiler_params=PARAMS,
        cost_estimate=pl.CostEstimate(
            flops=2 * ranks * chans * (8 * width * tokens + 16 * sizes[0] * sizes[0]),
            bytes_accessed=4 * ranks * own.size,
            transcendentals=ranks * chans * 2 * tokens,
        ),
        name="mixer_back",
    )(place, live, *tables, normed, coming, proj, long_out, own, *buffers)
    return (results[0], results[1], results[2:])


def final_copies(plan, start, place_ref, sources, flat_ref, sems):
    count = flat_ref.shape[1] // (2 * len(plan[0]))
    copies = []
    for side in range(2):
        core = place_ref[0] if side == 0 else 1 - place_ref[0]
        for half in range(2):
            for at, offset in enumerate(plan[half]):
                row = pl.multiple_of(((place_ref[1] ^ offset) * 2 + half) * count, 16)
                copies.append(
                    pltpu.make_async_copy(
                        sources[2 * side + half].at[at, pl.ds(start, count)],
                        flat_ref.at[core, pl.ds(row, count)],
                        sems.at[len(copies)],
                    )
                )
    return copies


def final_mlp_kernel(plan, start, aliased, *refs):
    (place_ref,), sources, _, outs, (flat_ref, sems) = grouped(
        refs, 1, 4, 2 if aliased else 0, 2, 2
    )
    up_ref, down_ref = outs
    step = pl.program_id(0)
    width = flat_ref.shape[2]
    hidden = flat_ref.shape[1] - width

    @pl.when(step == 0)
    def gather():
        copies = final_copies(plan, start, place_ref, sources, flat_ref, sems)
        for copy in copies:
            copy.start()
        for copy in copies:
            copy.wait()

    rows = up_ref.shape[1]
    part = pl.ds(pl.multiple_of(step * rows, 16), rows)
    for core in range(2):
        lanes = slice(core * hidden, (core + 1) * hidden)
        up_ref[0, :, 0, lanes] = flat_ref[core, part, :hidden].astype(F32)
        up_ref[0, :, 1, lanes] = flat_ref[core, part, hidden:].astype(F32)
    each = down_ref.shape[1]
    per_core = hidden // each
    at = pl.multiple_of(width + (step % per_core) * each, 16)
    down_ref[0] = flat_ref[step // per_core, pl.ds(at, each)].astype(F32)


def final_mlp(place, sources, plan, start, count, layer, layers, into):
    width = sources[0].shape[2]
    hidden = count - width
    steps = 4
    aliased = into is not None
    return pl.pallas_call(
        functools.partial(final_mlp_kernel, plan, start, aliased),
        grid=(steps,),
        out_shape=[
            jax.ShapeDtypeStruct((layers, width, 2, 2 * hidden), F32),
            jax.ShapeDtypeStruct((layers, 2 * hidden, width), F32),
        ],
        in_specs=[SMEM] + [ANY] * (6 if aliased else 4),
        out_specs=[
            pl.BlockSpec((1, width // steps, 2, 2 * hidden), lambda i: (layer, i, 0, 0)),
            pl.BlockSpec((1, 2 * hidden // steps, width), lambda i: (layer, i, 0)),
        ],
        input_output_aliases={5: 0, 6: 1} if aliased else {},
        scratch_shapes=[
            pltpu.VMEM((2, count, width), BF16),
            pltpu.SemaphoreType.DMA((4 * len(plan[0]),)),
        ],
        compiler_params=PARAMS,
        cost_estimate=pl.CostEstimate(
            flops=0, bytes_accessed=12 * count * width, transcendentals=0
        ),
        name="final_mlp",
    )(place, *sources, *(into if aliased else ()))


def final_mixer_kernel(plan, start, chans, aliased, *refs):
    (place_ref,), sources, _, outs, (flat_ref, sems) = grouped(
        refs, 1, 4, 3 if aliased else 0, 3, 2
    )
    into_ref, out_ref, filter_ref = outs
    copies = final_copies(plan, start, place_ref, sources, flat_ref, sems)
    for copy in copies:
        copy.start()
    for copy in copies:
        copy.wait()
    for core in range(2):
        lanes = slice(core * chans, (core + 1) * chans)
        for g in range(3):
            into_ref[0, g, lanes] = flat_ref[core, g * chans : (g + 1) * chans].astype(F32)
        out_ref[0, lanes] = flat_ref[core, 3 * chans : 4 * chans].astype(F32)
        filter_ref[0, lanes] = flat_ref[core, 4 * chans : 5 * chans].astype(F32)


def final_mixer(place, sources, plan, start, count, chans, layer, layers, into):
    width = sources[0].shape[2]
    aliased = into is not None
    return pl.pallas_call(
        functools.partial(final_mixer_kernel, plan, start, chans, aliased),
        grid=(1,),
        out_shape=[
            jax.ShapeDtypeStruct((layers, 3, 2 * chans, width), F32),
            jax.ShapeDtypeStruct((layers, 2 * chans, width), F32),
            jax.ShapeDtypeStruct((layers, 2 * chans, width), F32),
        ],
        in_specs=[SMEM] + [ANY] * (7 if aliased else 4),
        out_specs=[
            pl.BlockSpec((1, 3, 2 * chans, width), lambda i: (layer, 0, 0, 0)),
            pl.BlockSpec((1, 2 * chans, width), lambda i: (layer, 0, 0)),
            pl.BlockSpec((1, 2 * chans, width), lambda i: (layer, 0, 0)),
        ],
        input_output_aliases={5: 0, 6: 1, 7: 2} if aliased else {},
        scratch_shapes=[
            pltpu.VMEM((2, count, width), BF16),
            pltpu.SemaphoreType.DMA((4 * len(plan[0]),)),
        ],
        compiler_params=PARAMS,
        cost_estimate=pl.CostEstimate(
            flops=0, bytes_accessed=12 * count * width, transcendentals=0
        ),
        name="final_mixer",
    )(place, *sources, *(into if aliased else ()))


def norm_forward(values, gain):
    average = jnp.mean(values, axis=0, keepdims=True)
    centered = values - average
    inv_std = lax.rsqrt(jnp.mean(centered * centered, axis=0, keepdims=True) + EPS)
    normal_rows = centered * inv_std
    return ((normal_rows * gain).astype(BF16), (normal_rows, inv_std, gain))


def norm_back(grads, stored):
    normal_rows, inv_std, gain = stored
    scaled = grads * gain
    total = jnp.mean(scaled, axis=0, keepdims=True)
    crossed = jnp.mean(scaled * normal_rows, axis=0, keepdims=True)
    gain_grad = jnp.sum(grads * normal_rows, axis=1)
    return (inv_std * (scaled - total - normal_rows * crossed), gain_grad)


def on_device(
    input_long,
    input_short,
    length_long,
    length_short,
    gain_mixer,
    weight_in,
    short_taps,
    cond_taps,
    static_filter,
    weight_out,
    gain_mlp,
    weight_up,
    weight_down,
    grad_long,
    grad_short,
):
    count_long, seq_long, chan_width = input_long.shape
    count_short, seq_short = (input_short.shape[0], input_short.shape[1])
    layers = weight_in.shape[0]
    ranks = lax.axis_size("chan")
    pairs = lax.axis_size("batch") // 2
    place = lax.axis_index("chan")
    core = lax.axis_index("batch") % 2
    pair = lax.axis_index("batch") // 2
    width = chan_width * ranks
    hidden = weight_down.shape[1] // 2
    chans = chan_width // 2
    half_long = seq_long // 2
    tokens = half_long + seq_short
    mate = ("batch", 1)
    first = core == 0
    pieces = 4
    piece = pair % pieces
    plane = {1: ("batch", 2), 2: ("batch", 4)}
    extra_steps = []
    mask = 2 * pieces
    while mask < 2 * pairs:
        extra_steps.append(("batch", mask))
        mask *= 2
    spot = jnp.stack([core, piece]).astype(jnp.int32)
    plane_orders = ((1, 2), (2, 1))

    def exchange(blocks):
        came = [pick(blocks, place)]
        came += [swap(pick(blocks, place ^ r), ("chan", r)) for r in range(1, ranks)]
        return by_xor(jnp.stack(came), place)

    def to_tokens(long_rows, short_rows, extra=None):
        turned = jnp.swapaxes(long_rows, 1, 2).astype(BF16)
        halves = jnp.stack([turned[:, :, :half_long], turned[:, :, half_long:]])
        kept = pick(halves, core)
        came = swap(pick(halves, 1 - core), mate)
        ordered = jnp.where(first, jnp.concatenate([kept, came]), jnp.concatenate([came, kept]))
        parts = [ordered, jnp.swapaxes(short_rows, 1, 2).astype(BF16)]
        if extra is not None:
            parts.append(jnp.broadcast_to(extra[None], (ranks,) + extra.shape))
        gathered = exchange(jnp.concatenate(parts, axis=2))
        return gathered.reshape(width, -1)

    def from_tokens(values):
        gathered = exchange(values.reshape(ranks, chan_width, -1))
        halves = gathered[:, :, :half_long].reshape(2, count_long, chan_width, half_long)
        kept = pick(halves, core)
        came = swap(pick(halves, 1 - core), mate)
        ordered = jnp.where(
            first, jnp.concatenate([kept, came], axis=2), jnp.concatenate([came, kept], axis=2)
        )
        short_part = jnp.swapaxes(gathered[:, :, half_long:tokens], 1, 2)
        result = (jnp.swapaxes(ordered, 1, 2), short_part)
        return result + ((gathered[:, :, tokens:],) if values.shape[1] > tokens else ())

    def both_cores(values):
        return jnp.concatenate([values, swap(values, mate)], axis=1)

    def both_ordered(values):
        came = swap(values, mate)
        low, high = (jnp.where(first, values, came), jnp.where(first, came, values))
        return jnp.concatenate(
            [low[:, :half_long], high[:, :half_long], low[:, half_long:], high[:, half_long:]],
            axis=1,
        )

    def own_sum(sent, kept):
        return kept + swap(sent, mate).astype(F32)

    def mlp_rows(layer):
        up = lax.dynamic_slice_in_dim(weight_up[layer], core * hidden, hidden, 2)
        down = lax.dynamic_slice_in_dim(weight_down[layer], core * hidden, hidden, 0)
        return jnp.concatenate([up.reshape(width, 2 * hidden), down])

    def mixer_rows(layer):
        into = jnp.transpose(weight_in[layer], (1, 2, 0))
        into = lax.dynamic_slice_in_dim(into, core * chans, chans, 1)
        out = lax.dynamic_slice_in_dim(weight_out[layer], core * chans, chans, 0)
        taps = jnp.concatenate([short_taps[layer].reshape(9, chan_width), cond_taps[layer]]).T
        coarse = lax.reduce_precision(taps, 8, 7)
        static = jnp.concatenate([static_filter[layer].T, coarse, taps - coarse], axis=1)
        static = jnp.pad(static.astype(BF16), ((0, 0), (0, width - static.shape[1])))
        static = lax.dynamic_slice_in_dim(static, core * chans, chans, 0)
        spare = jnp.zeros((mixer_count - 5 * chans, width), BF16)
        return jnp.concatenate([into.reshape(3 * chans, width), out, static, spare])

    mixer_count = -(-5 * chans // (32 * pieces)) * 32 * pieces
    mlp_count = width + hidden
    own_rows = [
        {"mixer": mixer_rows(layer), "mlp": mlp_rows(layer)} for layer in range(layers)
    ]

    def half_rows(kind):
        return (mixer_count if kind == "mixer" else mlp_count) // (2 * pieces)

    def own_block(layer, kind, half):
        count = half_rows(kind)
        return lax.dynamic_slice_in_dim(
            own_rows[layer][kind], (piece * 2 + half) * count, count, 0
        )

    def gather_weights(wanted):
        parts = [own_block(layer, kind, half) for half in range(2) for layer, kind in wanted]
        block = jnp.concatenate(parts)[None]
        rows = block.shape[1] // 2
        far = swap(block, ("chan", FAR))
        near = swap(jnp.concatenate([block, far]), ("chan", NEAR))
        others = (FAR, NEAR, FAR ^ NEAR)
        foreign = jnp.concatenate([far, near])
        buffers, blocks = ([], [])
        for half in range(2):
            held = foreign[:, half * rows : (half + 1) * rows]
            held_blocks = [(0, other) for other in others]
            one, two = plane_orders[half]
            held = jnp.concatenate([held, swap(held, plane[one])])
            held_blocks = held_blocks + [(one, other) for other in others]
            buffers += [held, swap(held, plane[two])]
            blocks += [held_blocks, [(offset ^ two, other) for offset, other in held_blocks]]
        start = 0
        found = {}
        for layer, kind in wanted:
            count = half_rows(kind)
            plan = tuple((at // 2, tuple(blocks[at]), start, count) for at in range(4))
            found[layer, kind] = (own_rows[layer][kind], tuple(buffers), plan, ranks)
            start += count
        return found

    weights = gather_weights([(0, "mixer")])
    gains = jnp.stack([gain_mixer, gain_mlp], axis=1).reshape(2 * layers, chan_width)
    gains_coarse = lax.reduce_precision(gains, 8, 7)
    extra = jnp.concatenate([gains_coarse, gains - gains_coarse]).astype(BF16).T
    extra = jnp.pad(extra, ((0, 0), (0, 128 - extra.shape[1])))
    arrived = to_tokens(input_long, input_short, extra)
    gains = arrived[:, tokens:].astype(F32)
    gains = gains[:, : 2 * layers] + gains[:, 2 * layers : 4 * layers]
    gains = [[gains[:, 2 * layer + which][:, None] for which in range(2)] for layer in range(layers)]
    for layer in range(layers):
        wanted = [(layer, "mlp")] + ([(layer + 1, "mixer")] if layer + 1 < layers else [])
        weights.update(gather_weights(wanted))
    upstream = to_tokens(grad_long, grad_short).astype(F32)

    own_lengths = jnp.concatenate([length_long, length_short])
    other_lengths = swap(own_lengths, mate)
    low, high = (
        jnp.where(first, own_lengths, other_lengths),
        jnp.where(first, other_lengths, own_lengths),
    )
    spans = [pick(jnp.concatenate([low[:count_long], high[:count_long]]), place)]
    spans += [pick(side[count_long:], place) for side in (low, high)]
    live = jnp.concatenate(
        [
            jnp.arange(length) < span
            for length, span in zip((seq_long, seq_short, seq_short), spans)
        ]
    )
    live = jnp.broadcast_to(live.astype(F32)[None], (8, live.shape[0]))
    tables = (table(seq_long), table(seq_short))
    sizes = (seq_long, seq_short, chans, 2)

    residual_start = arrived[:, :tokens].astype(F32)
    residual = residual_start
    stored_all = []
    for layer in range(layers):
        normed, norm_stored = norm_forward(residual, gains[layer][0])
        normed = both_ordered(normed)
        proj, long_out, kept, sent = mixer_forward(
            spot, weights[layer, "mixer"], normed, live, tables, sizes
        )
        middle = residual + own_sum(sent, kept)
        normed_mlp, mlp_stored = norm_forward(middle, gains[layer][1])
        normed_mlp = both_cores(normed_mlp)
        gate_up, kept, sent = mlp_forward(spot, weights[layer, "mlp"], normed_mlp)
        residual = middle + own_sum(sent, kept)
        stored_all.append((normed, norm_stored, proj, long_out, normed_mlp, mlp_stored, gate_up))

    gone_long, gone_short = from_tokens((residual - residual_start).astype(BF16))
    output_long = input_long + gone_long.astype(F32)
    output_short = input_short + gone_short.astype(F32)

    orders = []
    for one, two in plane_orders:
        orders.append(
            tuple(
                (a * one + c * two, (b * NEAR) ^ (d * FAR))
                for a in range(2) for b in range(2) for c in range(2) for d in range(2)
            )
        )
    orders = tuple(orders)

    def scatter_grads(blocks):
        done = []
        for half in range(2):
            kept, sent = blocks[2 * half : 2 * half + 2]
            one, two = plane_orders[half]
            steps = [plane[one], ("chan", NEAR), plane[two], ("chan", FAR)]
            for at, step in enumerate(steps):
                came = swap(sent, step)
                middle = kept.shape[0] // 2
                if at + 1 < len(steps):
                    sent = (kept[middle:].astype(F32) + came[middle:].astype(F32)).astype(BF16)
                    kept = (kept[:middle].astype(F32) + came[:middle].astype(F32)).astype(BF16)
                else:
                    kept = (kept.astype(F32) + came.astype(F32)).astype(BF16)
            for step in extra_steps:
                kept = (kept.astype(F32) + swap(kept, step).astype(F32)).astype(BF16)
            done.append(kept)
        return done

    upstream_start = upstream
    reduced = []
    gain_grads = {}
    mlp_half, mixer_half = (half_rows("mlp"), half_rows("mixer"))
    blocks = mlp_half
    for layer in reversed(range(layers)):
        normed, norm_stored, proj, long_out, normed_mlp, mlp_stored, gate_up = stored_all[layer]
        coming = both_cores(upstream.astype(BF16))
        kept, sent, blocks = mlp_back(
            spot, weights[layer, "mlp"], normed_mlp, gate_up, coming, orders, 0, blocks
        )
        reduced.append(scatter_grads(blocks))
        change, gain_grads[layer, 1] = norm_back(own_sum(sent, kept), mlp_stored)
        upstream = upstream + change
        coming = both_ordered(upstream.astype(BF16))
        last = layer == 0
        kept, sent, blocks = mixer_back(
            spot, weights[layer, "mixer"], normed, coming, proj, long_out, live, tables, sizes,
            orders, 0 if last else mlp_half, mixer_half if last else mlp_half + mixer_half,
        )
        if last:
            reduced.append(scatter_grads(blocks))
        change, gain_grads[layer, 0] = norm_back(own_sum(sent, kept), norm_stored)
        upstream = upstream + change

    gain_parts = jnp.stack(
        [gain_grads[layer, which] for layer in range(layers) for which in range(2)], axis=1
    )
    gain_coarse = lax.reduce_precision(gain_parts, 8, 7)
    gain_lanes = jnp.concatenate([gain_coarse, gain_parts - gain_coarse], axis=1).astype(BF16)
    gain_lanes = jnp.pad(gain_lanes, ((0, 0), (0, 128 - gain_lanes.shape[1])))
    gone_long, gone_short, gain_sums = from_tokens(
        jnp.concatenate([(upstream - upstream_start).astype(BF16), gain_lanes], axis=1)
    )
    back_long = grad_long + gone_long.astype(F32)
    back_short = grad_short + gone_short.astype(F32)
    gain_sums = jnp.sum(gain_sums[:, :, : 4 * layers].astype(F32), axis=0)
    gain_sums = (gain_sums[:, : 2 * layers] + gain_sums[:, 2 * layers :]).T
    for step in [mate] + list(plane.values()) + extra_steps:
        gain_sums = gain_sums + swap(gain_sums, step)

    pair_orders = tuple((0, one, two, one ^ two) for one, two in plane_orders)

    def gather_grads(sums):
        halves = []
        for half in range(2):
            one, two = plane_orders[half]
            block = sums[half]
            block = jnp.concatenate([block, swap(block, plane[one])])
            halves.append(jnp.concatenate([block, swap(block, plane[two])]))
        return halves + [swap(block, mate) for block in halves]

    mlp_out, mixer_out = (None, None)
    for index, sums in enumerate(reduced):
        sources = gather_grads(sums)
        layer = layers - 1 - index
        if layer >= 0:
            mlp_out = final_mlp(
                spot, sources, pair_orders, 0, mlp_count, layer, layers, mlp_out
            )
        if index > 0:
            start = mlp_half if layer >= 0 else 0
            mixer_out = final_mixer(
                spot, sources, pair_orders, start, mixer_count, chans, layer + 1, layers, mixer_out
            )
    into_out, out_out, filter_out = mixer_out
    taps = jnp.swapaxes(filter_out[:, :, seq_long : seq_long + 12], 1, 2)

    return (
        output_long,
        output_short,
        back_long,
        back_short,
        gain_sums[0::2],
        jnp.transpose(into_out, (0, 3, 1, 2)),
        taps[:, :9].reshape(layers, 3, 3, chan_width),
        taps[:, 9:],
        jnp.swapaxes(filter_out[:, :, :seq_long], 1, 2),
        out_out,
        gain_sums[1::2],
        mlp_out[0],
        mlp_out[1],
    )


def solution(mesh):
    tokens = P("batch", None, "chan")
    placed = (
        tokens,
        tokens,
        P("batch"),
        P("batch"),
        P(None, "chan"),
        P(None, None, None, "chan"),
        P(None, None, None, "chan"),
        P(None, None, "chan"),
        P(None, None, "chan"),
        P(None, "chan", None),
        P(None, "chan"),
        P(None, None, None, "chan"),
        P(None, "chan", None),
        tokens,
        tokens,
    )
    return jax.shard_map(
        on_device,
        mesh=mesh,
        in_specs=placed,
        out_specs=(tokens,) * 4 + placed[4:13],
        check_vma=False,
    )
```

time: 921 us -> 733 us (0.80)
  the two profiles are of different devices: /device:TPU:9 before, /device:TPU:11 now
where the time goes in v2:
time: 733 us; the launch traced here: 723 us
  waiting for transfers between devices  344 us (47%)
  Pallas kernels  170 us (23%)
  starting transfers between devices  95.8 us (13%)
  other arithmetic  69.9 us (10%)
  local copies, waits for them, and re-layouts  40.9 us (6%)
    ppermute x96, waiting for transfers between devices, swap(): lax.ppermute(values, axis, [(i, i ^ mask) for i in range(lax.axis_size(ax...  344 us
    ppermute x96, starting transfers between devices, swap(): lax.ppermute(values, axis, [(i, i ^ mask) for i in range(lax.axis_size(ax...  95.8 us
    pallas_call x2, Pallas kernels, mlp_back(): pl.pallas_call(functools.partial(mlp_back_kernel, plan, orders, start, al...  43.8 us
    pallas_call x2, Pallas kernels, mixer_back(): pl.pallas_call(functools.partial(mixer_back_kernel, plan, orders, start,...  41.7 us
    pallas_call x2, Pallas kernels, mixer_forward(): pl.pallas_call(functools.partial(mixer_forward_kernel, plan, sizes), grid...  35.6 us
    pallas_call x2, Pallas kernels, mlp_forward(): pl.pallas_call(functools.partial(mlp_forward_kernel, plan), grid=(ranks,)...  24.8 us
    pallas_call x2, Pallas kernels, final_mlp(): pl.pallas_call(functools.partial(final_mlp_kernel, plan, start, aliased),...  15.7 us
    convert_element_type x12, other arithmetic, scatter_grads(): kept = (kept[:middle].astype(F32) + came[:middle].astype(F32)).astype(BF16)  15.6 us
  transfers between devices with their start and end apart: 96, of which 38 were waited for; matrix products, arithmetic and copies ran while one was open for 13% of the time, Pallas kernels for 17%

profile of v2, /device:TPU:11, one launch (start us, length us, event | category | flops | bytes accessed | tf_op | source)
XLA Modules:
  0.0 723.1 jit_solution(857003079696780714)
XLA Ops:
  39.2 27.8 %collective-permute-done.3 = bf16[192,512]{1,0:T(8,128)(2,1)S(1)} collective-permute-done((bf16[192,512]{1,0:T(8,128)(2,1)S(1)}, bf16[192,512]{1,0:T(8,128)(2,1)S(1)}, u32[]{:S(2)}, u32[]{:S(2)}) %collective-permute-start.3) | collective-permute-done | bytes 196640 | tf_op jit(solution)/shard_map/ppermute | solution.py:42
  84.0 17.5 %collective-permute-done.15 = bf16[2,416,768]{2,1,0:T(8,128)(2,1)S(1)} collective-permute-done((bf16[2,416,768]{2,1,0:T(8,128)(2,1)S(1)}, bf16[2,416,768]{2,1,0:T(8,128)(2,1)S(1)}, u32[]{:S(2)}, u32[]{:S(2)}) %collective-permute-start.15) | collective-permute-done | bytes 1277984 | tf_op jit(solution)/shard_map/ppermute | solution.py:42
  106.8 12.8 %mixer_forward.2 = (bf16[2,576,768]{2,1,0:T(8,128)(2,1)}, bf16[2,192,768]{2,1,0:T(8,128)(2,1)S(1)}, f32[768,384]{1,0:T(8,128)}, bf16[768,384]{1,0:T(8,128)(2,1)S(1)}) custom-call(s32[2]{0:T(128)S(1)} %pad_add_fusion.refs_0_, f32[8,768]{1,0:T(8,128)S(1)} %broadcast_in_dim.11.refs_1_, bf16[512,1024]{1,0:T(8,128)(2,1)} %constant.214.refs_2_, ...), custom_call_target="tpu_custom_call" | custom-call | flops 3422552064 | bytes 3145728 | tf_op jit(solution)/shard_map/mixer_forward/pallas_call | solution.py:541
  134.4 32.9 %collective-permute-done.17.refs_4_.refs_7_.refs_10_.refs_6_ = bf16[6,208,768]{2,1,0:T(8,128)(2,1)S(1)} collective-permute-done((bf16[6,208,768]{2,1,0:T(8,128)(2,1)S(1)}, bf16[6,208,768]{2,1,0:T(8,128)(2,1)S(1)}, u32[]{:S(2)}, u32[]{:S(2)}) %collective-permute-start.17) | collective-permute-done | bytes 1916960 | tf_op jit(solution)/shard_map/ppermute | solution.py:42
  169.2 12.4 %mlp_forward.2 = (bf16[4,768,768]{2,1,0:T(8,128)(2,1)}, f32[768,384]{1,0:T(8,128)S(1)}, bf16[768,384]{1,0:T(8,128)(2,1)S(1)}) custom-call(s32[2]{0:T(128)S(1)} %pad_add_fusion.refs_0_, bf16[768,768]{1,0:T(8,128)(2,1)} %pad_maximum_fusion.10.refs_1_, bf16[1152,768]{1,0:T(8,128)(2,1)} %pad_maximum_fusion.refs_2_.refs_4_, bf16[6,208,768]{2,1,0:T(8,128)(2,1)} %copy-done.15, ...), custom_call_target="tpu_custom_call" | custom-call | flops 5435817984 | bytes 11796480 | tf_op jit(solution)/shard_map/mlp_forward/pallas_call | solution.py:178
  194.0 16.9 %collective-permute-done.25 = bf16[2,288,768]{2,1,0:T(8,128)(2,1)S(1)} collective-permute-done((bf16[2,288,768]{2,1,0:T(8,128)(2,1)S(1)}, bf16[2,288,768]{2,1,0:T(8,128)(2,1)S(1)}, u32[]{:S(2)}, u32[]{:S(2)}) %collective-permute-start.25) | collective-permute-done | bytes 884768 | tf_op jit(solution)/shard_map/ppermute | solution.py:42
  214.5 22.8 %mixer_forward.3 = (bf16[2,576,768]{2,1,0:T(8,128)(2,1)}, bf16[2,192,768]{2,1,0:T(8,128)(2,1)S(1)}, f32[768,384]{1,0:T(8,128)}, bf16[768,384]{1,0:T(8,128)(2,1)S(1)}) custom-call(s32[2]{0:T(128)S(1)} %pad_add_fusion.refs_0_, f32[8,768]{1,0:T(8,128)S(1)} %broadcast_in_dim.11.refs_1_, bf16[512,1024]{1,0:T(8,128)(2,1)} %constant.214.refs_2_, ...), custom_call_target="tpu_custom_call" | custom-call | flops 3422552064 | bytes 3145728 | tf_op jit(solution)/shard_map/mixer_forward/pallas_call | solution.py:541
  250.8 22.2 %collective-permute-done.27.refs_4_.refs_6_ = bf16[6,144,768]{2,1,0:T(8,128)(2,1)S(1)} collective-permute-done((bf16[6,144,768]{2,1,0:T(8,128)(2,1)S(1)}, bf16[6,144,768]{2,1,0:T(8,128)(2,1)S(1)}, u32[]{:S(2)}, u32[]{:S(2)}) %collective-permute-start.27) | collective-permute-done | bytes 1327136 | tf_op jit(solution)/shard_map/ppermute | solution.py:42
  275.0 12.4 %mlp_forward.3 = (bf16[4,768,768]{2,1,0:T(8,128)(2,1)}, f32[768,384]{1,0:T(8,128)S(1)}, bf16[768,384]{1,0:T(8,128)(2,1)S(1)}) custom-call(s32[2]{0:T(128)S(1)} %pad_add_fusion.refs_0_, bf16[768,768]{1,0:T(8,128)(2,1)} %pad_maximum_fusion.12.refs_1_, bf16[1152,768]{1,0:T(8,128)(2,1)} %pad_maximum_fusion.1.refs_2_.refs_4_, bf16[6,144,768]{2,1,0:T(8,128)(2,1)} %copy-done.25, ...), custom_call_target="tpu_custom_call" | custom-call | flops 5435817984 | bytes 11796480 | tf_op jit(solution)/shard_map/mlp_forward/pallas_call | solution.py:178
  287.4 21.8 %mlp_back.2 = (f32[768,384]{1,0:T(8,128)S(1)}, bf16[768,384]{1,0:T(8,128)(2,1)S(1)}, bf16[8,144,768]{2,1,0:T(8,128)(2,1)}, bf16[8,144,768]{2,1,0:T(8,128)(2,1)},...) custom-call(s32[2]{0:T(128)S(1)} %pad_add_fusion.refs_0_, bf16[768,768]{1,0:T(8,128)(2,1)} %pad_maximum_fusion.12.refs_1_, ...), custom_call_target="tpu_custom_call" | custom-call | flops 10871635968 | bytes 18874368 | tf_op jit(solution)/shard_map/mlp_back/pallas_call | solution.py:287
  321.4 21.0 %mixer_back.2 = (f32[768,384]{1,0:T(8,128)}, bf16[768,384]{1,0:T(8,128)(2,1)S(1)}, bf16[8,208,768]{2,1,0:T(8,128)(2,1)}, bf16[8,208,768]{2,1,0:T(8,128)(2,1)}, b...) custom-call(s32[2]{0:T(128)S(1)} %pad_add_fusion.refs_0_, f32[8,768]{1,0:T(8,128)S(1)} %broadcast_in_dim.11.refs_1_, ...), custom_call_target="tpu_custom_call" | custom-call | flops 6845104128 | bytes 6291456 | tf_op jit(solution)/shard_map/mixer_back/pallas_call | solution.py:663
  346.8 8.2 %collective-permute-done.82 = bf16[8,144,768]{2,1,0:T(8,128)(2,1)} collective-permute-done((bf16[8,144,768]{2,1,0:T(8,128)(2,1)}, bf16[8,144,768]{2,1,0:T(8,128)(2,1)}, u32[]{:S(2)}, u32[]{:S(2)}) %collective-permute-start.82) | collective-permute-done | bytes 1769504 | tf_op jit(solution)/shard_map/ppermute | solution.py:42
  364.1 22.0 %mlp_back.3 = (f32[768,384]{1,0:T(8,128)S(1)}, bf16[768,384]{1,0:T(8,128)(2,1)S(1)}, bf16[8,208,768]{2,1,0:T(8,128)(2,1)}, bf16[8,208,768]{2,1,0:T(8,128)(2,1)},...) custom-call(s32[2]{0:T(128)S(1)} %pad_add_fusion.refs_0_, ...), custom_call_target="tpu_custom_call", output_to_operand_aliasing={{2}: (9, {}), {3}: (10, {}), {4}: (11, {}), {5}: (12, {})} | custom-call | flops 10871635968 | bytes 18874368 | tf_op jit(solution)/shard_map/mlp_back/pallas_call | solution.py:287
  389.3 9.1 %collective-permute-done.89 = bf16[4,144,768]{2,1,0:T(8,128)(2,1)} collective-permute-done((bf16[4,144,768]{2,1,0:T(8,128)(2,1)}, bf16[4,144,768]{2,1,0:T(8,128)(2,1)}, u32[]{:S(2)}, u32[]{:S(2)}) %collective-permute-start.89) | collective-permute-done | bytes 884768 | tf_op jit(solution)/shard_map/ppermute | solution.py:42
  401.5 52.8 %collective-permute-done.84 = bf16[2,144,768]{2,1,0:T(8,128)(2,1)S(1)} collective-permute-done((bf16[2,144,768]{2,1,0:T(8,128)(2,1)S(1)}, bf16[2,144,768]{2,1,0:T(8,128)(2,1)S(1)}, u32[]{:S(2)}, u32[]{:S(2)}) %collective-permute-start.84) | collective-permute-done | bytes 442400 | tf_op jit(solution)/shard_map/ppermute | solution.py:42
  456.8 7.6 %collective-permute-done.85 = bf16[1,144,768]{2,1,0:T(8,128)(2,1)S(1)} collective-permute-done((bf16[1,144,768]{2,1,0:T(8,128)(2,1)S(1)}, bf16[1,144,768]{2,1,0:T(8,128)(2,1)S(1)}, u32[]{:S(2)}, u32[]{:S(2)}) %collective-permute-start.85) | collective-permute-done | bytes 221216 | tf_op jit(solution)/shard_map/ppermute | solution.py:42
  477.3 20.8 %mixer_back.3 = (f32[768,384]{1,0:T(8,128)}, bf16[768,384]{1,0:T(8,128)(2,1)S(1)}, bf16[8,64,768]{2,1,0:T(8,128)(2,1)}, bf16[8,64,768]{2,1,0:T(8,128)(2,1)}, bf1...) custom-call(s32[2]{0:T(128)S(1)} %pad_add_fusion.refs_0_, f32[8,768]{1,0:T(8,128)S(1)} %broadcast_in_dim.11.refs_1_, ...), custom_call_target="tpu_custom_call" | custom-call | flops 6845104128 | bytes 6291456 | tf_op jit(solution)/shard_map/mixer_back/pallas_call | solution.py:663
  517.3 10.5 %collective-permute-done.49 = bf16[192,512]{1,0:T(8,128)(2,1)S(1)} collective-permute-done((bf16[192,512]{1,0:T(8,128)(2,1)S(1)}, bf16[192,512]{1,0:T(8,128)(2,1)S(1)}, u32[]{:S(2)}, u32[]{:S(2)}) %collective-permute-start.49) | collective-permute-done | bytes 196640 | tf_op jit(solution)/shard_map/ppermute | solution.py:42
  542.7 20.3 %collective-permute-done.69 = bf16[4,208,768]{2,1,0:T(8,128)(2,1)S(1)} collective-permute-done((bf16[4,208,768]{2,1,0:T(8,128)(2,1)S(1)}, bf16[4,208,768]{2,1,0:T(8,128)(2,1)S(1)}, u32[]{:S(2)}, u32[]{:S(2)}) %collective-permute-start.69) | collective-permute-done | bytes 1277984 | tf_op jit(solution)/shard_map/ppermute | solution.py:42
  565.5 24.9 %collective-permute-done.75 = bf16[4,208,768]{2,1,0:T(8,128)(2,1)S(1)} collective-permute-done((bf16[4,208,768]{2,1,0:T(8,128)(2,1)S(1)}, bf16[4,208,768]{2,1,0:T(8,128)(2,1)S(1)}, u32[]{:S(2)}, u32[]{:S(2)}) %collective-permute-start.75) | collective-permute-done | bytes 1277984 | tf_op jit(solution)/shard_map/ppermute | solution.py:42
  612.4 20.5 %collective-permute-done.77 = bf16[1,208,768]{2,1,0:T(8,128)(2,1)S(1)} collective-permute-done((bf16[1,208,768]{2,1,0:T(8,128)(2,1)S(1)}, bf16[1,208,768]{2,1,0:T(8,128)(2,1)S(1)}, u32[]{:S(2)}, u32[]{:S(2)}) %collective-permute-start.77) | collective-permute-done | bytes 319520 | tf_op jit(solution)/shard_map/ppermute | solution.py:42
  634.0 8.3 %collective-permute-done.72 = bf16[1,208,768]{2,1,0:T(8,128)(2,1)S(1)} collective-permute-done((bf16[1,208,768]{2,1,0:T(8,128)(2,1)S(1)}, bf16[1,208,768]{2,1,0:T(8,128)(2,1)S(1)}, u32[]{:S(2)}, u32[]{:S(2)}) %collective-permute-start.72) | collective-permute-done | bytes 319520 | tf_op jit(solution)/shard_map/ppermute | solution.py:42
  693.3 8.3 %final_mlp.2 = (f32[2,768,2,768]{3,2,1,0:T(2,128)}, f32[2,768,768]{2,1,0:T(8,128)}) custom-call(s32[2]{0:T(128)S(1)} %pad_add_fusion.refs_0_, bf16[4,144,768]{2,1,0:T(8,128)(2,1)S(1)} %pad_maximum_fusion.18.refs_1_, bf16[4,144,768]{2,1,0:T(8,128)(2,1)S(1)} %pad_maximum_fusion.19.refs_2_, bf16[4,144,768]{2,1,0:T(8,128)(2,1)} %copy-done.33, ...), custom_call_target="tpu_custom_call" | custom-call | bytes 10616832 | tf_op jit(solution)/shard_map/final_mlp/pallas_call | solution.py:753
  715.3 7.4 %final_mlp.3 = (f32[2,768,2,768]{3,2,1,0:T(2,128)}, f32[2,768,768]{2,1,0:T(8,128)}) custom-call(s32[2]{0:T(128)S(1)} %pad_add_fusion.refs_0_, bf16[4,208,768]{2,1,0:T(8,128)(2,1)S(1)} %copy-done.1, bf16[4,208,768]{2,1,0:T(8,128)(2,1)} %pad_maximum_fusion.8.refs_2_, ...), custom_call_target="tpu_custom_call", output_to_operand_aliasing={{0}: (5, {}), {1}: (6, {})} | custom-call | bytes 10616832 | tf_op jit(solution)/shard_map/final_mlp/pallas_call | solution.py:753
  (520 shorter events, 279.2 us)
Async XLA Ops:
  25.2 45.1 %collective-permute-start.14 = (bf16[1,416,768]{2,1,0:T(8,128)(2,1)}, bf16[1,416,768]{2,1,0:T(8,128)(2,1)}, u32[]{:S(2)}, u32[]{:S(2)}) collective-permute-start(bf16[1,416,768]{2,1,0:T(8,128)(2,1)} %maximum_bitcast_fusion), channel_id=1, source_target_pairs={{0,3},{1,2},{2,1},{3,0},{4,7},{5,6},{6,5},{7,4},{8,11},{9,10},{10,... | collective-permute-start | bytes 1916936 | tf_op jit(solution)/shard_map/ppermute | solution.py:42
  31.3 35.7 %collective-permute-start.3 = (bf16[192,512]{1,0:T(8,128)(2,1)S(1)}, bf16[192,512]{1,0:T(8,128)(2,1)S(1)}, u32[]{:S(2)}, u32[]{:S(2)}) collective-permute-start(bf16[192,512]{1,0:T(8,128)(2,1)S(1)} %get-tuple-element.255), channel_id=1, source_target_pairs={{0,3},{1,2},{2,1},{3,0},{4,7},{5,6},{6,5},{7,4},{8,11},{9,10},{10,... | collective-permute-start | bytes 589832 | tf_op jit(solution)/shard_map/ppermute | solution.py:42
  32.5 37.0 %collective-permute-start.2 = (bf16[192,512]{1,0:T(8,128)(2,1)S(1)}, bf16[192,512]{1,0:T(8,128)(2,1)S(1)}, u32[]{:S(2)}, u32[]{:S(2)}) collective-permute-start(bf16[192,512]{1,0:T(8,128)(2,1)S(1)} %get-tuple-element.256), channel_id=1, source_target_pairs={{0,2},{1,3},{2,0},{3,1},{4,6},{5,7},{6,4},{7,5},{8,10},{9,11},{10,... | collective-permute-start | bytes 589832 | tf_op jit(solution)/shard_map/ppermute | solution.py:42
  37.5 38.0 %collective-permute-start.7 = (bf16[2,128,768]{2,1,0:T(8,128)(2,1)S(1)}, bf16[2,128,768]{2,1,0:T(8,128)(2,1)S(1)}, u32[]{:S(2)}, u32[]{:S(2)}) collective-permute-start(bf16[2,128,768]{2,1,0:T(8,128)(2,1)S(1)} %pad_maximum_fusion.35), channel_id=1, source_target_pairs={{0,1},{1,0},{2,3},{3,2},{4,5},{5,4},{6,7},{7,6},{8,9},{9,8},{10,11... | collective-permute-start | bytes 1179656 | tf_op jit(solution)/shard_map/ppermute | solution.py:42
  123.4 63.2 %collective-permute-start.24 = (bf16[1,288,768]{2,1,0:T(8,128)(2,1)S(1)}, bf16[1,288,768]{2,1,0:T(8,128)(2,1)S(1)}, u32[]{:S(2)}, u32[]{:S(2)}) collective-permute-start(bf16[1,288,768]{2,1,0:T(8,128)(2,1)S(1)} %maximum_bitcast_fusion.1), channel_id=1, source_target_pairs={{0,3},{1,2},{2,1},{3,0},{4,7},{5,6},{6,5},{7,4},{8,11},{9,10},{10,... | collective-permute-start | bytes 1327112 | tf_op jit(solution)/shard_map/ppermute | solution.py:42
  125.4 41.9 %collective-permute-start.17 = (bf16[6,208,768]{2,1,0:T(8,128)(2,1)S(1)}, bf16[6,208,768]{2,1,0:T(8,128)(2,1)S(1)}, u32[]{:S(2)}, u32[]{:S(2)}) collective-permute-start(bf16[6,208,768]{2,1,0:T(8,128)(2,1)S(1)} %pad_maximum_fusion.2.refs_3_.refs_6_.refs_9_.refs_5_), channel_id=1, source_target_pairs={{0,16},{4,20},{8,24},{12,28},{16,0},{20,4},{24,8},{28,12},{1,17},{... | collective-permute-start | bytes 5750792 | tf_op jit(solution)/shard_map/ppermute | solution.py:42
  127.8 41.4 %collective-permute-start.19 = (bf16[6,208,768]{2,1,0:T(8,128)(2,1)S(1)}, bf16[6,208,768]{2,1,0:T(8,128)(2,1)}, u32[]{:S(2)}, u32[]{:S(2)}) collective-permute-start(bf16[6,208,768]{2,1,0:T(8,128)(2,1)S(1)} %pad_maximum_fusion.3.refs_5_.refs_8_.refs_11_.refs_7_), channel_id=1, source_target_pairs={{0,8},{4,12},{8,0},{12,4},{16,24},{20,28},{24,16},{28,20},{1,9},{5... | collective-permute-start | bytes 5750792 | tf_op jit(solution)/shard_map/ppermute | solution.py:42
  191.3 46.0 %collective-permute-start.36 = (bf16[192,384]{1,0:T(8,128)(2,1)}, bf16[192,384]{1,0:T(8,128)(2,1)}, u32[]{:S(2)}, u32[]{:S(2)}) collective-permute-start(bf16[192,384]{1,0:T(8,128)(2,1)} %get-tuple-element.263), channel_id=1, source_target_pairs={{0,1},{1,0},{2,3},{3,2},{4,5},{5,4},{6,7},{7,6},{8,9},{9,8},{10,11... | collective-permute-start | bytes 442376 | tf_op jit(solution)/shard_map/ppermute | solution.py:42
  191.3 48.7 %collective-permute-start.37 = (bf16[192,384]{1,0:T(8,128)(2,1)}, bf16[192,384]{1,0:T(8,128)(2,1)}, u32[]{:S(2)}, u32[]{:S(2)}) collective-permute-start(bf16[192,384]{1,0:T(8,128)(2,1)} %get-tuple-element.264), channel_id=1, source_target_pairs={{0,2},{1,3},{2,0},{3,1},{4,6},{5,7},{6,4},{7,5},{8,10},{9,11},{10,... | collective-permute-start | bytes 442376 | tf_op jit(solution)/shard_map/ppermute | solution.py:42
  193.4 46.5 %collective-permute-start.38 = (bf16[192,384]{1,0:T(8,128)(2,1)S(1)}, bf16[192,384]{1,0:T(8,128)(2,1)}, u32[]{:S(2)}, u32[]{:S(2)}) collective-permute-start(bf16[192,384]{1,0:T(8,128)(2,1)S(1)} %get-tuple-element.265), channel_id=1, source_target_pairs={{0,3},{1,2},{2,1},{3,0},{4,7},{5,6},{6,5},{7,4},{8,11},{9,10},{10,... | collective-permute-start | bytes 442376 | tf_op jit(solution)/shard_map/ppermute | solution.py:42
  314.6 40.4 %collective-permute-start.82 = (bf16[8,144,768]{2,1,0:T(8,128)(2,1)}, bf16[8,144,768]{2,1,0:T(8,128)(2,1)}, u32[]{:S(2)}, u32[]{:S(2)}) collective-permute-start(bf16[8,144,768]{2,1,0:T(8,128)(2,1)} %get-tuple-element.102), channel_id=1, source_target_pairs={{0,8},{4,12},{8,0},{12,4},{16,24},{20,28},{24,16},{28,20},{1,9},{5... | collective-permute-start | bytes 5308424 | tf_op jit(solution)/shard_map/ppermute | solution.py:42
  314.9 45.3 %collective-permute-start.88 = (bf16[8,144,768]{2,1,0:T(8,128)(2,1)}, bf16[8,144,768]{2,1,0:T(8,128)(2,1)}, u32[]{:S(2)}, u32[]{:S(2)}) collective-permute-start(bf16[8,144,768]{2,1,0:T(8,128)(2,1)} %get-tuple-element.104), channel_id=1, source_target_pairs={{0,16},{4,20},{8,24},{12,28},{16,0},{20,4},{24,8},{28,12},{1,17},{... | collective-permute-start | bytes 5308424 | tf_op jit(solution)/shard_map/ppermute | solution.py:42
  388.0 111.6 %collective-permute-start.34 = (bf16[2,192,256]{2,1,0:T(8,128)(2,1)}, bf16[2,192,256]{2,1,0:T(8,128)(2,1)}, u32[]{:S(2)}, u32[]{:S(2)}) collective-permute-start(bf16[2,192,256]{2,1,0:T(8,128)(2,1)} %get-tuple-element.285), channel_id=1, source_target_pairs={{0,4},{4,0},{8,12},{12,8},{16,20},{20,16},{24,28},{28,24},{1,5},{5... | collective-permute-start | bytes 589832 | tf_op jit(solution)/shard_map/ppermute | solution.py:42
  388.1 125.4 %collective-permute-start.68 = (bf16[8,208,768]{2,1,0:T(8,128)(2,1)}, bf16[8,208,768]{2,1,0:T(8,128)(2,1)}, u32[]{:S(2)}, u32[]{:S(2)}) collective-permute-start(bf16[8,208,768]{2,1,0:T(8,128)(2,1)} %get-tuple-element.92), channel_id=1, source_target_pairs={{0,8},{4,12},{8,0},{12,4},{16,24},{20,28},{24,16},{28,20},{1,9},{5... | collective-permute-start | bytes 7667720 | tf_op jit(solution)/shard_map/ppermute | solution.py:42
  388.3 139.5 %collective-permute-start.74 = (bf16[8,208,768]{2,1,0:T(8,128)(2,1)}, bf16[8,208,768]{2,1,0:T(8,128)(2,1)}, u32[]{:S(2)}, u32[]{:S(2)}) collective-permute-start(bf16[8,208,768]{2,1,0:T(8,128)(2,1)} %get-tuple-element.94), channel_id=1, source_target_pairs={{0,16},{4,20},{8,24},{12,28},{16,0},{20,4},{24,8},{28,12},{1,17},{... | collective-permute-start | bytes 7667720 | tf_op jit(solution)/shard_map/ppermute | solution.py:42
  398.4 55.8 %collective-permute-start.84 = (bf16[2,144,768]{2,1,0:T(8,128)(2,1)S(1)}, bf16[2,144,768]{2,1,0:T(8,128)(2,1)S(1)}, u32[]{:S(2)}, u32[]{:S(2)}) collective-permute-start(bf16[2,144,768]{2,1,0:T(8,128)(2,1)S(1)} %get-tuple-element.212), channel_id=1, source_target_pairs={{0,16},{4,20},{8,24},{12,28},{16,0},{20,4},{24,8},{28,12},{1,17},{... | collective-permute-start | bytes 1327112 | tf_op jit(solution)/shard_map/ppermute | solution.py:42
  400.6 66.5 %collective-permute-start.90 = (bf16[2,144,768]{2,1,0:T(8,128)(2,1)S(1)}, bf16[2,144,768]{2,1,0:T(8,128)(2,1)S(1)}, u32[]{:S(2)}, u32[]{:S(2)}) collective-permute-start(bf16[2,144,768]{2,1,0:T(8,128)(2,1)S(1)} %get-tuple-element.210), channel_id=1, source_target_pairs={{0,8},{4,12},{8,0},{12,4},{16,24},{20,28},{24,16},{28,20},{1,9},{5... | collective-permute-start | bytes 1327112 | tf_op jit(solution)/shard_map/ppermute | solution.py:42
  531.6 133.3 %collective-permute-start.93 = (bf16[2,144,768]{2,1,0:T(8,128)(2,1)S(1)}, bf16[2,144,768]{2,1,0:T(8,128)(2,1)S(1)}, u32[]{:S(2)}, u32[]{:S(2)}) collective-permute-start(bf16[2,144,768]{2,1,0:T(8,128)(2,1)S(1)} %copy-done.39), channel_id=1, source_target_pairs={{0,8},{4,12},{8,0},{12,4},{16,24},{20,28},{24,16},{28,20},{1,9},{5... | collective-permute-start | bytes 1327112 | tf_op jit(solution)/shard_map/ppermute | solution.py:42
  535.6 54.8 %collective-permute-start.75 = (bf16[4,208,768]{2,1,0:T(8,128)(2,1)S(1)}, bf16[4,208,768]{2,1,0:T(8,128)(2,1)S(1)}, u32[]{:S(2)}, u32[]{:S(2)}) collective-permute-start(bf16[4,208,768]{2,1,0:T(8,128)(2,1)S(1)} %get-tuple-element.192), channel_id=1, source_target_pairs={{0,1},{1,0},{2,3},{3,2},{4,5},{5,4},{6,7},{7,6},{8,9},{9,8},{10,11... | collective-permute-start | bytes 3833864 | tf_op jit(solution)/shard_map/ppermute | solution.py:42
  538.1 147.2 %collective-permute-start.94 = (bf16[4,144,768]{2,1,0:T(8,128)(2,1)S(1)}, bf16[4,144,768]{2,1,0:T(8,128)(2,1)S(1)}, u32[]{:S(2)}, u32[]{:S(2)}) collective-permute-start(bf16[4,144,768]{2,1,0:T(8,128)(2,1)S(1)} %pad_maximum_fusion.18.refs_1_), channel_id=1, source_target_pairs={{0,4},{4,0},{8,12},{12,8},{16,20},{20,16},{24,28},{28,24},{1,5},{5... | collective-permute-start | bytes 2654216 | tf_op jit(solution)/shard_map/ppermute | solution.py:42
  540.5 51.0 %collective-permute-start.51 = (f32[4,192]{0,1:T(8,128)S(1)}, f32[4,192]{0,1:T(8,128)S(1)}, u32[]{:S(2)}, u32[]{:S(2)}) collective-permute-start(f32[4,192]{0,1:T(8,128)S(1)} %fusion.48), channel_id=1, source_target_pairs={{0,4},{4,0},{8,12},{12,8},{16,20},{20,16},{24,28},{28,24},{1,5},{5... | collective-permute-start | bytes 9224 | tf_op jit(solution)/shard_map/ppermute | solution.py:42
  563.0 35.8 %collective-permute-start.55 = (bf16[4,64,768]{2,1,0:T(8,128)(2,1)S(1)}, bf16[4,64,768]{2,1,0:T(8,128)(2,1)S(1)}, u32[]{:S(2)}, u32[]{:S(2)}) collective-permute-start(bf16[4,64,768]{2,1,0:T(8,128)(2,1)S(1)} %get-tuple-element.222), channel_id=1, source_target_pairs={{0,1},{1,0},{2,3},{3,2},{4,5},{5,4},{6,7},{7,6},{8,9},{9,8},{10,11... | collective-permute-start | bytes 1179656 | tf_op jit(solution)/shard_map/ppermute | solution.py:42
  656.9 44.8 %collective-permute-start.80 = (bf16[4,208,768]{2,1,0:T(8,128)(2,1)S(1)}, bf16[4,208,768]{2,1,0:T(8,128)(2,1)}, u32[]{:S(2)}, u32[]{:S(2)}) collective-permute-start(bf16[4,208,768]{2,1,0:T(8,128)(2,1)S(1)} %pad_maximum_fusion.7.refs_1_), channel_id=1, source_target_pairs={{0,4},{4,0},{8,12},{12,8},{16,20},{20,16},{24,28},{28,24},{1,5},{5... | collective-permute-start | bytes 3833864 | tf_op jit(solution)/shard_map/ppermute | solution.py:42
  664.0 37.7 %collective-permute-start.81 = (bf16[4,208,768]{2,1,0:T(8,128)(2,1)}, bf16[4,208,768]{2,1,0:T(8,128)(2,1)}, u32[]{:S(2)}, u32[]{:S(2)}) collective-permute-start(bf16[4,208,768]{2,1,0:T(8,128)(2,1)} %pad_maximum_fusion.8.refs_2_), channel_id=1, source_target_pairs={{0,4},{4,0},{8,12},{12,8},{16,20},{20,16},{24,28},{28,24},{1,5},{5... | collective-permute-start | bytes 3833864 | tf_op jit(solution)/shard_map/ppermute | solution.py:42
  (124 other events, 1468.0 us)

commit v3 on v2

--- a/solution.py
+++ b/solution.py
@@ -40,6 +40,10 @@
 def swap(values, step):
     axis, mask = step
     return lax.ppermute(values, axis, [(i, i ^ mask) for i in range(lax.axis_size(axis))])
+
+
+def after(values, *others):
+    return lax.optimization_barrier((values,) + others)[0]
 
 
 def pick(values, index):
@@ -87,22 +91,18 @@
                 copy.wait()
 
 
-def spill_copies(orders, count, start, place_ref, rows_ref, outs, sems, slot, wanted):
+def spill_copies(routes, count, place_ref, rows_ref, outs, sems, slot, wanted):
     copies = []
-    for half, blocks in enumerate(orders):
-        for at, (offset, other) in enumerate(blocks):
-            if other != wanted:
-                continue
-            middle = len(blocks) // 2
-            target = outs[2 * half + (1 if at >= middle else 0)].at[at % middle]
-            row = pl.multiple_of(((place_ref[1] ^ offset) * 2 + half) * count, 16)
-            copies.append(
-                pltpu.make_async_copy(
-                    rows_ref.at[slot, pl.ds(row, count)],
-                    target.at[pl.ds(start, count)],
-                    sems.at[slot, len(copies)],
-                )
+    for targets, half, offset, start in routes:
+        out, at = targets[wanted]
+        row = pl.multiple_of(((place_ref[1] ^ offset) * 2 + half) * count, 16)
+        copies.append(
+            pltpu.make_async_copy(
+                rows_ref.at[slot, pl.ds(row, count)],
+                outs[out].at[at, pl.ds(start, count)],
+                sems.at[slot, len(copies)],
             )
+        )
     return copies
 
 
@@ -195,16 +195,12 @@
             pltpu.SemaphoreType.DMA((ranks, 8)),
         ],
         compiler_params=PARAMS,
-        cost_estimate=pl.CostEstimate(
-            flops=6 * ranks * hidden * width * tokens,
-            bytes_accessed=2 * ranks * own.size + 4 * ranks * hidden * tokens,
-            transcendentals=ranks * hidden * tokens,
-        ),
+        cost_estimate=pl.CostEstimate(flops=1, bytes_accessed=1, transcendentals=0),
         name="mlp_forward",
     )(place, normed, own, *buffers)
 
 
-def spill(orders, count, start, place_ref, grads_ref, outs, sems, per_step):
+def spill(routes, count, place_ref, grads_ref, outs, sems, per_step):
     step = pl.program_id(0)
     ranks = per_step * pl.num_programs(0)
     for wanted in range(ranks):
@@ -214,12 +210,12 @@
         @pl.when(step == at)
         def leave():
             for copy in spill_copies(
-                orders, count, start, place_ref, grads_ref, outs, sems, slot, wanted
+                routes, count, place_ref, grads_ref, outs, sems, slot, wanted
             ):
                 copy.start()
 
 
-def spill_wait(orders, count, start, place_ref, grads_ref, outs, sems, per_step, last):
+def spill_wait(routes, count, place_ref, grads_ref, outs, sems, per_step, last):
     step = pl.program_id(0)
     steps = 4 // per_step
     for wanted in range(4):
@@ -234,14 +230,14 @@
         @pl.when(step == due)
         def gone():
             for copy in spill_copies(
-                orders, count, start, place_ref, grads_ref, outs, sems, slot, wanted
+                routes, count, place_ref, grads_ref, outs, sems, slot, wanted
             ):
                 copy.wait()
 
 
-def mlp_back_kernel(plan, orders, start, aliased, *refs):
-    (place_ref, normed_ref, coming_ref, gate_up_ref, own_ref), buffers, _, outs, scratch = grouped(
-        refs, 5, len(plan), 4 if aliased else 0, 6, 5
+def mlp_back_kernel(plan, routes, count, *refs):
+    (place_ref, normed_ref, coming_ref, gate_up_ref, own_ref), buffers, outs, scratch = grouped(
+        refs, 5, len(plan), 6, 5
     )
     kept_ref, sent_ref = outs[:2]
     flat_ref, grads_ref, total, sems, out_sems = scratch
@@ -249,8 +245,7 @@
     step = pl.program_id(0)
     width = normed_ref.shape[0]
     hidden = flat_ref.shape[1] - width
-    count = flat_ref.shape[1] // (2 * len(orders[0]) // flat_ref.shape[0])
-    spilled = (orders, count, start, place_ref, grads_ref, outs[2:], out_sems, 1)
+    spilled = (routes, count, place_ref, grads_ref, outs[2:], out_sems, 1)
     spill_wait(*spilled, False)
     slot = step % 2
     gate = gate_up_ref[0, :hidden].astype(F32)
@@ -273,25 +268,20 @@
     spill_wait(*spilled, True)
 
 
-def mlp_back(place, rows, normed, gate_up, coming, orders, start, into):
+def mlp_back(place, rows, normed, gate_up, coming, routes, blocks, block_rows):
     own, buffers, plan, ranks = rows
     count, width = own.shape
     tokens = normed.shape[1]
     hidden = count - width
     half = tokens // 2
-    aliased = not isinstance(into, int)
-    blocks = jax.ShapeDtypeStruct(
-        (len(orders[0]) // 2, into[0].shape[1] if aliased else into, width), BF16
-    )
-    first_alias = 5 + len(buffers)
     results = pl.pallas_call(
-        functools.partial(mlp_back_kernel, plan, orders, start, aliased),
+        functools.partial(mlp_back_kernel, plan, routes, plan[0][3]),
         grid=(ranks,),
         out_shape=[
             jax.ShapeDtypeStruct((width, half), F32),
             jax.ShapeDtypeStruct((width, half), BF16),
         ]
-        + [blocks] * 4,
+        + [jax.ShapeDtypeStruct((blocks, block_rows, width), BF16)] * 4,
         in_specs=[
             SMEM,
             whole((width, tokens)),
@@ -299,9 +289,8 @@
             pl.BlockSpec((1, 2 * hidden, tokens), lambda r: (r, 0, 0)),
             ANY,
         ]
-        + [ANY] * (len(buffers) + (4 if aliased else 0)),
+        + [ANY] * len(buffers),
         out_specs=[whole((width, half)), whole((width, half))] + [ANY] * 4,
-        input_output_aliases={first_alias + i: 2 + i for i in range(4)} if aliased else {},
         scratch_shapes=[
             pltpu.VMEM((ranks, count, width), BF16),
             pltpu.VMEM((2, count, width), BF16),
@@ -316,7 +305,7 @@
             transcendentals=ranks * hidden * tokens,
         ),
         name="mlp_back",
-    )(place, normed, coming, gate_up, own, *buffers, *(into if aliased else ()))
+    )(place, normed, coming, gate_up, own, *buffers)
     return (results[0], results[1], results[2:])
 
 
@@ -564,17 +553,13 @@
             pltpu.SemaphoreType.DMA((ranks, 8)),
         ],
         compiler_params=PARAMS,
-        cost_estimate=pl.CostEstimate(
-            flops=2 * ranks * chans * (4 * width * tokens + 8 * sizes[0] * sizes[0]),
-            bytes_accessed=2 * ranks * own.size,
-            transcendentals=ranks * chans * 2 * tokens,
-        ),
+        cost_estimate=pl.CostEstimate(flops=1, bytes_accessed=1, transcendentals=0),
         name="mixer_forward",
     )(place, live, *tables, normed, own, *buffers)
 
 
-def mixer_back_kernel(plan, orders, start, sizes, *refs):
-    inputs, buffers, outs, scratch = grouped(refs, 9, len(plan), 6, 6)
+def mixer_back_kernel(plan, routes, count, sizes, targets, *refs):
+    inputs, buffers, outs, scratch = grouped(refs, 9, len(plan), 2 + targets, 6)
     place_ref, live_ref, long_ref, short_ref, normed_ref, coming_ref = inputs[:6]
     proj_ref, long_out_ref, own_ref = inputs[6:]
     kept_ref, sent_ref = outs[:2]
@@ -637,8 +622,7 @@
         spare = flat_ref.shape[1] - 5 * chans
         if spare:
             grads_ref[at, 5 * chans :] = jnp.zeros((spare, flat_ref.shape[2]), BF16)
-    count = flat_ref.shape[1] // (2 * len(orders[0]) // flat_ref.shape[0])
-    spilled = (orders, count, start, place_ref, grads_ref, outs[2:], out_sems, per_step)
+    spilled = (routes, count, place_ref, grads_ref, outs[2:], out_sems, per_step)
     spill(*spilled)
     add_total(total, tn(into, grad_proj))
 
@@ -651,7 +635,10 @@
     spill_wait(*spilled, True)
 
 
-def mixer_back(place, rows, normed, coming, proj, long_out, live, tables, sizes, orders, start, into):
+def mixer_back(
+    place, rows, normed, coming, proj, long_out, live, tables, sizes, routes, blocks, block_rows
+):
+    outs = 1 + max(target[0] for route in routes for target in route[0].values())
     own, buffers, plan, ranks = rows
     count, width = own.shape
     tokens = normed.shape[1]
@@ -659,15 +646,14 @@
     chans, per_step = sizes[2:]
     steps = ranks // per_step
     group = per_step * chans
-    blocks = jax.ShapeDtypeStruct((len(orders[0]) // 2, into, width), BF16)
     results = pl.pallas_call(
-        functools.partial(mixer_back_kernel, plan, orders, start, sizes),
+        functools.partial(mixer_back_kernel, plan, routes, plan[0][3], sizes, outs),
         grid=(steps,),
         out_shape=[
             jax.ShapeDtypeStruct((width, half), F32),
             jax.ShapeDtypeStruct((width, half), BF16),
         ]
-        + [blocks] * 4,
+        + [jax.ShapeDtypeStruct((blocks, block_rows, width), BF16)] * outs,
         in_specs=[SMEM, whole(live.shape)]
         + [whole(t.shape) for t in tables]
         + [
@@ -678,7 +664,7 @@
             ANY,
         ]
         + [ANY] * len(buffers),
-        out_specs=[whole((width, half)), whole((width, half))] + [ANY] * 4,
+        out_specs=[whole((width, half)), whole((width, half))] + [ANY] * outs,
         scratch_shapes=[
             pltpu.VMEM((ranks, count, width), BF16),
             pltpu.VMEM((ranks, count, width), BF16),
@@ -688,37 +674,30 @@
             pltpu.SemaphoreType.DMA((ranks, 8)),
         ],
         compiler_params=PARAMS,
-        cost_estimate=pl.CostEstimate(
-            flops=2 * ranks * chans * (8 * width * tokens + 16 * sizes[0] * sizes[0]),
-            bytes_accessed=4 * ranks * own.size,
-            transcendentals=ranks * chans * 2 * tokens,
-        ),
+        cost_estimate=pl.CostEstimate(flops=1, bytes_accessed=1, transcendentals=0),
         name="mixer_back",
     )(place, live, *tables, normed, coming, proj, long_out, own, *buffers)
     return (results[0], results[1], results[2:])
 
 
-def final_copies(plan, start, place_ref, sources, flat_ref, sems):
-    count = flat_ref.shape[1] // (2 * len(plan[0]))
+def final_copies(place_ref, sources, flat_ref, sems):
     copies = []
-    for side in range(2):
+    for side, source in enumerate(sources):
         core = place_ref[0] if side == 0 else 1 - place_ref[0]
-        for half in range(2):
-            for at, offset in enumerate(plan[half]):
-                row = pl.multiple_of(((place_ref[1] ^ offset) * 2 + half) * count, 16)
-                copies.append(
-                    pltpu.make_async_copy(
-                        sources[2 * side + half].at[at, pl.ds(start, count)],
-                        flat_ref.at[core, pl.ds(row, count)],
-                        sems.at[len(copies)],
-                    )
+        count = source.shape[1]
+        for offset in range(source.shape[0]):
+            row = pl.multiple_of((place_ref[1] ^ offset) * count, 16)
+            copies.append(
+                pltpu.make_async_copy(
+                    source.at[offset], flat_ref.at[core, pl.ds(row, count)], sems.at[len(copies)]
                 )
+            )
     return copies
 
 
-def final_mlp_kernel(plan, start, aliased, *refs):
+def final_mlp_kernel(aliased, *refs):
     (place_ref,), sources, _, outs, (flat_ref, sems) = grouped(
-        refs, 1, 4, 2 if aliased else 0, 2, 2
+        refs, 1, 2, 2 if aliased else 0, 2, 2
     )
     up_ref, down_ref = outs
     step = pl.program_id(0)
@@ -727,7 +706,7 @@
 
     @pl.when(step == 0)
     def gather():
-        copies = final_copies(plan, start, place_ref, sources, flat_ref, sems)
+        copies = final_copies(place_ref, sources, flat_ref, sems)
         for copy in copies:
             copy.start()
         for copy in copies:
@@ -745,42 +724,40 @@
     down_ref[0] = flat_ref[step // per_core, pl.ds(at, each)].astype(F32)
 
 
-def final_mlp(place, sources, plan, start, count, layer, layers, into):
+def final_mlp(place, sources, count, layer, layers, into):
     width = sources[0].shape[2]
     hidden = count - width
     steps = 4
     aliased = into is not None
     return pl.pallas_call(
-        functools.partial(final_mlp_kernel, plan, start, aliased),
+        functools.partial(final_mlp_kernel, aliased),
         grid=(steps,),
         out_shape=[
             jax.ShapeDtypeStruct((layers, width, 2, 2 * hidden), F32),
             jax.ShapeDtypeStruct((layers, 2 * hidden, width), F32),
         ],
-        in_specs=[SMEM] + [ANY] * (6 if aliased else 4),
+        in_specs=[SMEM] + [ANY] * (4 if aliased else 2),
         out_specs=[
             pl.BlockSpec((1, width // steps, 2, 2 * hidden), lambda i: (layer, i, 0, 0)),
             pl.BlockSpec((1, 2 * hidden // steps, width), lambda i: (layer, i, 0)),
         ],
-        input_output_aliases={5: 0, 6: 1} if aliased else {},
+        input_output_aliases={3: 0, 4: 1} if aliased else {},
         scratch_shapes=[
             pltpu.VMEM((2, count, width), BF16),
-            pltpu.SemaphoreType.DMA((4 * len(plan[0]),)),
+            pltpu.SemaphoreType.DMA((2 * sources[0].shape[0],)),
         ],
         compiler_params=PARAMS,
-        cost_estimate=pl.CostEstimate(
-            flops=0, bytes_accessed=12 * count * width, transcendentals=0
-        ),
+        cost_estimate=pl.CostEstimate(flops=1, bytes_accessed=1, transcendentals=0),
         name="final_mlp",
     )(place, *sources, *(into if aliased else ()))
 
 
-def final_mixer_kernel(plan, start, chans, aliased, *refs):
+def final_mixer_kernel(chans, aliased, *refs):
     (place_ref,), sources, _, outs, (flat_ref, sems) = grouped(
-        refs, 1, 4, 3 if aliased else 0, 3, 2
+        refs, 1, 2, 3 if aliased else 0, 3, 2
     )
     into_ref, out_ref, filter_ref = outs
-    copies = final_copies(plan, start, place_ref, sources, flat_ref, sems)
+    copies = final_copies(place_ref, sources, flat_ref, sems)
     for copy in copies:
         copy.start()
     for copy in copies:
@@ -793,32 +770,30 @@
         filter_ref[0, lanes] = flat_ref[core, 4 * chans : 5 * chans].astype(F32)
 
 
-def final_mixer(place, sources, plan, start, count, chans, layer, layers, into):
+def final_mixer(place, sources, count, chans, layer, layers, into):
     width = sources[0].shape[2]
     aliased = into is not None
     return pl.pallas_call(
-        functools.partial(final_mixer_kernel, plan, start, chans, aliased),
+        functools.partial(final_mixer_kernel, chans, aliased),
         grid=(1,),
         out_shape=[
             jax.ShapeDtypeStruct((layers, 3, 2 * chans, width), F32),
             jax.ShapeDtypeStruct((layers, 2 * chans, width), F32),
             jax.ShapeDtypeStruct((layers, 2 * chans, width), F32),
         ],
-        in_specs=[SMEM] + [ANY] * (7 if aliased else 4),
+        in_specs=[SMEM] + [ANY] * (5 if aliased else 2),
         out_specs=[
             pl.BlockSpec((1, 3, 2 * chans, width), lambda i: (layer, 0, 0, 0)),
             pl.BlockSpec((1, 2 * chans, width), lambda i: (layer, 0, 0)),
             pl.BlockSpec((1, 2 * chans, width), lambda i: (layer, 0, 0)),
         ],
-        input_output_aliases={5: 0, 6: 1, 7: 2} if aliased else {},
+        input_output_aliases={3: 0, 4: 1, 5: 2} if aliased else {},
         scratch_shapes=[
             pltpu.VMEM((2, count, width), BF16),
-            pltpu.SemaphoreType.DMA((4 * len(plan[0]),)),
+            pltpu.SemaphoreType.DMA((2 * sources[0].shape[0],)),
         ],
         compiler_params=PARAMS,
-        cost_estimate=pl.CostEstimate(
-            flops=0, bytes_accessed=12 * count * width, transcendentals=0
-        ),
+        cost_estimate=pl.CostEstimate(flops=1, bytes_accessed=1, transcendentals=0),
         name="final_mixer",
     )(place, *sources, *(into if aliased else ()))
 
@@ -880,37 +855,48 @@
     while mask < 2 * pairs:
         extra_steps.append(("batch", mask))
         mask *= 2
-    spot = jnp.stack([core, piece]).astype(jnp.int32)
+    spot = jnp.stack([core, piece, place]).astype(jnp.int32)
     plane_orders = ((1, 2), (2, 1))
-
-    def exchange(blocks):
-        came = [pick(blocks, place)]
-        came += [swap(pick(blocks, place ^ r), ("chan", r)) for r in range(1, ranks)]
-        return by_xor(jnp.stack(came), place)
 
     def to_tokens(long_rows, short_rows, extra=None):
         turned = jnp.swapaxes(long_rows, 1, 2).astype(BF16)
-        halves = jnp.stack([turned[:, :, :half_long], turned[:, :, half_long:]])
+        halves = jnp.stack([turned[..., :half_long], turned[..., half_long:]])
         kept = pick(halves, core)
         came = swap(pick(halves, 1 - core), mate)
         ordered = jnp.where(first, jnp.concatenate([kept, came]), jnp.concatenate([came, kept]))
         parts = [ordered, jnp.swapaxes(short_rows, 1, 2).astype(BF16)]
         if extra is not None:
             parts.append(jnp.broadcast_to(extra[None], (ranks,) + extra.shape))
-        gathered = exchange(jnp.concatenate(parts, axis=2))
-        return gathered.reshape(width, -1)
+        yield from exchange(jnp.concatenate(parts, axis=2), lambda v: v.reshape(width, -1))
+
+    def exchange(blocks, then):
+        came = {0: pick(blocks, place)}
+        both = jnp.stack([pick(blocks, place ^ FAR), pick(blocks, place ^ NEAR ^ FAR)])
+        first_came = swap(both, ("chan", FAR))
+        first_came = after(first_came, *(yield [both]))
+        came[FAR] = first_came[0]
+        both = jnp.stack([pick(blocks, place ^ NEAR), first_came[1]])
+        second_came = swap(both, ("chan", NEAR))
+        second_came = after(second_came, *(yield [both]))
+        came[NEAR], came[NEAR ^ FAR] = (second_came[0], second_came[1])
+        result = then(by_xor(jnp.stack([came[r] for r in range(ranks)]), place))
+        yield result
 
     def from_tokens(values):
-        gathered = exchange(values.reshape(ranks, chan_width, -1))
+        steps = exchange(values.reshape(ranks, chan_width, -1), lambda gathered: gathered)
+        ties = yield next(steps)
+        ties = yield steps.send(ties)
+        gathered = steps.send(ties)
         halves = gathered[:, :, :half_long].reshape(2, count_long, chan_width, half_long)
         kept = pick(halves, core)
-        came = swap(pick(halves, 1 - core), mate)
+        sent = pick(halves, 1 - core)
+        came = swap(sent, mate)
+        came = after(came, *(yield [sent]))
         ordered = jnp.where(
             first, jnp.concatenate([kept, came], axis=2), jnp.concatenate([came, kept], axis=2)
         )
         short_part = jnp.swapaxes(gathered[:, :, half_long:tokens], 1, 2)
-        result = (jnp.swapaxes(ordered, 1, 2), short_part)
-        return result + ((gathered[:, :, tokens:],) if values.shape[1] > tokens else ())
+        yield (jnp.swapaxes(ordered, 1, 2), short_part, gathered[:, :, tokens:])
 
     def both_cores(values):
         return jnp.concatenate([values, swap(values, mate)], axis=1)
@@ -958,45 +944,58 @@
             own_rows[layer][kind], (piece * 2 + half) * count, count, 0
         )
 
-    def gather_weights(wanted):
-        parts = [own_block(layer, kind, half) for half in range(2) for layer, kind in wanted]
-        block = jnp.concatenate(parts)[None]
-        rows = block.shape[1] // 2
+    others = (FAR, NEAR, FAR ^ NEAR)
+
+    def gather(layer, kind):
+        block = jnp.concatenate([own_block(layer, kind, half) for half in range(2)])[None]
+        count = half_rows(kind)
         far = swap(block, ("chan", FAR))
-        near = swap(jnp.concatenate([block, far]), ("chan", NEAR))
-        others = (FAR, NEAR, FAR ^ NEAR)
+        far = after(far, *(yield [block]))
+        both = jnp.concatenate([block, far])
+        near = swap(both, ("chan", NEAR))
+        near = after(near, *(yield [both]))
         foreign = jnp.concatenate([far, near])
-        buffers, blocks = ([], [])
-        for half in range(2):
-            held = foreign[:, half * rows : (half + 1) * rows]
-            held_blocks = [(0, other) for other in others]
-            one, two = plane_orders[half]
-            held = jnp.concatenate([held, swap(held, plane[one])])
-            held_blocks = held_blocks + [(one, other) for other in others]
-            buffers += [held, swap(held, plane[two])]
-            blocks += [held_blocks, [(offset ^ two, other) for offset, other in held_blocks]]
-        start = 0
-        found = {}
-        for layer, kind in wanted:
-            count = half_rows(kind)
-            plan = tuple((at // 2, tuple(blocks[at]), start, count) for at in range(4))
-            found[layer, kind] = (own_rows[layer][kind], tuple(buffers), plan, ranks)
-            start += count
-        return found
-
-    weights = gather_weights([(0, "mixer")])
+        held = [foreign[:, half * count : (half + 1) * count] for half in range(2)]
+        came = [swap(held[half], plane[plane_orders[half][0]]) for half in range(2)]
+        ties = yield held
+        held = [jnp.concatenate([held[half], after(came[half], *ties)]) for half in range(2)]
+        buffers, plan = ([], [])
+        for half, (one, two) in enumerate(plane_orders):
+            blocks = [(0, other) for other in others] + [(one, other) for other in others]
+            buffers += [held[half], swap(held[half], plane[two])]
+            plan.append((half, tuple(blocks), 0, count))
+            plan.append((half, tuple((offset ^ two, other) for offset, other in blocks), 0, count))
+        weights[layer, kind] = (own_rows[layer][kind], tuple(buffers), tuple(plan), ranks)
+        yield held
+
+    line = []
+
+    def go(steps, *ties):
+        line[:] = steps.send((*line, *ties))
+
+    def begin(steps):
+        line.extend(next(steps))
+        return steps
+
+    def finish(steps):
+        return steps.send(tuple(line))
+
+    weights = {}
     gains = jnp.stack([gain_mixer, gain_mlp], axis=1).reshape(2 * layers, chan_width)
     gains_coarse = lax.reduce_precision(gains, 8, 7)
-    extra = jnp.concatenate([gains_coarse, gains - gains_coarse]).astype(BF16).T
-    extra = jnp.pad(extra, ((0, 0), (0, 128 - extra.shape[1])))
-    arrived = to_tokens(input_long, input_short, extra)
-    gains = arrived[:, tokens:].astype(F32)
-    gains = gains[:, : 2 * layers] + gains[:, 2 * layers : 4 * layers]
-    gains = [[gains[:, 2 * layer + which][:, None] for which in range(2)] for layer in range(layers)]
-    for layer in range(layers):
-        wanted = [(layer, "mlp")] + ([(layer + 1, "mixer")] if layer + 1 < layers else [])
-        weights.update(gather_weights(wanted))
-    upstream = to_tokens(grad_long, grad_short).astype(F32)
+    gains = jnp.concatenate([gains_coarse, gains - gains_coarse]).astype(BF16).T
+    gains = jnp.pad(gains, ((0, 0), (0, 128 - gains.shape[1])))
+    mixer_0 = begin(gather(0, "mixer"))
+    input_steps = begin(to_tokens(input_long, input_short, gains))
+    mlp_0 = begin(gather(0, "mlp"))
+    go(mixer_0)
+    go(input_steps)
+    go(mixer_0)
+    go(mlp_0)
+    arrived = finish(input_steps)
+    gains = arrived[:, tokens : tokens + 4 * layers].astype(F32)
+    gains = gains[:, : 2 * layers] + gains[:, 2 * layers :]
+    gains = gains.T.reshape(layers, 2, width, 1)
 
     own_lengths = jnp.concatenate([length_long, length_short])
     other_lengths = swap(own_lengths, mate)
@@ -1020,75 +1019,154 @@
     residual = residual_start
     stored_all = []
     for layer in range(layers):
-        normed, norm_stored = norm_forward(residual, gains[layer][0])
+        normed, norm_stored = norm_forward(residual, gains[layer, 0])
         normed = both_ordered(normed)
+        if layer == 0:
+            mixer_1 = begin(gather(1, "mixer"))
+            go(mixer_0)
+            go(mlp_0)
+        else:
+            go(mlp_1)
         proj, long_out, kept, sent = mixer_forward(
-            spot, weights[layer, "mixer"], normed, live, tables, sizes
+            spot, weights[layer, "mixer"], after(normed, *line), live, tables, sizes
         )
+        if layer == 0:
+            go(mixer_1, kept)
+        else:
+            grad_steps = begin(to_tokens(grad_long, grad_short))
+        sent = after(sent, *line)
         middle = residual + own_sum(sent, kept)
-        normed_mlp, mlp_stored = norm_forward(middle, gains[layer][1])
+        normed_mlp, mlp_stored = norm_forward(middle, gains[layer, 1])
         normed_mlp = both_cores(normed_mlp)
-        gate_up, kept, sent = mlp_forward(spot, weights[layer, "mlp"], normed_mlp)
+        if layer == 0:
+            go(mlp_0)
+            mlp_1 = begin(gather(1, "mlp"))
+            go(mixer_1)
+            go(mlp_1)
+            go(mixer_1)
+            go(mlp_1)
+        else:
+            go(grad_steps)
+        gate_up, kept, sent = mlp_forward(
+            spot, weights[layer, "mlp"], after(normed_mlp, *line)
+        )
         residual = middle + own_sum(sent, kept)
         stored_all.append((normed, norm_stored, proj, long_out, normed_mlp, mlp_stored, gate_up))
-
-    gone_long, gone_short = from_tokens((residual - residual_start).astype(BF16))
-    output_long = input_long + gone_long.astype(F32)
-    output_short = input_short + gone_short.astype(F32)
-
-    orders = []
-    for one, two in plane_orders:
-        orders.append(
-            tuple(
-                (a * one + c * two, (b * NEAR) ^ (d * FAR))
-                for a in range(2) for b in range(2) for c in range(2) for d in range(2)
-            )
-        )
-    orders = tuple(orders)
-
-    def scatter_grads(blocks):
-        done = []
-        for half in range(2):
-            kept, sent = blocks[2 * half : 2 * half + 2]
-            one, two = plane_orders[half]
-            steps = [plane[one], ("chan", NEAR), plane[two], ("chan", FAR)]
-            for at, step in enumerate(steps):
-                came = swap(sent, step)
-                middle = kept.shape[0] // 2
-                if at + 1 < len(steps):
-                    sent = (kept[middle:].astype(F32) + came[middle:].astype(F32)).astype(BF16)
-                    kept = (kept[:middle].astype(F32) + came[:middle].astype(F32)).astype(BF16)
-                else:
-                    kept = (kept.astype(F32) + came.astype(F32)).astype(BF16)
-            for step in extra_steps:
-                kept = (kept.astype(F32) + swap(kept, step).astype(F32)).astype(BF16)
-            done.append(kept)
-        return done
+    upstream = finish(grad_steps).astype(F32)
+
+    output_steps = from_tokens((residual - residual_start).astype(BF16))
+
+    chan_order = (0, FAR, NEAR, NEAR ^ FAR)
+
+    def routes(near_first, count):
+        found = []
+        for half, (one, two) in enumerate(plane_orders):
+            for a in range(2):
+                for c in range(2):
+                    if near_first:
+                        targets = {r: (i // 2, 4 * a + 2 * c + i % 2) for i, r in enumerate(chan_order)}
+                    else:
+                        targets = {r: (2 * half + a, ranks * c + i) for i, r in enumerate(chan_order)}
+                    found.append((targets, half, a * one + c * two, near_first * half * count))
+        return tuple(found)
+
+    def added(values):
+        return sum(value.astype(F32) for value in values).astype(BF16)
+
+    def spread_sums(block, early):
+        for step in extra_steps:
+            block = added([block, swap(block, step)])
+        parts = [(block, plane_orders[early])] if early is not None else []
+        if early is None:
+            middle = block.shape[1] // 2
+            parts = [(block[:, :middle], plane_orders[0]), (block[:, middle:], plane_orders[1])]
+        came = [swap(part, plane[one]) for part, (one, _) in parts]
+        ties = yield [part for part, _ in parts]
+        both = [jnp.concatenate([part, after(c, *ties)]) for (part, _), c in zip(parts, came)]
+        came = [swap(part, plane[two]) for part, (_, (_, two)) in zip(both, parts)]
+        ties = yield both
+        pieces_of = []
+        for part, c, (_, (one, two)) in zip(both, came, parts):
+            c = after(c, *ties)
+            by = {0: part[:1], one: part[1:], two: c[:1], one ^ two: c[1:]}
+            pieces_of.append(jnp.concatenate([by[offset] for offset in range(pieces)]))
+        mine = jnp.concatenate(pieces_of, axis=1)
+        came = swap(mine, mate)
+        ties = yield [mine]
+        yield (mine, after(came, *ties))
+
+    def scatter(blocks, early):
+        near_first = len(blocks) == 2
+        if near_first:
+            came = swap(blocks[1], ("chan", NEAR))
+            ties = yield [blocks[1]]
+            block = added([blocks[0], after(came, *ties)])
+            count = block.shape[1] // 2
+            parts = [block[:, half * count : (half + 1) * count] for half in range(2)]
+            kept = [part[:4] for part in parts]
+            sent = [part[4:] for part in parts]
+        else:
+            kept, sent = (blocks[0::2], blocks[1::2])
+        came = [swap(part, plane[one]) for part, (one, _) in zip(sent, plane_orders)]
+        ties = yield list(sent)
+        came = [after(value, *ties) for value in came]
+        middle = kept[0].shape[0] // 2
+        sent = [added([k[middle:], c[middle:]]) for k, c in zip(kept, came)]
+        kept = [added([k[:middle], c[:middle]]) for k, c in zip(kept, came)]
+        came = [swap(part, plane[two]) for part, (_, two) in zip(sent, plane_orders)]
+        ties = yield sent
+        came = [after(value, *ties) for value in came]
+        block = jnp.concatenate([added([k, c]) for k, c in zip(kept, came)], axis=1)
+        for mask in (FAR,) if near_first else (NEAR, FAR):
+            kept, sent = (block[: block.shape[0] // 2], block[block.shape[0] // 2 :])
+            came = swap(sent, ("chan", mask))
+            ties = yield [sent]
+            block = added([kept, after(came, *ties)])
+        yield from spread_sums(block, early)
 
     upstream_start = upstream
-    reduced = []
     gain_grads = {}
+    scatters = []
     mlp_half, mixer_half = (half_rows("mlp"), half_rows("mixer"))
-    blocks = mlp_half
+
+    line[:] = []
     for layer in reversed(range(layers)):
         normed, norm_stored, proj, long_out, normed_mlp, mlp_stored, gate_up = stored_all[layer]
+        last = layer == 0
         coming = both_cores(upstream.astype(BF16))
         kept, sent, blocks = mlp_back(
-            spot, weights[layer, "mlp"], normed_mlp, gate_up, coming, orders, 0, blocks
+            spot, weights[layer, "mlp"], normed_mlp, gate_up, coming,
+            routes(False, mlp_half), 2 * ranks, mlp_half,
         )
-        reduced.append(scatter_grads(blocks))
+        if last:
+            go(scatters[0], kept)
+            go(scatters[1], kept)
+        scatters.append(begin(scatter(blocks, None if last else 0)))
+        sent = after(sent, *line)
         change, gain_grads[layer, 1] = norm_back(own_sum(sent, kept), mlp_stored)
         upstream = upstream + change
         coming = both_ordered(upstream.astype(BF16))
-        last = layer == 0
+        if last:
+            go(scatters[0])
+            go(scatters[1])
+        else:
+            begin(output_steps)
         kept, sent, blocks = mixer_back(
-            spot, weights[layer, "mixer"], normed, coming, proj, long_out, live, tables, sizes,
-            orders, 0 if last else mlp_half, mixer_half if last else mlp_half + mixer_half,
+            spot, weights[layer, "mixer"], normed, after(coming, *line), proj, long_out, live,
+            tables, sizes, routes(True, mixer_half), 2 * ranks, 2 * mixer_half,
         )
         if last:
-            reduced.append(scatter_grads(blocks))
+            go(scatters[2], kept)
+        else:
+            go(scatters[0], kept)
+        scatters.append(begin(scatter(blocks, None if last else 1)))
+        sent = after(sent, *line)
         change, gain_grads[layer, 0] = norm_back(own_sum(sent, kept), norm_stored)
         upstream = upstream + change
+        if not last:
+            go(output_steps)
+
+    mlp_early, mixer_early, mlp_late, mixer_late = scatters
 
     gain_parts = jnp.stack(
         [gain_grads[layer, which] for layer in range(layers) for which in range(2)], axis=1
@@ -1096,9 +1174,38 @@
     gain_coarse = lax.reduce_precision(gain_parts, 8, 7)
     gain_lanes = jnp.concatenate([gain_coarse, gain_parts - gain_coarse], axis=1).astype(BF16)
     gain_lanes = jnp.pad(gain_lanes, ((0, 0), (0, 128 - gain_lanes.shape[1])))
-    gone_long, gone_short, gain_sums = from_tokens(
-        jnp.concatenate([(upstream - upstream_start).astype(BF16), gain_lanes], axis=1)
-    )
+    go(mlp_early)
+    go(mixer_early)
+    go(output_steps)
+    go(mlp_late)
+    go(mlp_early)
+    go(mixer_late)
+    go(mixer_early)
+    go(mlp_late)
+    changed = jnp.concatenate([(upstream - upstream_start).astype(BF16), gain_lanes], axis=1)
+    back_steps = begin(from_tokens(after(changed, *line)))
+    go(mixer_late)
+    go(mlp_early)
+    go(mixer_early)
+    go(mlp_late)
+    go(mixer_late)
+    mlp_out = final_mlp(spot, finish(mlp_early), mlp_count, 1, layers, None)
+    line.append(mlp_out[1])
+    go(mixer_early)
+    go(back_steps)
+    go(mlp_late)
+    go(mixer_late)
+    mixer_out = final_mixer(spot, finish(mixer_early), mixer_count, chans, 1, layers, None)
+    line.append(mixer_out[1])
+    go(back_steps)
+    go(mlp_late)
+    go(mixer_late)
+    go(mixer_late)
+
+    gone_long, gone_short, _ = finish(output_steps)
+    output_long = input_long + gone_long.astype(F32)
+    output_short = input_short + gone_short.astype(F32)
+    gone_long, gone_short, gain_sums = finish(back_steps)
     back_long = grad_long + gone_long.astype(F32)
     back_short = grad_short + gone_short.astype(F32)
     gain_sums = jnp.sum(gain_sums[:, :, : 4 * layers].astype(F32), axis=0)
@@ -1106,30 +1213,8 @@
     for step in [mate] + list(plane.values()) + extra_steps:
         gain_sums = gain_sums + swap(gain_sums, step)
 
-    pair_orders = tuple((0, one, two, one ^ two) for one, two in plane_orders)
-
-    def gather_grads(sums):
-        halves = []
-        for half in range(2):
-            one, two = plane_orders[half]
-            block = sums[half]
-            block = jnp.concatenate([block, swap(block, plane[one])])
-            halves.append(jnp.concatenate([block, swap(block, plane[two])]))
-        return halves + [swap(block, mate) for block in halves]
-
-    mlp_out, mixer_out = (None, None)
-    for index, sums in enumerate(reduced):
-        sources = gather_grads(sums)
-        layer = layers - 1 - index
-        if layer >= 0:
-            mlp_out = final_mlp(
-                spot, sources, pair_orders, 0, mlp_count, layer, layers, mlp_out
-            )
-        if index > 0:
-            start = mlp_half if layer >= 0 else 0
-            mixer_out = final_mixer(
-                spot, sources, pair_orders, start, mixer_count, chans, layer + 1, layers, mixer_out
-            )
+    mlp_out = final_mlp(spot, finish(mlp_late), mlp_count, 0, layers, mlp_out)
+    mixer_out = final_mixer(spot, finish(mixer_late), mixer_count, chans, 0, layers, mixer_out)
     into_out, out_out, filter_out = mixer_out
     taps = jnp.swapaxes(filter_out[:, :, seq_long : seq_long + 12], 1, 2)
 

time: 733 us -> 620 us (0.85)
  the two profiles are of different devices: /device:TPU:11 before, /device:TPU:0 now
where the time goes in v3:
time: 620 us; the launch traced here: 610 us
  waiting for transfers between devices  195 us (31%)
  Pallas kernels  158 us (25%)
  starting transfers between devices  129 us (21%)
  other arithmetic  81.4 us (13%)
  local copies, waits for them, and re-layouts  43.3 us (7%)
    ppermute x96, waiting for transfers between devices, swap(): lax.ppermute(values, axis, [(i, i ^ mask) for i in range(lax.axis_size(ax...  195 us
    ppermute x96, starting transfers between devices, swap(): lax.ppermute(values, axis, [(i, i ^ mask) for i in range(lax.axis_size(ax...  129 us
    pallas_call x2, Pallas kernels, mlp_back(): pl.pallas_call(functools.partial(mlp_back_kernel, plan, routes, plan[0][3...  44.4 us
    pallas_call x2, Pallas kernels, mixer_back(): pl.pallas_call(functools.partial(mixer_back_kernel, plan, routes, plan[0]...  41.5 us
    pallas_call x2, Pallas kernels, mixer_forward(): pl.pallas_call(functools.partial(mixer_forward_kernel, plan, sizes), grid...  25.7 us
    pallas_call x2, Pallas kernels, mlp_forward(): pl.pallas_call(functools.partial(mlp_forward_kernel, plan), grid=(ranks,)...  24.8 us
    convert_element_type x20, other arithmetic, added(): return sum((value.astype(F32) for value in values)).astype(BF16)  24.3 us
    unnamed x176, local copies, waits for them, and re-layouts  17.1 us
  transfers between devices with their start and end apart: 96, of which 32 were waited for; matrix products, arithmetic and copies ran while one was open for 18% of the time, Pallas kernels for 19%

profile of v3, /device:TPU:0, one launch (start us, length us, event | category | flops | bytes accessed | tf_op | source)
XLA Modules:
  0.0 610.4 jit_solution(404207786098868376)
XLA Ops:
  42.4 8.1 %collective-permute-done.1 = bf16[2,192,512]{2,1,0:T(8,128)(2,1)S(1)} collective-permute-done((bf16[2,192,512]{2,1,0:T(8,128)(2,1)S(1)}, bf16[2,192,512]{2,1,0:T(8,128)(2,1)S(1)}, u32[]{:S(2)}, u32[]{:S(2)}) %collective-permute-start.1) | collective-permute-done | bytes 393248 | tf_op jit(solution)/shard_map/ppermute | solution.py:42
  50.6 15.7 %collective-permute-start.3 = (bf16[2,192,512]{2,1,0:T(8,128)(2,1)S(1)}, bf16[2,192,512]{2,1,0:T(8,128)(2,1)S(1)}, u32[]{:S(2)}, u32[]{:S(2)}) collective-permute-start(bf16[2,192,512]{2,1,0:T(8,128)(2,1)S(1)} %pad_maximum_fusion.38), channel_id=1, source_target_pairs={{0,1},{1,0},{2,3},{3,2},{4,5},{5,4},{6,7},{7,6},{8,9},{9,8},{10,11... | collective-permute-start | bytes 1179656 | tf_op jit(solution)/shard_map/ppermute | solution.py:42
  84.6 9.3 %collective-permute-done.8 = bf16[2,288,768]{2,1,0:T(8,128)(2,1)} collective-permute-done((bf16[2,288,768]{2,1,0:T(8,128)(2,1)}, bf16[2,288,768]{2,1,0:T(8,128)(2,1)}, u32[]{:S(2)}, u32[]{:S(2)}) %collective-permute-start.8) | collective-permute-done | bytes 884768 | tf_op jit(solution)/shard_map/ppermute | solution.py:42
  103.5 12.7 %mixer_forward.2 = (bf16[2,576,768]{2,1,0:T(8,128)(2,1)}, bf16[2,192,768]{2,1,0:T(8,128)(2,1)S(1)}, f32[768,384]{1,0:T(8,128)}, bf16[768,384]{1,0:T(8,128)(2,1)S(1)}) custom-call(s32[3]{0:T(128)S(1)} %pad_add_fusion.refs_0_, f32[8,768]{1,0:T(8,128)S(1)} %broadcast_in_dim.15.refs_1_, bf16[512,1024]{1,0:T(8,128)(2,1)} %constant.214.refs_2_, ...), custom_call_target="tpu_custom_call" | custom-call | flops 1 | bytes 1 | tf_op jit(solution)/shard_map/mixer_forward/pallas_call | solution.py:530
  128.7 28.5 %collective-permute-done.22 = bf16[3,64,768]{2,1,0:T(8,128)(2,1)S(1)} collective-permute-done((bf16[3,64,768]{2,1,0:T(8,128)(2,1)S(1)}, bf16[3,64,768]{2,1,0:T(8,128)(2,1)S(1)}, u32[]{:S(2)}, u32[]{:S(2)}) %collective-permute-start.22) | collective-permute-done | bytes 294944 | tf_op jit(solution)/shard_map/ppermute | solution.py:42
  162.0 12.4 %mlp_forward.2 = (bf16[4,768,768]{2,1,0:T(8,128)(2,1)}, f32[768,384]{1,0:T(8,128)S(1)}, bf16[768,384]{1,0:T(8,128)(2,1)S(1)}) custom-call(s32[3]{0:T(128)S(1)} %pad_add_fusion.refs_0_, bf16[768,768]{1,0:T(8,128)(2,1)} %pad_maximum_fusion.8.refs_1_, bf16[1152,768]{1,0:T(8,128)(2,1)} %pad_maximum_fusion.refs_2_.refs_4_, bf16[6,144,768]{2,1,0:T(8,128)(2,1)} %copy-done.8, ...), custom_call_target="tpu_custom_call" | custom-call | flops 1 | bytes 1 | tf_op jit(solution)/shard_map/mlp_forward/pallas_call | solution.py:178
  197.5 12.9 %mixer_forward.3 = (bf16[2,576,768]{2,1,0:T(8,128)(2,1)}, bf16[2,192,768]{2,1,0:T(8,128)(2,1)S(1)}, f32[768,384]{1,0:T(8,128)}, bf16[768,384]{1,0:T(8,128)(2,1)S(1)}) custom-call(s32[3]{0:T(128)S(1)} %pad_add_fusion.refs_0_, f32[8,768]{1,0:T(8,128)S(1)} %broadcast_in_dim.15.refs_1_, bf16[512,1024]{1,0:T(8,128)(2,1)} %constant.214.refs_2_, ...), custom_call_target="tpu_custom_call" | custom-call | flops 1 | bytes 1 | tf_op jit(solution)/shard_map/mixer_forward/pallas_call | solution.py:530
  221.3 20.8 %collective-permute-done.35.refs_4_.refs_6_ = bf16[6,144,768]{2,1,0:T(8,128)(2,1)S(1)} collective-permute-done((bf16[6,144,768]{2,1,0:T(8,128)(2,1)S(1)}, bf16[6,144,768]{2,1,0:T(8,128)(2,1)S(1)}, u32[]{:S(2)}, u32[]{:S(2)}) %collective-permute-start.35) | collective-permute-done | bytes 1327136 | tf_op jit(solution)/shard_map/ppermute | solution.py:42
  243.4 12.4 %mlp_forward.3 = (bf16[4,768,768]{2,1,0:T(8,128)(2,1)}, f32[768,384]{1,0:T(8,128)S(1)}, bf16[768,384]{1,0:T(8,128)(2,1)S(1)}) custom-call(s32[3]{0:T(128)S(1)} %pad_add_fusion.refs_0_, bf16[768,768]{1,0:T(8,128)(2,1)} %pad_maximum_fusion.10.refs_1_, bf16[1152,768]{1,0:T(8,128)(2,1)} %pad_maximum_fusion.1.refs_2_.refs_4_, bf16[6,144,768]{2,1,0:T(8,128)(2,1)} %copy-done.11, ...), custom_call_target="tpu_custom_call" | custom-call | flops 1 | bytes 1 | tf_op jit(solution)/shard_map/mlp_forward/pallas_call | solution.py:178
  255.8 22.3 %mlp_back.2 = (f32[768,384]{1,0:T(8,128)S(1)}, bf16[768,384]{1,0:T(8,128)(2,1)S(1)}, bf16[8,144,768]{2,1,0:T(8,128)(2,1)}, bf16[8,144,768]{2,1,0:T(8,128)(2,1)},...) custom-call(s32[3]{0:T(128)S(1)} %pad_add_fusion.refs_0_, bf16[768,768]{1,0:T(8,128)(2,1)} %pad_maximum_fusion.10.refs_1_, ...), custom_call_target="tpu_custom_call" | custom-call | flops 10871635968 | bytes 18874368 | tf_op jit(solution)/shard_map/mlp_back/pallas_call | solution.py:277
  287.4 20.6 %mixer_back.2 = (f32[768,384]{1,0:T(8,128)}, bf16[768,384]{1,0:T(8,128)(2,1)S(1)}, bf16[8,128,768]{2,1,0:T(8,128)(2,1)}, bf16[8,128,768]{2,1,0:T(8,128)(2,1)}) custom-call(s32[3]{0:T(128)S(1)} %pad_add_fusion.refs_0_, f32[8,768]{1,0:T(8,128)S(1)} %broadcast_in_dim.15.refs_1_, bf16[512,1024]{1,0:T(8,128)(2,1)} %constant.214.refs_2_, ...), custom_call_target="tpu_custom_call" | custom-call | flops 1 | bytes 1 | tf_op jit(solution)/shard_map/mixer_back/pallas_call | solution.py:649
  308.0 11.5 %collective-permute-done.41 = bf16[8,144,768]{2,1,0:T(8,128)(2,1)} collective-permute-done((bf16[8,144,768]{2,1,0:T(8,128)(2,1)}, bf16[8,144,768]{2,1,0:T(8,128)(2,1)}, u32[]{:S(2)}, u32[]{:S(2)}) %collective-permute-start.41) | collective-permute-done | bytes 1769504 | tf_op jit(solution)/shard_map/ppermute | solution.py:42
  331.0 6.8 %collective-permute-done.38 = bf16[2,192,384]{2,1,0:T(8,128)(2,1)S(1)} collective-permute-done((bf16[2,192,384]{2,1,0:T(8,128)(2,1)S(1)}, bf16[2,192,384]{2,1,0:T(8,128)(2,1)S(1)}, u32[]{:S(2)}, u32[]{:S(2)}) %collective-permute-start.38) | collective-permute-done | bytes 294944 | tf_op jit(solution)/shard_map/ppermute | solution.py:42
  339.7 22.1 %mlp_back.3 = (f32[768,384]{1,0:T(8,128)S(1)}, bf16[768,384]{1,0:T(8,128)(2,1)S(1)}, bf16[8,144,768]{2,1,0:T(8,128)(2,1)}, bf16[8,144,768]{2,1,0:T(8,128)(2,1)},...) custom-call(s32[3]{0:T(128)S(1)} %pad_add_fusion.refs_0_, bf16[768,768]{1,0:T(8,128)(2,1)} %pad_maximum_fusion.8.refs_1_, ...), custom_call_target="tpu_custom_call" | custom-call | flops 10871635968 | bytes 18874368 | tf_op jit(solution)/shard_map/mlp_back/pallas_call | solution.py:277
  378.3 18.0 %collective-permute-done.52 = bf16[2,288,768]{2,1,0:T(8,128)(2,1)S(1)} collective-permute-done((bf16[2,288,768]{2,1,0:T(8,128)(2,1)S(1)}, bf16[2,288,768]{2,1,0:T(8,128)(2,1)S(1)}, u32[]{:S(2)}, u32[]{:S(2)}) %collective-permute-start.52) | collective-permute-done | bytes 884768 | tf_op jit(solution)/shard_map/ppermute | solution.py:42
  401.6 20.9 %mixer_back.3 = (f32[768,384]{1,0:T(8,128)}, bf16[768,384]{1,0:T(8,128)(2,1)S(1)}, bf16[8,128,768]{2,1,0:T(8,128)(2,1)}, bf16[8,128,768]{2,1,0:T(8,128)(2,1)}) custom-call(s32[3]{0:T(128)S(1)} %pad_add_fusion.refs_0_, f32[8,768]{1,0:T(8,128)S(1)} %broadcast_in_dim.15.refs_1_, bf16[512,1024]{1,0:T(8,128)(2,1)} %constant.214.refs_2_, ...), custom_call_target="tpu_custom_call" | custom-call | flops 1 | bytes 1 | tf_op jit(solution)/shard_map/mixer_back/pallas_call | solution.py:649
  430.7 8.7 %collective-permute-done.54 = bf16[1,288,768]{2,1,0:T(8,128)(2,1)S(1)} collective-permute-done((bf16[1,288,768]{2,1,0:T(8,128)(2,1)S(1)}, bf16[1,288,768]{2,1,0:T(8,128)(2,1)S(1)}, u32[]{:S(2)}, u32[]{:S(2)}) %collective-permute-start.54) | collective-permute-done | bytes 442400 | tf_op jit(solution)/shard_map/ppermute | solution.py:42
  456.5 11.6 %collective-permute-done.65 = bf16[4,144,768]{2,1,0:T(8,128)(2,1)} collective-permute-done((bf16[4,144,768]{2,1,0:T(8,128)(2,1)}, bf16[4,144,768]{2,1,0:T(8,128)(2,1)}, u32[]{:S(2)}, u32[]{:S(2)}) %collective-permute-start.65) | collective-permute-done | bytes 884768 | tf_op jit(solution)/shard_map/ppermute | solution.py:42
  471.7 9.0 %collective-permute-start.67 = (bf16[2,288,768]{2,1,0:T(8,128)(2,1)S(1)}, bf16[2,288,768]{2,1,0:T(8,128)(2,1)S(1)}, u32[]{:S(2)}, u32[]{:S(2)}) collective-permute-start(bf16[2,288,768]{2,1,0:T(8,128)(2,1)S(1)} %fusion.16), channel_id=1, source_target_pairs={{0,1},{1,0},{2,3},{3,2},{4,5},{5,4},{6,7},{7,6},{8,9},{9,8},{10,11... | collective-permute-start | bytes 2654216 | tf_op jit(solution)/shard_map/ppermute | solution.py:42
  486.2 12.2 %collective-permute-done.67 = bf16[2,288,768]{2,1,0:T(8,128)(2,1)S(1)} collective-permute-done((bf16[2,288,768]{2,1,0:T(8,128)(2,1)S(1)}, bf16[2,288,768]{2,1,0:T(8,128)(2,1)S(1)}, u32[]{:S(2)}, u32[]{:S(2)}) %collective-permute-start.67) | collective-permute-done | bytes 884768 | tf_op jit(solution)/shard_map/ppermute | solution.py:42
  498.8 9.7 %collective-permute-done.74 = bf16[4,64,768]{2,1,0:T(8,128)(2,1)S(1)} collective-permute-done((bf16[4,64,768]{2,1,0:T(8,128)(2,1)S(1)}, bf16[4,64,768]{2,1,0:T(8,128)(2,1)S(1)}, u32[]{:S(2)}, u32[]{:S(2)}) %collective-permute-start.74) | collective-permute-done | bytes 393248 | tf_op jit(solution)/shard_map/ppermute | solution.py:42
  528.6 6.6 %final_mlp.2 = (f32[2,768,2,768]{3,2,1,0:T(2,128)}, f32[2,768,768]{2,1,0:T(8,128)}) custom-call(s32[3]{0:T(128)S(1)} %pad_add_fusion.refs_0_, bf16[4,288,768]{2,1,0:T(8,128)(2,1)S(1)} %pad_maximum_fusion.2.refs_1_, bf16[4,288,768]{2,1,0:T(8,128)(2,1)} %copy-done.38), custom_call_target="tpu_custom_call" | custom-call | flops 1 | bytes 1 | tf_op jit(solution)/shard_map/final_mlp/pallas_call | solution.py:732
  536.1 20.6 %collective-permute-start.84 = (bf16[2,192,512]{2,1,0:T(8,128)(2,1)S(1)}, bf16[2,192,512]{2,1,0:T(8,128)(2,1)S(1)}, u32[]{:S(2)}, u32[]{:S(2)}) collective-permute-start(bf16[2,192,512]{2,1,0:T(8,128)(2,1)S(1)} %pad_maximum_fusion.42), channel_id=1, source_target_pairs={{0,1},{1,0},{2,3},{3,2},{4,5},{5,4},{6,7},{7,6},{8,9},{9,8},{10,11... | collective-permute-start | bytes 1179656 | tf_op jit(solution)/shard_map/ppermute | solution.py:42
  603.4 6.6 %final_mlp.3 = (f32[2,768,2,768]{3,2,1,0:T(2,128)}, f32[2,768,768]{2,1,0:T(8,128)}) custom-call(s32[3]{0:T(128)S(1)} %pad_add_fusion.refs_0_, bf16[4,288,768]{2,1,0:T(8,128)(2,1)S(1)} %maximum_maximum_fusion.refs_1_, bf16[4,288,768]{2,1,0:T(8,128)(2,1)} %collective-permute-done.95.refs_2_, ...), custom_call_target="tpu_custom_call", output_to_operand_aliasing={{0}: (3, {}), {1}: (4, {})} | custom-call | flops 1 | bytes 1 | tf_op jit(solution)/shard_map/final_mlp/pallas_call | solution.py:732
  (609 shorter events, 267.1 us)
Async XLA Ops:
  1.4 33.1 %collective-permute-start.6 = (s32[6]{0:T(128)S(1)}, s32[6]{0:T(128)S(1)}, u32[]{:S(2)}, u32[]{:S(2)}) collective-permute-start(s32[6]{0:T(128)S(1)} %pad_add_fusion.1), channel_id=1, source_target_pairs={{0,4},{4,0},{8,12},{12,8},{16,20},{20,16},{24,28},{28,24},{1,5},{5... | collective-permute-start | bytes 80 | tf_op jit(solution)/shard_map/ppermute | solution.py:42
  7.7 32.7 %collective-permute-start.2 = (bf16[1,128,768]{2,1,0:T(8,128)(2,1)}, bf16[1,128,768]{2,1,0:T(8,128)(2,1)}, u32[]{:S(2)}, u32[]{:S(2)}) collective-permute-start(bf16[1,128,768]{2,1,0:T(8,128)(2,1)} %maximum_bitcast_fusion.2), channel_id=1, source_target_pairs={{0,3},{1,2},{2,1},{3,0},{4,7},{5,6},{6,5},{7,4},{8,11},{9,10},{10,... | collective-permute-start | bytes 589832 | tf_op jit(solution)/shard_map/ppermute | solution.py:42
  13.4 102.8 %collective-permute-start.13 = (bf16[1,128,768]{2,1,0:T(8,128)(2,1)}, bf16[1,128,768]{2,1,0:T(8,128)(2,1)}, u32[]{:S(2)}, u32[]{:S(2)}) collective-permute-start(bf16[1,128,768]{2,1,0:T(8,128)(2,1)} %maximum_bitcast_fusion.3), channel_id=1, source_target_pairs={{0,3},{1,2},{2,1},{3,0},{4,7},{5,6},{6,5},{7,4},{8,11},{9,10},{10,... | collective-permute-start | bytes 589832 | tf_op jit(solution)/shard_map/ppermute | solution.py:42
  26.4 43.8 %collective-permute-start.4 = (bf16[1,288,768]{2,1,0:T(8,128)(2,1)}, bf16[1,288,768]{2,1,0:T(8,128)(2,1)}, u32[]{:S(2)}, u32[]{:S(2)}) collective-permute-start(bf16[1,288,768]{2,1,0:T(8,128)(2,1)} %maximum_bitcast_fusion), channel_id=1, source_target_pairs={{0,3},{1,2},{2,1},{3,0},{4,7},{5,6},{6,5},{7,4},{8,11},{9,10},{10,... | collective-permute-start | bytes 1327112 | tf_op jit(solution)/shard_map/ppermute | solution.py:42
  119.3 41.7 %collective-permute-start.23 = (bf16[6,144,768]{2,1,0:T(8,128)(2,1)S(1)}, bf16[6,144,768]{2,1,0:T(8,128)(2,1)S(1)}, u32[]{:S(2)}, u32[]{:S(2)}) collective-permute-start(bf16[6,144,768]{2,1,0:T(8,128)(2,1)S(1)} %pad_maximum_fusion.3.refs_3_.refs_5_), channel_id=1, source_target_pairs={{0,16},{4,20},{8,24},{12,28},{16,0},{20,4},{24,8},{28,12},{1,17},{... | collective-permute-start | bytes 3981320 | tf_op jit(solution)/shard_map/ppermute | solution.py:42
  119.8 42.2 %collective-permute-start.24 = (bf16[6,144,768]{2,1,0:T(8,128)(2,1)S(1)}, bf16[6,144,768]{2,1,0:T(8,128)(2,1)}, u32[]{:S(2)}, u32[]{:S(2)}) collective-permute-start(bf16[6,144,768]{2,1,0:T(8,128)(2,1)S(1)} %pad_maximum_fusion.4.refs_5_.refs_7_), channel_id=1, source_target_pairs={{0,8},{4,12},{8,0},{12,4},{16,24},{20,28},{24,16},{28,20},{1,9},{5... | collective-permute-start | bytes 3981320 | tf_op jit(solution)/shard_map/ppermute | solution.py:42
  126.8 31.3 %collective-permute-start.21 = (bf16[3,64,768]{2,1,0:T(8,128)(2,1)S(1)}, bf16[3,64,768]{2,1,0:T(8,128)(2,1)S(1)}, u32[]{:S(2)}, u32[]{:S(2)}) collective-permute-start(bf16[3,64,768]{2,1,0:T(8,128)(2,1)S(1)} %get-tuple-element.413), channel_id=1, source_target_pairs={{0,8},{4,12},{8,0},{12,4},{16,24},{20,28},{24,16},{28,20},{1,9},{5... | collective-permute-start | bytes 884744 | tf_op jit(solution)/shard_map/ppermute | solution.py:42
  210.6 31.5 %collective-permute-start.35 = (bf16[6,144,768]{2,1,0:T(8,128)(2,1)S(1)}, bf16[6,144,768]{2,1,0:T(8,128)(2,1)S(1)}, u32[]{:S(2)}, u32[]{:S(2)}) collective-permute-start(bf16[6,144,768]{2,1,0:T(8,128)(2,1)S(1)} %pad_maximum_fusion.5.refs_3_.refs_5_), channel_id=1, source_target_pairs={{0,16},{4,20},{8,24},{12,28},{16,0},{20,4},{24,8},{28,12},{1,17},{... | collective-permute-start | bytes 3981320 | tf_op jit(solution)/shard_map/ppermute | solution.py:42
  212.1 31.3 %collective-permute-start.36 = (bf16[6,144,768]{2,1,0:T(8,128)(2,1)S(1)}, bf16[6,144,768]{2,1,0:T(8,128)(2,1)}, u32[]{:S(2)}, u32[]{:S(2)}) collective-permute-start(bf16[6,144,768]{2,1,0:T(8,128)(2,1)S(1)} %pad_maximum_fusion.6.refs_5_.refs_7_), channel_id=1, source_target_pairs={{0,8},{4,12},{8,0},{12,4},{16,24},{20,28},{24,16},{28,20},{1,9},{5... | collective-permute-start | bytes 3981320 | tf_op jit(solution)/shard_map/ppermute | solution.py:42
  278.2 41.3 %collective-permute-start.41 = (bf16[8,144,768]{2,1,0:T(8,128)(2,1)}, bf16[8,144,768]{2,1,0:T(8,128)(2,1)}, u32[]{:S(2)}, u32[]{:S(2)}) collective-permute-start(bf16[8,144,768]{2,1,0:T(8,128)(2,1)} %get-tuple-element.172), channel_id=1, source_target_pairs={{0,8},{4,12},{8,0},{12,4},{16,24},{20,28},{24,16},{28,20},{1,9},{5... | collective-permute-start | bytes 5308424 | tf_op jit(solution)/shard_map/ppermute | solution.py:42
  279.9 41.0 %collective-permute-start.44 = (bf16[8,144,768]{2,1,0:T(8,128)(2,1)}, bf16[8,144,768]{2,1,0:T(8,128)(2,1)}, u32[]{:S(2)}, u32[]{:S(2)}) collective-permute-start(bf16[8,144,768]{2,1,0:T(8,128)(2,1)} %get-tuple-element.173), channel_id=1, source_target_pairs={{0,16},{4,20},{8,24},{12,28},{16,0},{20,4},{24,8},{28,12},{1,17},{... | collective-permute-start | bytes 5308424 | tf_op jit(solution)/shard_map/ppermute | solution.py:42
  329.4 41.9 %collective-permute-start.46 = (bf16[8,128,768]{2,1,0:T(8,128)(2,1)}, bf16[8,128,768]{2,1,0:T(8,128)(2,1)}, u32[]{:S(2)}, u32[]{:S(2)}) collective-permute-start(bf16[8,128,768]{2,1,0:T(8,128)(2,1)} %get-tuple-element.184), channel_id=1, source_target_pairs={{0,1},{1,0},{2,3},{3,2},{4,5},{5,4},{6,7},{7,6},{8,9},{9,8},{10,11... | collective-permute-start | bytes 4718600 | tf_op jit(solution)/shard_map/ppermute | solution.py:42
  329.4 32.5 %collective-permute-start.47 = (bf16[4,144,768]{2,1,0:T(8,128)(2,1)}, bf16[4,144,768]{2,1,0:T(8,128)(2,1)S(1)}, u32[]{:S(2)}, u32[]{:S(2)}) collective-permute-start(bf16[4,144,768]{2,1,0:T(8,128)(2,1)} %add_convert_fusion.15), channel_id=1, source_target_pairs={{0,16},{4,20},{8,24},{12,28},{16,0},{20,4},{24,8},{28,12},{1,17},{... | collective-permute-start | bytes 2654216 | tf_op jit(solution)/shard_map/ppermute | solution.py:42
  374.9 49.6 %collective-permute-start.55 = (bf16[8,144,768]{2,1,0:T(8,128)(2,1)}, bf16[8,144,768]{2,1,0:T(8,128)(2,1)}, u32[]{:S(2)}, u32[]{:S(2)}) collective-permute-start(bf16[8,144,768]{2,1,0:T(8,128)(2,1)} %get-tuple-element.194), channel_id=1, source_target_pairs={{0,8},{4,12},{8,0},{12,4},{16,24},{20,28},{24,16},{28,20},{1,9},{5... | collective-permute-start | bytes 5308424 | tf_op jit(solution)/shard_map/ppermute | solution.py:42
  376.5 49.3 %collective-permute-start.59 = (bf16[8,144,768]{2,1,0:T(8,128)(2,1)}, bf16[8,144,768]{2,1,0:T(8,128)(2,1)}, u32[]{:S(2)}, u32[]{:S(2)}) collective-permute-start(bf16[8,144,768]{2,1,0:T(8,128)(2,1)} %get-tuple-element.195), channel_id=1, source_target_pairs={{0,16},{4,20},{8,24},{12,28},{16,0},{20,4},{24,8},{28,12},{1,17},{... | collective-permute-start | bytes 5308424 | tf_op jit(solution)/shard_map/ppermute | solution.py:42
  396.6 46.1 %collective-permute-start.45 = (bf16[2,192,384]{2,1,0:T(8,128)(2,1)}, bf16[2,192,384]{2,1,0:T(8,128)(2,1)S(1)}, u32[]{:S(2)}, u32[]{:S(2)}) collective-permute-start(bf16[2,192,384]{2,1,0:T(8,128)(2,1)} %pad_maximum_fusion.46), channel_id=1, source_target_pairs={{0,1},{1,0},{2,3},{3,2},{4,5},{5,4},{6,7},{7,6},{8,9},{9,8},{10,11... | collective-permute-start | bytes 884744 | tf_op jit(solution)/shard_map/ppermute | solution.py:42
  397.8 42.5 %collective-permute-start.60 = (bf16[2,64,768]{2,1,0:T(8,128)(2,1)S(1)}, bf16[2,64,768]{2,1,0:T(8,128)(2,1)}, u32[]{:S(2)}, u32[]{:S(2)}) collective-permute-start(bf16[2,64,768]{2,1,0:T(8,128)(2,1)S(1)} %get-tuple-element.359), channel_id=1, source_target_pairs={{0,8},{4,12},{8,0},{12,4},{16,24},{20,28},{24,16},{28,20},{1,9},{5... | collective-permute-start | bytes 589832 | tf_op jit(solution)/shard_map/ppermute | solution.py:42
  399.4 41.3 %collective-permute-start.53 = (bf16[2,64,768]{2,1,0:T(8,128)(2,1)}, bf16[2,64,768]{2,1,0:T(8,128)(2,1)}, u32[]{:S(2)}, u32[]{:S(2)}) collective-permute-start(bf16[2,64,768]{2,1,0:T(8,128)(2,1)} %get-tuple-element.360), channel_id=1, source_target_pairs={{0,16},{4,20},{8,24},{12,28},{16,0},{20,4},{24,8},{28,12},{1,17},{... | collective-permute-start | bytes 589832 | tf_op jit(solution)/shard_map/ppermute | solution.py:42
  425.9 55.5 %collective-permute-start.62 = (bf16[8,128,768]{2,1,0:T(8,128)(2,1)}, bf16[8,128,768]{2,1,0:T(8,128)(2,1)}, u32[]{:S(2)}, u32[]{:S(2)}) collective-permute-start(bf16[8,128,768]{2,1,0:T(8,128)(2,1)} %get-tuple-element.209), channel_id=1, source_target_pairs={{0,1},{1,0},{2,3},{3,2},{4,5},{5,4},{6,7},{7,6},{8,9},{9,8},{10,11... | collective-permute-start | bytes 4718600 | tf_op jit(solution)/shard_map/ppermute | solution.py:42
  440.3 40.4 %collective-permute-start.63 = (bf16[1,288,768]{2,1,0:T(8,128)(2,1)S(1)}, bf16[1,288,768]{2,1,0:T(8,128)(2,1)S(1)}, u32[]{:S(2)}, u32[]{:S(2)}) collective-permute-start(bf16[1,288,768]{2,1,0:T(8,128)(2,1)S(1)} %add_convert_fusion.17), channel_id=1, source_target_pairs={{0,8},{4,12},{8,0},{12,4},{16,24},{20,28},{24,16},{28,20},{1,9},{5... | collective-permute-start | bytes 1327112 | tf_op jit(solution)/shard_map/ppermute | solution.py:42
  442.7 42.5 %collective-permute-start.68 = (bf16[1,128,768]{2,1,0:T(8,128)(2,1)}, bf16[1,128,768]{2,1,0:T(8,128)(2,1)}, u32[]{:S(2)}, u32[]{:S(2)}) collective-permute-start(bf16[1,128,768]{2,1,0:T(8,128)(2,1)} %fusion.31), channel_id=1, source_target_pairs={{0,3},{1,2},{2,1},{3,0},{4,7},{5,6},{6,5},{7,4},{8,11},{9,10},{10,... | collective-permute-start | bytes 589832 | tf_op jit(solution)/shard_map/ppermute | solution.py:42
  524.6 32.1 %collective-permute-start.81 = (bf16[1,144,768]{2,1,0:T(8,128)(2,1)S(1)}, bf16[1,144,768]{2,1,0:T(8,128)(2,1)S(1)}, u32[]{:S(2)}, u32[]{:S(2)}) collective-permute-start(bf16[1,144,768]{2,1,0:T(8,128)(2,1)S(1)} %get-tuple-element.420), channel_id=1, source_target_pairs={{0,16},{4,20},{8,24},{12,28},{16,0},{20,4},{24,8},{28,12},{1,17},{... | collective-permute-start | bytes 663560 | tf_op jit(solution)/shard_map/ppermute | solution.py:42
  526.5 31.9 %collective-permute-start.76 = (bf16[1,128,768]{2,1,0:T(8,128)(2,1)S(1)}, bf16[1,128,768]{2,1,0:T(8,128)(2,1)S(1)}, u32[]{:S(2)}, u32[]{:S(2)}) collective-permute-start(bf16[1,128,768]{2,1,0:T(8,128)(2,1)S(1)} %pad_maximum_fusion.47), channel_id=1, source_target_pairs={{0,3},{1,2},{2,1},{3,0},{4,7},{5,6},{6,5},{7,4},{8,11},{9,10},{10,... | collective-permute-start | bytes 589832 | tf_op jit(solution)/shard_map/ppermute | solution.py:42
  570.9 32.5 %collective-permute-start.95 = (bf16[4,288,768]{2,1,0:T(8,128)(2,1)S(1)}, bf16[4,288,768]{2,1,0:T(8,128)(2,1)}, u32[]{:S(2)}, u32[]{:S(2)}) collective-permute-start(bf16[4,288,768]{2,1,0:T(8,128)(2,1)S(1)} %maximum_maximum_fusion.refs_1_), channel_id=1, source_target_pairs={{0,4},{4,0},{8,12},{12,8},{16,20},{20,16},{24,28},{28,24},{1,5},{5... | collective-permute-start | bytes 5308424 | tf_op jit(solution)/shard_map/ppermute | solution.py:42
  (154 other events, 1570.8 us)

commit v4 on v3

--- a/solution.py
+++ b/solution.py
@@ -307,6 +307,73 @@
         name="mlp_back",
     )(place, normed, coming, gate_up, own, *buffers)
     return (results[0], results[1], results[2:])
+
+
+def mlp_turn_kernel(plan, routes, count, *refs):
+    (place_ref, normed_ref, coming_ref, own_ref), buffers, outs, scratch = grouped(
+        refs, 4, len(plan), 8, 6
+    )
+    flat_ref, grads_ref, total, back_total, sems, out_sems = scratch
+    fill(plan, place_ref, own_ref, buffers, flat_ref, sems, 1)
+    step = pl.program_id(0)
+    width = normed_ref.shape[0]
+    hidden = flat_ref.shape[1] - width
+    spilled = (routes, count, place_ref, grads_ref, outs[4:], out_sems, 1)
+    spill_wait(*spilled, False)
+    slot = step % 2
+    gate_up = tn(flat_ref[step, :width], normed_ref[...])
+    gate, up = (gate_up[:hidden], gate_up[hidden:])
+    grad_act = nn(flat_ref[step, width:], coming_ref[...])
+    gelu, slope = gelu_parts(gate)
+    activated = (gelu * up).astype(BF16)
+    grad_gate = (grad_act * up * slope).astype(BF16)
+    grad_up = (grad_act * gelu).astype(BF16)
+    add_total(total, tn(flat_ref[step, width:], activated))
+    grads_ref[slot, width:] = nt(activated, coming_ref[...]).astype(BF16)
+    grads_ref[slot, :width, :hidden] = nt(normed_ref[...], grad_gate).astype(BF16)
+    grads_ref[slot, :width, hidden:] = nt(normed_ref[...], grad_up).astype(BF16)
+    spill(*spilled)
+    add_total(
+        back_total,
+        nn(flat_ref[step, :width, :hidden], grad_gate)
+        + nn(flat_ref[step, :width, hidden:], grad_up),
+    )
+    split_total(total, outs[0], outs[1])
+    split_total(back_total, outs[2], outs[3])
+    spill_wait(*spilled, True)
+
+
+def mlp_turn(place, rows, normed, coming, routes, blocks, block_rows):
+    own, buffers, plan, ranks = rows
+    count, width = own.shape
+    tokens = normed.shape[1]
+    hidden = count - width
+    half = tokens // 2
+    results = pl.pallas_call(
+        functools.partial(mlp_turn_kernel, plan, routes, plan[0][3]),
+        grid=(ranks,),
+        out_shape=[
+            jax.ShapeDtypeStruct((width, half), F32),
+            jax.ShapeDtypeStruct((width, half), BF16),
+        ]
+        * 2
+        + [jax.ShapeDtypeStruct((blocks, block_rows, width), BF16)] * 4,
+        in_specs=[SMEM, whole((width, tokens)), whole((width, tokens)), ANY]
+        + [ANY] * len(buffers),
+        out_specs=[whole((width, half))] * 4 + [ANY] * 4,
+        scratch_shapes=[
+            pltpu.VMEM((ranks, count, width), BF16),
+            pltpu.VMEM((2, count, width), BF16),
+            pltpu.VMEM((width, tokens), F32),
+            pltpu.VMEM((width, tokens), F32),
+            pltpu.SemaphoreType.DMA((ranks, 8)),
+            pltpu.SemaphoreType.DMA((2, 8)),
+        ],
+        compiler_params=PARAMS,
+        cost_estimate=pl.CostEstimate(flops=1, bytes_accessed=1, transcendentals=0),
+        name="mlp_turn",
+    )(place, normed, coming, own, *buffers)
+    return (results[:4], results[4:])
 
 
 def delayed(layout, values, by):
@@ -1015,6 +1082,21 @@
     tables = (table(seq_long), table(seq_short))
     sizes = (seq_long, seq_short, chans, 2)
 
+    chan_order = (0, FAR, NEAR, NEAR ^ FAR)
+
+    def routes(near_first, count, single=False):
+        found = []
+        for half, (one, two) in enumerate(((1, 2), (1, 2)) if single else plane_orders):
+            for a in range(2):
+                for c in range(2):
+                    if near_first:
+                        targets = {r: (i // 2, 4 * a + 2 * c + i % 2) for i, r in enumerate(chan_order)}
+                    else:
+                        targets = {r: (2 * half + a, ranks * c + i) for i, r in enumerate(chan_order)}
+                    found.append((targets, half, a * one + c * two, near_first * half * count))
+        return tuple(found)
+
+    mlp_half, mixer_half = (half_rows("mlp"), half_rows("mixer"))
     residual_start = arrived[:, :tokens].astype(F32)
     residual = residual_start
     stored_all = []
@@ -1045,30 +1127,21 @@
             go(mlp_1)
             go(mixer_1)
             go(mlp_1)
+            gate_up, kept, sent = mlp_forward(
+                spot, weights[layer, "mlp"], after(normed_mlp, *line)
+            )
         else:
             go(grad_steps)
-        gate_up, kept, sent = mlp_forward(
-            spot, weights[layer, "mlp"], after(normed_mlp, *line)
-        )
+            upstream = finish(grad_steps).astype(F32)
+            coming = both_cores(upstream.astype(BF16))
+            gate_up = None
+            (kept, sent, *turned), blocks = mlp_turn(
+                spot, weights[layer, "mlp"], after(normed_mlp, *line), coming, routes(False, mlp_half),
+                2 * ranks, mlp_half,
+            )
         residual = middle + own_sum(sent, kept)
         stored_all.append((normed, norm_stored, proj, long_out, normed_mlp, mlp_stored, gate_up))
-    upstream = finish(grad_steps).astype(F32)
-
     output_steps = from_tokens((residual - residual_start).astype(BF16))
-
-    chan_order = (0, FAR, NEAR, NEAR ^ FAR)
-
-    def routes(near_first, count):
-        found = []
-        for half, (one, two) in enumerate(plane_orders):
-            for a in range(2):
-                for c in range(2):
-                    if near_first:
-                        targets = {r: (i // 2, 4 * a + 2 * c + i % 2) for i, r in enumerate(chan_order)}
-                    else:
-                        targets = {r: (2 * half + a, ranks * c + i) for i, r in enumerate(chan_order)}
-                    found.append((targets, half, a * one + c * two, near_first * half * count))
-        return tuple(found)
 
     def added(values):
         return sum(value.astype(F32) for value in values).astype(BF16)
@@ -1095,25 +1168,26 @@
         ties = yield [mine]
         yield (mine, after(came, *ties))
 
-    def scatter(blocks, early):
+    def scatter(blocks, early, single=False):
         near_first = len(blocks) == 2
+        orders = ((1, 2),) if single else plane_orders
         if near_first:
             came = swap(blocks[1], ("chan", NEAR))
             ties = yield [blocks[1]]
             block = added([blocks[0], after(came, *ties)])
-            count = block.shape[1] // 2
-            parts = [block[:, half * count : (half + 1) * count] for half in range(2)]
+            count = block.shape[1] // len(orders)
+            parts = [block[:, i * count : (i + 1) * count] for i in range(len(orders))]
             kept = [part[:4] for part in parts]
             sent = [part[4:] for part in parts]
         else:
             kept, sent = (blocks[0::2], blocks[1::2])
-        came = [swap(part, plane[one]) for part, (one, _) in zip(sent, plane_orders)]
+        came = [swap(part, plane[one]) for part, (one, _) in zip(sent, orders)]
         ties = yield list(sent)
         came = [after(value, *ties) for value in came]
         middle = kept[0].shape[0] // 2
         sent = [added([k[middle:], c[middle:]]) for k, c in zip(kept, came)]
         kept = [added([k[:middle], c[:middle]]) for k, c in zip(kept, came)]
-        came = [swap(part, plane[two]) for part, (_, two) in zip(sent, plane_orders)]
+        came = [swap(part, plane[two]) for part, (_, two) in zip(sent, orders)]
         ties = yield sent
         came = [after(value, *ties) for value in came]
         block = jnp.concatenate([added([k, c]) for k, c in zip(kept, came)], axis=1)
@@ -1127,17 +1201,19 @@
     upstream_start = upstream
     gain_grads = {}
     scatters = []
-    mlp_half, mixer_half = (half_rows("mlp"), half_rows("mixer"))
 
     line[:] = []
     for layer in reversed(range(layers)):
         normed, norm_stored, proj, long_out, normed_mlp, mlp_stored, gate_up = stored_all[layer]
         last = layer == 0
-        coming = both_cores(upstream.astype(BF16))
-        kept, sent, blocks = mlp_back(
-            spot, weights[layer, "mlp"], normed_mlp, gate_up, coming,
-            routes(False, mlp_half), 2 * ranks, mlp_half,
-        )
+        if gate_up is None:
+            kept, sent = turned
+        else:
+            coming = both_cores(upstream.astype(BF16))
+            kept, sent, blocks = mlp_back(
+                spot, weights[layer, "mlp"], normed_mlp, gate_up, coming,
+                routes(False, mlp_half), 2 * ranks, mlp_half,
+            )
         if last:
             go(scatters[0], kept)
             go(scatters[1], kept)
@@ -1146,20 +1222,19 @@
         change, gain_grads[layer, 1] = norm_back(own_sum(sent, kept), mlp_stored)
         upstream = upstream + change
         coming = both_ordered(upstream.astype(BF16))
-        if last:
-            go(scatters[0])
-            go(scatters[1])
-        else:
+        if not last:
             begin(output_steps)
         kept, sent, blocks = mixer_back(
             spot, weights[layer, "mixer"], normed, after(coming, *line), proj, long_out, live,
-            tables, sizes, routes(True, mixer_half), 2 * ranks, 2 * mixer_half,
+            tables, sizes, routes(True, mixer_half, not last), 2 * ranks, 2 * mixer_half,
         )
         if last:
+            scatters.append(begin(scatter(blocks, None)))
             go(scatters[2], kept)
+            go(scatters[0], kept)
         else:
             go(scatters[0], kept)
-        scatters.append(begin(scatter(blocks, None if last else 1)))
+            scatters.append(begin(scatter(blocks, 1, True)))
         sent = after(sent, *line)
         change, gain_grads[layer, 0] = norm_back(own_sum(sent, kept), norm_stored)
         upstream = upstream + change
@@ -1174,46 +1249,60 @@
     gain_coarse = lax.reduce_precision(gain_parts, 8, 7)
     gain_lanes = jnp.concatenate([gain_coarse, gain_parts - gain_coarse], axis=1).astype(BF16)
     gain_lanes = jnp.pad(gain_lanes, ((0, 0), (0, 128 - gain_lanes.shape[1])))
+    go(output_steps)
+    go(mixer_early)
+    go(mlp_late)
     go(mlp_early)
+    gone_long, gone_short, _ = finish(output_steps)
+    output_long = input_long + gone_long.astype(F32)
+    output_short = input_short + gone_short.astype(F32)
+    line.append(output_long)
+    go(mixer_late)
+    changed = jnp.concatenate([(upstream - upstream_start).astype(BF16), gain_lanes], axis=1)
+    back_steps = begin(from_tokens(after(changed, *line)))
     go(mixer_early)
-    go(output_steps)
     go(mlp_late)
     go(mlp_early)
     go(mixer_late)
     go(mixer_early)
+    go(back_steps)
     go(mlp_late)
-    changed = jnp.concatenate([(upstream - upstream_start).astype(BF16), gain_lanes], axis=1)
-    back_steps = begin(from_tokens(after(changed, *line)))
     go(mixer_late)
     go(mlp_early)
     go(mixer_early)
+    go(back_steps)
     go(mlp_late)
     go(mixer_late)
     mlp_out = final_mlp(spot, finish(mlp_early), mlp_count, 1, layers, None)
     line.append(mlp_out[1])
     go(mixer_early)
-    go(back_steps)
-    go(mlp_late)
-    go(mixer_late)
-    mixer_out = final_mixer(spot, finish(mixer_early), mixer_count, chans, 1, layers, None)
-    line.append(mixer_out[1])
-    go(back_steps)
-    go(mlp_late)
-    go(mixer_late)
-    go(mixer_late)
-
-    gone_long, gone_short, _ = finish(output_steps)
-    output_long = input_long + gone_long.astype(F32)
-    output_short = input_short + gone_short.astype(F32)
     gone_long, gone_short, gain_sums = finish(back_steps)
     back_long = grad_long + gone_long.astype(F32)
     back_short = grad_short + gone_short.astype(F32)
+    line.append(back_long)
     gain_sums = jnp.sum(gain_sums[:, :, : 4 * layers].astype(F32), axis=0)
     gain_sums = (gain_sums[:, : 2 * layers] + gain_sums[:, 2 * layers :]).T
-    for step in [mate] + list(plane.values()) + extra_steps:
-        gain_sums = gain_sums + swap(gain_sums, step)
-
+
+
+    def reduced(values):
+        for step in [mate] + list(plane.values()) + extra_steps:
+            came = swap(values, step)
+            values = values + after(came, *(yield [values]))
+        yield values
+
+    gain_steps = begin(reduced(gain_sums))
+    go(mlp_late)
+    go(gain_steps)
+    go(mixer_late)
+    go(gain_steps)
+    for _ in extra_steps:
+        go(gain_steps)
+    mixer_out = final_mixer(spot, finish(mixer_early), mixer_count, chans, 1, layers, None)
+    line.append(mixer_out[1])
+    gain_sums = finish(gain_steps)
     mlp_out = final_mlp(spot, finish(mlp_late), mlp_count, 0, layers, mlp_out)
+    line.append(mlp_out[1])
+    go(mixer_late)
     mixer_out = final_mixer(spot, finish(mixer_late), mixer_count, chans, 0, layers, mixer_out)
     into_out, out_out, filter_out = mixer_out
     taps = jnp.swapaxes(filter_out[:, :, seq_long : seq_long + 12], 1, 2)

time: 620 us -> 597 us (0.963)
  starting transfers between devices: 129 us -> 104 us
    pallas_call x0 -> x1, Pallas kernels: none -> 31.9 us  [mlp_turn(): pl.pallas_call(functools.partial(mlp_turn_kernel, plan, routes, plan[0][3...]
    ppermute x96 -> x94, starting transfers between devices: 129 us -> 104 us  [swap(): lax.ppermute(values, axis, [(i, i ^ mask) for i in range(lax.axis_size(ax...]
    pallas_call x2 -> x1, Pallas kernels: 44.4 us -> 22.1 us  [mlp_back(): pl.pallas_call(functools.partial(mlp_back_kernel, plan, routes, plan[0][3...]
    pallas_call x2 -> x1, Pallas kernels: 24.8 us -> 12.4 us  [mlp_forward(): pl.pallas_call(functools.partial(mlp_forward_kernel, plan), grid=(ranks,)...]
    ppermute x96 -> x94, waiting for transfers between devices: 195 us -> 198 us  [swap(): lax.ppermute(values, axis, [(i, i ^ mask) for i in range(lax.axis_size(ax...]
    unnamed x176 -> x140, local copies, waits for them, and re-layouts: 17.1 us -> 18.9 us
  transfers between devices with their start and end apart: 96 -> 94, of which waited for: 32 -> 33; matrix products, arithmetic and copies ran while one was open for 18% -> 17% of each run, Pallas kernels for 19% -> 20%
where the time goes in v4:
time: 597 us; the launch traced here: 587 us
  waiting for transfers between devices  198 us (33%)
  Pallas kernels  155 us (26%)
  starting transfers between devices  104 us (17%)
  other arithmetic  82.7 us (14%)
  local copies, waits for them, and re-layouts  44.2 us (7%)
    ppermute x94, waiting for transfers between devices, swap(): lax.ppermute(values, axis, [(i, i ^ mask) for i in range(lax.axis_size(ax...  198 us
    ppermute x94, starting transfers between devices, swap(): lax.ppermute(values, axis, [(i, i ^ mask) for i in range(lax.axis_size(ax...  104 us
    pallas_call x2, Pallas kernels, mixer_back(): pl.pallas_call(functools.partial(mixer_back_kernel, plan, routes, plan[0]...  41.3 us
    pallas_call x1, Pallas kernels, mlp_turn(): pl.pallas_call(functools.partial(mlp_turn_kernel, plan, routes, plan[0][3...  31.9 us
    convert_element_type x20, other arithmetic, added(): return sum((value.astype(F32) for value in values)).astype(BF16)  25.7 us
    pallas_call x2, Pallas kernels, mixer_forward(): pl.pallas_call(functools.partial(mixer_forward_kernel, plan, sizes), grid...  25.6 us
    pallas_call x1, Pallas kernels, mlp_back(): pl.pallas_call(functools.partial(mlp_back_kernel, plan, routes, plan[0][3...  22.1 us
    unnamed x140, local copies, waits for them, and re-layouts  18.9 us
  transfers between devices with their start and end apart: 94, of which 33 were waited for; matrix products, arithmetic and copies ran while one was open for 17% of the time, Pallas kernels for 20%

profile of v4, /device:TPU:0, one launch (start us, length us, event | category | flops | bytes accessed | tf_op | source)
XLA Modules:
  0.0 587.4 jit_solution(2396612534411198881)
XLA Ops:
  44.8 8.5 %collective-permute-done.1 = bf16[2,192,512]{2,1,0:T(8,128)(2,1)S(1)} collective-permute-done((bf16[2,192,512]{2,1,0:T(8,128)(2,1)S(1)}, bf16[2,192,512]{2,1,0:T(8,128)(2,1)S(1)}, u32[]{:S(2)}, u32[]{:S(2)}) %collective-permute-start.1) | collective-permute-done | bytes 393248 | tf_op jit(solution)/shard_map/ppermute | solution.py:42
  53.3 13.0 %collective-permute-start.3 = (bf16[2,192,512]{2,1,0:T(8,128)(2,1)S(1)}, bf16[2,192,512]{2,1,0:T(8,128)(2,1)S(1)}, u32[]{:S(2)}, u32[]{:S(2)}) collective-permute-start(bf16[2,192,512]{2,1,0:T(8,128)(2,1)S(1)} %pad_maximum_fusion.38), channel_id=1, source_target_pairs={{0,1},{1,0},{2,3},{3,2},{4,5},{5,4},{6,7},{7,6},{8,9},{9,8},{10,11... | collective-permute-start | bytes 1179656 | tf_op jit(solution)/shard_map/ppermute | solution.py:42
  82.9 11.1 %collective-permute-done.8 = bf16[2,288,768]{2,1,0:T(8,128)(2,1)} collective-permute-done((bf16[2,288,768]{2,1,0:T(8,128)(2,1)}, bf16[2,288,768]{2,1,0:T(8,128)(2,1)}, u32[]{:S(2)}, u32[]{:S(2)}) %collective-permute-start.8) | collective-permute-done | bytes 884768 | tf_op jit(solution)/shard_map/ppermute | solution.py:42
  103.4 12.7 %mixer_forward.2 = (bf16[2,576,768]{2,1,0:T(8,128)(2,1)}, bf16[2,192,768]{2,1,0:T(8,128)(2,1)S(1)}, f32[768,384]{1,0:T(8,128)}, bf16[768,384]{1,0:T(8,128)(2,1)S(1)}) custom-call(s32[3]{0:T(128)S(1)} %pad_add_fusion.refs_0_, f32[8,768]{1,0:T(8,128)S(1)} %broadcast_in_dim.15.refs_1_, bf16[512,1024]{1,0:T(8,128)(2,1)} %constant.214.refs_2_, ...), custom_call_target="tpu_custom_call" | custom-call | flops 1 | bytes 1 | tf_op jit(solution)/shard_map/mixer_forward/pallas_call | solution.py:597
  128.6 28.5 %collective-permute-done.22 = bf16[3,64,768]{2,1,0:T(8,128)(2,1)S(1)} collective-permute-done((bf16[3,64,768]{2,1,0:T(8,128)(2,1)S(1)}, bf16[3,64,768]{2,1,0:T(8,128)(2,1)S(1)}, u32[]{:S(2)}, u32[]{:S(2)}) %collective-permute-start.22) | collective-permute-done | bytes 294944 | tf_op jit(solution)/shard_map/ppermute | solution.py:42
  162.9 12.4 %mlp_forward.1 = (bf16[4,768,768]{2,1,0:T(8,128)(2,1)}, f32[768,384]{1,0:T(8,128)S(1)}, bf16[768,384]{1,0:T(8,128)(2,1)S(1)}) custom-call(s32[3]{0:T(128)S(1)} %pad_add_fusion.refs_0_, bf16[768,768]{1,0:T(8,128)(2,1)} %pad_maximum_fusion.8.refs_1_, bf16[1152,768]{1,0:T(8,128)(2,1)} %pad_maximum_fusion.refs_2_.refs_4_, bf16[6,144,768]{2,1,0:T(8,128)(2,1)} %copy-done.3, ...), custom_call_target="tpu_custom_call" | custom-call | flops 1 | bytes 1 | tf_op jit(solution)/shard_map/mlp_forward/pallas_call | solution.py:178
  196.2 12.9 %mixer_forward.3 = (bf16[2,576,768]{2,1,0:T(8,128)(2,1)}, bf16[2,192,768]{2,1,0:T(8,128)(2,1)S(1)}, f32[768,384]{1,0:T(8,128)}, bf16[768,384]{1,0:T(8,128)(2,1)S(1)}) custom-call(s32[3]{0:T(128)S(1)} %pad_add_fusion.refs_0_, f32[8,768]{1,0:T(8,128)S(1)} %broadcast_in_dim.15.refs_1_, bf16[512,1024]{1,0:T(8,128)(2,1)} %constant.214.refs_2_, ...), custom_call_target="tpu_custom_call" | custom-call | flops 1 | bytes 1 | tf_op jit(solution)/shard_map/mixer_forward/pallas_call | solution.py:597
  217.4 23.6 %collective-permute-done.37.refs_5_ = bf16[6,144,768]{2,1,0:T(8,128)(2,1)S(1)} collective-permute-done((bf16[6,144,768]{2,1,0:T(8,128)(2,1)}, bf16[6,144,768]{2,1,0:T(8,128)(2,1)S(1)}, u32[]{:S(2)}, u32[]{:S(2)}) %collective-permute-start.37) | collective-permute-done | bytes 1327136 | tf_op jit(solution)/shard_map/ppermute | solution.py:42
  242.1 31.9 %mlp_turn.1 = (f32[768,384]{1,0:T(8,128)}, bf16[768,384]{1,0:T(8,128)(2,1)S(1)}, f32[768,384]{1,0:T(8,128)}, bf16[768,384]{1,0:T(8,128)(2,1)S(1)}, bf16[8,144,76...) custom-call(s32[3]{0:T(128)S(1)} %pad_add_fusion.refs_0_, ...), custom_call_target="tpu_custom_call" | custom-call | flops 1 | bytes 1 | tf_op jit(solution)/shard_map/mlp_turn/pallas_call | solution.py:352
  282.9 20.6 %mixer_back.2 = (f32[768,384]{1,0:T(8,128)}, bf16[768,384]{1,0:T(8,128)(2,1)S(1)}, bf16[8,128,768]{2,1,0:T(8,128)(2,1)}, bf16[8,128,768]{2,1,0:T(8,128)(2,1)}) custom-call(s32[3]{0:T(128)S(1)} %pad_add_fusion.refs_0_, f32[8,768]{1,0:T(8,128)S(1)} %broadcast_in_dim.15.refs_1_, bf16[512,1024]{1,0:T(8,128)(2,1)} %constant.214.refs_2_, ...), custom_call_target="tpu_custom_call" | custom-call | flops 1 | bytes 1 | tf_op jit(solution)/shard_map/mixer_back/pallas_call | solution.py:716
  303.5 11.9 %collective-permute-done.41 = bf16[8,144,768]{2,1,0:T(8,128)(2,1)} collective-permute-done((bf16[8,144,768]{2,1,0:T(8,128)(2,1)}, bf16[8,144,768]{2,1,0:T(8,128)(2,1)}, u32[]{:S(2)}, u32[]{:S(2)}) %collective-permute-start.41) | collective-permute-done | bytes 1769504 | tf_op jit(solution)/shard_map/ppermute | solution.py:42
  326.4 7.1 %collective-permute-done.40 = bf16[2,192,384]{2,1,0:T(8,128)(2,1)S(1)} collective-permute-done((bf16[2,192,384]{2,1,0:T(8,128)(2,1)S(1)}, bf16[2,192,384]{2,1,0:T(8,128)(2,1)S(1)}, u32[]{:S(2)}, u32[]{:S(2)}) %collective-permute-start.40) | collective-permute-done | bytes 294944 | tf_op jit(solution)/shard_map/ppermute | solution.py:42
  335.5 22.1 %mlp_back.1 = (f32[768,384]{1,0:T(8,128)S(1)}, bf16[768,384]{1,0:T(8,128)(2,1)S(1)}, bf16[8,144,768]{2,1,0:T(8,128)(2,1)}, bf16[8,144,768]{2,1,0:T(8,128)(2,1)},...) custom-call(s32[3]{0:T(128)S(1)} %pad_add_fusion.refs_0_, bf16[768,768]{1,0:T(8,128)(2,1)} %pad_maximum_fusion.8.refs_1_, ...), custom_call_target="tpu_custom_call" | custom-call | flops 10871635968 | bytes 18874368 | tf_op jit(solution)/shard_map/mlp_back/pallas_call | solution.py:277
  360.9 6.1 %collective-permute-done.52 = bf16[8,128,768]{2,1,0:T(8,128)(2,1)} collective-permute-done((bf16[8,128,768]{2,1,0:T(8,128)(2,1)}, bf16[8,128,768]{2,1,0:T(8,128)(2,1)}, u32[]{:S(2)}, u32[]{:S(2)}) %collective-permute-start.52) | collective-permute-done | bytes 1572896 | tf_op jit(solution)/shard_map/ppermute | solution.py:42
  378.1 20.8 %mixer_back.3 = (f32[768,384]{1,0:T(8,128)}, bf16[768,384]{1,0:T(8,128)(2,1)S(1)}, bf16[8,128,768]{2,1,0:T(8,128)(2,1)}, bf16[8,128,768]{2,1,0:T(8,128)(2,1)}) custom-call(s32[3]{0:T(128)S(1)} %pad_add_fusion.refs_0_, f32[8,768]{1,0:T(8,128)S(1)} %broadcast_in_dim.15.refs_1_, bf16[512,1024]{1,0:T(8,128)(2,1)} %constant.214.refs_2_, ...), custom_call_target="tpu_custom_call" | custom-call | flops 1 | bytes 1 | tf_op jit(solution)/shard_map/mixer_back/pallas_call | solution.py:716
  398.9 12.7 %collective-permute-done.51 = bf16[8,144,768]{2,1,0:T(8,128)(2,1)} collective-permute-done((bf16[8,144,768]{2,1,0:T(8,128)(2,1)}, bf16[8,144,768]{2,1,0:T(8,128)(2,1)}, u32[]{:S(2)}, u32[]{:S(2)}) %collective-permute-start.51) | collective-permute-done | bytes 1769504 | tf_op jit(solution)/shard_map/ppermute | solution.py:42
  422.2 5.8 collective-permute-done.59
  436.1 16.1 %collective-permute-done.60 = bf16[4,144,768]{2,1,0:T(8,128)(2,1)} collective-permute-done((bf16[4,144,768]{2,1,0:T(8,128)(2,1)}, bf16[4,144,768]{2,1,0:T(8,128)(2,1)}, u32[]{:S(2)}, u32[]{:S(2)}) %collective-permute-start.60) | collective-permute-done | bytes 884768 | tf_op jit(solution)/shard_map/ppermute | solution.py:42
  468.3 10.5 %collective-permute-done.68 = bf16[2,288,768]{2,1,0:T(8,128)(2,1)S(1)} collective-permute-done((bf16[2,288,768]{2,1,0:T(8,128)(2,1)S(1)}, bf16[2,288,768]{2,1,0:T(8,128)(2,1)S(1)}, u32[]{:S(2)}, u32[]{:S(2)}) %collective-permute-start.68) | collective-permute-done | bytes 884768 | tf_op jit(solution)/shard_map/ppermute | solution.py:42
  484.5 7.0 %collective-permute-done.65 = bf16[1,128,768]{2,1,0:T(8,128)(2,1)S(1)} collective-permute-done((bf16[1,128,768]{2,1,0:T(8,128)(2,1)S(1)}, bf16[1,128,768]{2,1,0:T(8,128)(2,1)S(1)}, u32[]{:S(2)}, u32[]{:S(2)}) %collective-permute-start.65) | collective-permute-done | bytes 196640 | tf_op jit(solution)/shard_map/ppermute | solution.py:42
  493.7 6.0 %collective-permute-done.74 = bf16[1,288,768]{2,1,0:T(8,128)(2,1)S(1)} collective-permute-done((bf16[1,288,768]{2,1,0:T(8,128)(2,1)S(1)}, bf16[1,288,768]{2,1,0:T(8,128)(2,1)S(1)}, u32[]{:S(2)}, u32[]{:S(2)}) %collective-permute-start.74) | collective-permute-done | bytes 442400 | tf_op jit(solution)/shard_map/ppermute | solution.py:42
  499.7 14.2 %collective-permute-start.70 = (bf16[2,192,512]{2,1,0:T(8,128)(2,1)S(1)}, bf16[2,192,512]{2,1,0:T(8,128)(2,1)S(1)}, u32[]{:S(2)}, u32[]{:S(2)}) collective-permute-start(bf16[2,192,512]{2,1,0:T(8,128)(2,1)S(1)} %pad_maximum_fusion.41), channel_id=1, source_target_pairs={{0,1},{1,0},{2,3},{3,2},{4,5},{5,4},{6,7},{7,6},{8,9},{9,8},{10,11... | collective-permute-start | bytes 1179656 | tf_op jit(solution)/shard_map/ppermute | solution.py:42
  531.2 6.6 %final_mlp.2 = (f32[2,768,2,768]{3,2,1,0:T(2,128)}, f32[2,768,768]{2,1,0:T(8,128)}) custom-call(s32[3]{0:T(128)S(1)} %pad_add_fusion.refs_0_, bf16[4,288,768]{2,1,0:T(8,128)(2,1)S(1)} %pad_maximum_fusion.2.refs_1_, bf16[4,288,768]{2,1,0:T(8,128)(2,1)} %copy-done.28), custom_call_target="tpu_custom_call" | custom-call | flops 1 | bytes 1 | tf_op jit(solution)/shard_map/final_mlp/pallas_call | solution.py:799
  563.4 6.6 %final_mlp.3 = (f32[2,768,2,768]{3,2,1,0:T(2,128)}, f32[2,768,768]{2,1,0:T(8,128)}) custom-call(s32[3]{0:T(128)S(1)} %pad_add_fusion.refs_0_, bf16[4,288,768]{2,1,0:T(8,128)(2,1)S(1)} %maximum_maximum_fusion.refs_1_, bf16[4,288,768]{2,1,0:T(8,128)(2,1)} %copy-done.20, ...), custom_call_target="tpu_custom_call", output_to_operand_aliasing={{0}: (3, {}), {1}: (4, {})} | custom-call | flops 1 | bytes 1 | tf_op jit(solution)/shard_map/final_mlp/pallas_call | solution.py:799
  (568 shorter events, 255.8 us)
Async XLA Ops:
  1.4 35.8 %collective-permute-start.6 = (s32[6]{0:T(128)S(1)}, s32[6]{0:T(128)S(1)}, u32[]{:S(2)}, u32[]{:S(2)}) collective-permute-start(s32[6]{0:T(128)S(1)} %pad_add_fusion.1), channel_id=1, source_target_pairs={{0,4},{4,0},{8,12},{12,8},{16,20},{20,16},{24,28},{28,24},{1,5},{5... | collective-permute-start | bytes 80 | tf_op jit(solution)/shard_map/ppermute | solution.py:42
  4.0 33.9 %collective-permute-start = (bf16[2,192,256]{2,1,0:T(8,128)(2,1)}, bf16[2,192,256]{2,1,0:T(8,128)(2,1)}, u32[]{:S(2)}, u32[]{:S(2)}) collective-permute-start(bf16[2,192,256]{2,1,0:T(8,128)(2,1)} %get-tuple-element.433), channel_id=1, source_target_pairs={{0,4},{4,0},{8,12},{12,8},{16,20},{20,16},{24,28},{28,24},{1,5},{5... | collective-permute-start | bytes 589832 | tf_op jit(solution)/shard_map/ppermute | solution.py:42
  7.7 35.0 %collective-permute-start.2 = (bf16[1,128,768]{2,1,0:T(8,128)(2,1)}, bf16[1,128,768]{2,1,0:T(8,128)(2,1)}, u32[]{:S(2)}, u32[]{:S(2)}) collective-permute-start(bf16[1,128,768]{2,1,0:T(8,128)(2,1)} %maximum_bitcast_fusion.2), channel_id=1, source_target_pairs={{0,3},{1,2},{2,1},{3,0},{4,7},{5,6},{6,5},{7,4},{8,11},{9,10},{10,... | collective-permute-start | bytes 589832 | tf_op jit(solution)/shard_map/ppermute | solution.py:42
  13.5 102.6 %collective-permute-start.13 = (bf16[1,128,768]{2,1,0:T(8,128)(2,1)}, bf16[1,128,768]{2,1,0:T(8,128)(2,1)}, u32[]{:S(2)}, u32[]{:S(2)}) collective-permute-start(bf16[1,128,768]{2,1,0:T(8,128)(2,1)} %maximum_bitcast_fusion.3), channel_id=1, source_target_pairs={{0,3},{1,2},{2,1},{3,0},{4,7},{5,6},{6,5},{7,4},{8,11},{9,10},{10,... | collective-permute-start | bytes 589832 | tf_op jit(solution)/shard_map/ppermute | solution.py:42
  26.3 44.0 %collective-permute-start.4 = (bf16[1,288,768]{2,1,0:T(8,128)(2,1)}, bf16[1,288,768]{2,1,0:T(8,128)(2,1)}, u32[]{:S(2)}, u32[]{:S(2)}) collective-permute-start(bf16[1,288,768]{2,1,0:T(8,128)(2,1)} %maximum_bitcast_fusion), channel_id=1, source_target_pairs={{0,3},{1,2},{2,1},{3,0},{4,7},{5,6},{6,5},{7,4},{8,11},{9,10},{10,... | collective-permute-start | bytes 1327112 | tf_op jit(solution)/shard_map/ppermute | solution.py:42
  119.2 42.5 %collective-permute-start.23 = (bf16[6,144,768]{2,1,0:T(8,128)(2,1)S(1)}, bf16[6,144,768]{2,1,0:T(8,128)(2,1)S(1)}, u32[]{:S(2)}, u32[]{:S(2)}) collective-permute-start(bf16[6,144,768]{2,1,0:T(8,128)(2,1)S(1)} %pad_maximum_fusion.3.refs_3_.refs_5_), channel_id=1, source_target_pairs={{0,16},{4,20},{8,24},{12,28},{16,0},{20,4},{24,8},{28,12},{1,17},{... | collective-permute-start | bytes 3981320 | tf_op jit(solution)/shard_map/ppermute | solution.py:42
  119.8 43.0 %collective-permute-start.24 = (bf16[6,144,768]{2,1,0:T(8,128)(2,1)S(1)}, bf16[6,144,768]{2,1,0:T(8,128)(2,1)}, u32[]{:S(2)}, u32[]{:S(2)}) collective-permute-start(bf16[6,144,768]{2,1,0:T(8,128)(2,1)S(1)} %pad_maximum_fusion.4.refs_5_.refs_7_), channel_id=1, source_target_pairs={{0,8},{4,12},{8,0},{12,4},{16,24},{20,28},{24,16},{28,20},{1,9},{5... | collective-permute-start | bytes 3981320 | tf_op jit(solution)/shard_map/ppermute | solution.py:42
  126.2 30.9 %collective-permute-start.22 = (bf16[3,64,768]{2,1,0:T(8,128)(2,1)S(1)}, bf16[3,64,768]{2,1,0:T(8,128)(2,1)S(1)}, u32[]{:S(2)}, u32[]{:S(2)}) collective-permute-start(bf16[3,64,768]{2,1,0:T(8,128)(2,1)S(1)} %get-tuple-element.406), channel_id=1, source_target_pairs={{0,16},{4,20},{8,24},{12,28},{16,0},{20,4},{24,8},{28,12},{1,17},{... | collective-permute-start | bytes 884744 | tf_op jit(solution)/shard_map/ppermute | solution.py:42
  209.2 31.8 %collective-permute-start.37 = (bf16[6,144,768]{2,1,0:T(8,128)(2,1)}, bf16[6,144,768]{2,1,0:T(8,128)(2,1)S(1)}, u32[]{:S(2)}, u32[]{:S(2)}) collective-permute-start(bf16[6,144,768]{2,1,0:T(8,128)(2,1)} %pad_maximum_fusion.5.refs_4_), channel_id=1, source_target_pairs={{0,16},{4,20},{8,24},{12,28},{16,0},{20,4},{24,8},{28,12},{1,17},{... | collective-permute-start | bytes 3981320 | tf_op jit(solution)/shard_map/ppermute | solution.py:42
  210.0 32.0 %collective-permute-start.38 = (bf16[6,144,768]{2,1,0:T(8,128)(2,1)}, bf16[6,144,768]{2,1,0:T(8,128)(2,1)}, u32[]{:S(2)}, u32[]{:S(2)}) collective-permute-start(bf16[6,144,768]{2,1,0:T(8,128)(2,1)} %pad_maximum_fusion.6.refs_6_), channel_id=1, source_target_pairs={{0,8},{4,12},{8,0},{12,4},{16,24},{20,28},{24,16},{28,20},{1,9},{5... | collective-permute-start | bytes 3981320 | tf_op jit(solution)/shard_map/ppermute | solution.py:42
  274.1 41.3 %collective-permute-start.41 = (bf16[8,144,768]{2,1,0:T(8,128)(2,1)}, bf16[8,144,768]{2,1,0:T(8,128)(2,1)}, u32[]{:S(2)}, u32[]{:S(2)}) collective-permute-start(bf16[8,144,768]{2,1,0:T(8,128)(2,1)} %get-tuple-element.171), channel_id=1, source_target_pairs={{0,8},{4,12},{8,0},{12,4},{16,24},{20,28},{24,16},{28,20},{1,9},{5... | collective-permute-start | bytes 5308424 | tf_op jit(solution)/shard_map/ppermute | solution.py:42
  275.7 41.0 %collective-permute-start.44 = (bf16[8,144,768]{2,1,0:T(8,128)(2,1)}, bf16[8,144,768]{2,1,0:T(8,128)(2,1)}, u32[]{:S(2)}, u32[]{:S(2)}) collective-permute-start(bf16[8,144,768]{2,1,0:T(8,128)(2,1)} %get-tuple-element.172), channel_id=1, source_target_pairs={{0,16},{4,20},{8,24},{12,28},{16,0},{20,4},{24,8},{28,12},{1,17},{... | collective-permute-start | bytes 5308424 | tf_op jit(solution)/shard_map/ppermute | solution.py:42
  325.1 41.8 %collective-permute-start.52 = (bf16[8,128,768]{2,1,0:T(8,128)(2,1)}, bf16[8,128,768]{2,1,0:T(8,128)(2,1)}, u32[]{:S(2)}, u32[]{:S(2)}) collective-permute-start(bf16[8,128,768]{2,1,0:T(8,128)(2,1)} %get-tuple-element.183), channel_id=1, source_target_pairs={{0,1},{1,0},{2,3},{3,2},{4,5},{5,4},{6,7},{7,6},{8,9},{9,8},{10,11... | collective-permute-start | bytes 4718600 | tf_op jit(solution)/shard_map/ppermute | solution.py:42
  325.2 32.4 %collective-permute-start.46 = (bf16[4,144,768]{2,1,0:T(8,128)(2,1)}, bf16[4,144,768]{2,1,0:T(8,128)(2,1)S(1)}, u32[]{:S(2)}, u32[]{:S(2)}) collective-permute-start(bf16[4,144,768]{2,1,0:T(8,128)(2,1)} %add_convert_fusion.15), channel_id=1, source_target_pairs={{0,16},{4,20},{8,24},{12,28},{16,0},{20,4},{24,8},{28,12},{1,17},{... | collective-permute-start | bytes 2654216 | tf_op jit(solution)/shard_map/ppermute | solution.py:42
  326.0 31.6 %collective-permute-start.49 = (bf16[4,144,768]{2,1,0:T(8,128)(2,1)}, bf16[4,144,768]{2,1,0:T(8,128)(2,1)S(1)}, u32[]{:S(2)}, u32[]{:S(2)}) collective-permute-start(bf16[4,144,768]{2,1,0:T(8,128)(2,1)} %add_convert_fusion.14), channel_id=1, source_target_pairs={{0,8},{4,12},{8,0},{12,4},{16,24},{20,28},{24,16},{28,20},{1,9},{5... | collective-permute-start | bytes 2654216 | tf_op jit(solution)/shard_map/ppermute | solution.py:42
  369.8 41.7 %collective-permute-start.51 = (bf16[8,144,768]{2,1,0:T(8,128)(2,1)}, bf16[8,144,768]{2,1,0:T(8,128)(2,1)}, u32[]{:S(2)}, u32[]{:S(2)}) collective-permute-start(bf16[8,144,768]{2,1,0:T(8,128)(2,1)} %get-tuple-element.192), channel_id=1, source_target_pairs={{0,8},{4,12},{8,0},{12,4},{16,24},{20,28},{24,16},{28,20},{1,9},{5... | collective-permute-start | bytes 5308424 | tf_op jit(solution)/shard_map/ppermute | solution.py:42
  370.3 44.0 %collective-permute-start.55 = (bf16[8,144,768]{2,1,0:T(8,128)(2,1)}, bf16[8,144,768]{2,1,0:T(8,128)(2,1)}, u32[]{:S(2)}, u32[]{:S(2)}) collective-permute-start(bf16[8,144,768]{2,1,0:T(8,128)(2,1)} %get-tuple-element.195), channel_id=1, source_target_pairs={{0,16},{4,20},{8,24},{12,28},{16,0},{20,4},{24,8},{28,12},{1,17},{... | collective-permute-start | bytes 5308424 | tf_op jit(solution)/shard_map/ppermute | solution.py:42
  374.0 46.4 %collective-permute-start.45 = (bf16[2,192,384]{2,1,0:T(8,128)(2,1)}, bf16[2,192,384]{2,1,0:T(8,128)(2,1)S(1)}, u32[]{:S(2)}, u32[]{:S(2)}) collective-permute-start(bf16[2,192,384]{2,1,0:T(8,128)(2,1)} %pad_maximum_fusion.46), channel_id=1, source_target_pairs={{0,1},{1,0},{2,3},{3,2},{4,5},{5,4},{6,7},{7,6},{8,9},{9,8},{10,11... | collective-permute-start | bytes 884744 | tf_op jit(solution)/shard_map/ppermute | solution.py:42
  374.0 54.0 %collective-permute-start.59 = (bf16[4,128,768]{2,1,0:T(8,128)(2,1)}, bf16[4,128,768]{2,1,0:T(8,128)(2,1)}, u32[]{:S(2)}, u32[]{:S(2)}) collective-permute-start(bf16[4,128,768]{2,1,0:T(8,128)(2,1)} %slice.588), channel_id=1, source_target_pairs={{0,8},{4,12},{8,0},{12,4},{16,24},{20,28},{24,16},{28,20},{1,9},{5... | collective-permute-start | bytes 2359304 | tf_op jit(solution)/shard_map/ppermute | solution.py:42
  375.8 41.5 %collective-permute-start.50 = (bf16[2,288,768]{2,1,0:T(8,128)(2,1)S(1)}, bf16[2,288,768]{2,1,0:T(8,128)(2,1)S(1)}, u32[]{:S(2)}, u32[]{:S(2)}) collective-permute-start(bf16[2,288,768]{2,1,0:T(8,128)(2,1)S(1)} %pad_maximum_fusion.16), channel_id=1, source_target_pairs={{0,1},{1,0},{2,3},{3,2},{4,5},{5,4},{6,7},{7,6},{8,9},{9,8},{10,11... | collective-permute-start | bytes 2654216 | tf_op jit(solution)/shard_map/ppermute | solution.py:42
  411.6 49.3 %collective-permute-start.62 = (bf16[8,128,768]{2,1,0:T(8,128)(2,1)}, bf16[8,128,768]{2,1,0:T(8,128)(2,1)}, u32[]{:S(2)}, u32[]{:S(2)}) collective-permute-start(bf16[8,128,768]{2,1,0:T(8,128)(2,1)} %get-tuple-element.201), channel_id=1, source_target_pairs={{0,1},{1,0},{2,3},{3,2},{4,5},{5,4},{6,7},{7,6},{8,9},{9,8},{10,11... | collective-permute-start | bytes 4718600 | tf_op jit(solution)/shard_map/ppermute | solution.py:42
  418.4 38.5 %collective-permute-start.57 = (bf16[1,288,768]{2,1,0:T(8,128)(2,1)}, bf16[1,288,768]{2,1,0:T(8,128)(2,1)}, u32[]{:S(2)}, u32[]{:S(2)}) collective-permute-start(bf16[1,288,768]{2,1,0:T(8,128)(2,1)} %slice.593), channel_id=1, source_target_pairs={{0,3},{1,2},{2,1},{3,0},{4,7},{5,6},{6,5},{7,4},{8,11},{9,10},{10,... | collective-permute-start | bytes 1327112 | tf_op jit(solution)/shard_map/ppermute | solution.py:42
  428.0 30.9 %collective-permute-start.56 = (bf16[2,192,256]{2,1,0:T(8,128)(2,1)}, bf16[2,192,256]{2,1,0:T(8,128)(2,1)}, u32[]{:S(2)}, u32[]{:S(2)}) collective-permute-start(bf16[2,192,256]{2,1,0:T(8,128)(2,1)} %get-tuple-element.423), channel_id=1, source_target_pairs={{0,4},{4,0},{8,12},{12,8},{16,20},{20,16},{24,28},{28,24},{1,5},{5... | collective-permute-start | bytes 589832 | tf_op jit(solution)/shard_map/ppermute | solution.py:42
  483.0 31.2 %collective-permute-start.72 = (bf16[2,288,768]{2,1,0:T(8,128)(2,1)S(1)}, bf16[2,288,768]{2,1,0:T(8,128)(2,1)S(1)}, u32[]{:S(2)}, u32[]{:S(2)}) collective-permute-start(bf16[2,288,768]{2,1,0:T(8,128)(2,1)S(1)} %pad_maximum_fusion.19), channel_id=1, source_target_pairs={{0,16},{4,20},{8,24},{12,28},{16,0},{20,4},{24,8},{28,12},{1,17},{... | collective-permute-start | bytes 2654216 | tf_op jit(solution)/shard_map/ppermute | solution.py:42
  (134 other events, 1354.1 us)

commit v5 on v4

--- a/solution.py
+++ b/solution.py
@@ -1233,12 +1233,12 @@
             go(scatters[2], kept)
             go(scatters[0], kept)
         else:
-            go(scatters[0], kept)
             scatters.append(begin(scatter(blocks, 1, True)))
         sent = after(sent, *line)
         change, gain_grads[layer, 0] = norm_back(own_sum(sent, kept), norm_stored)
         upstream = upstream + change
         if not last:
+            go(scatters[0])
             go(output_steps)
 
     mlp_early, mixer_early, mlp_late, mixer_late = scatters
@@ -1285,7 +1285,12 @@
 
 
     def reduced(values):
-        for step in [mate] + list(plane.values()) + extra_steps:
+        came = swap(values, mate)
+        values = values + after(came, *(yield [values]))
+        came = [swap(values, ("batch", 2 * offset)) for offset in range(1, pieces)]
+        ties = yield [values]
+        values = values + sum(after(value, *ties) for value in came)
+        for step in extra_steps:
             came = swap(values, step)
             values = values + after(came, *(yield [values]))
         yield values
@@ -1294,7 +1299,6 @@
     go(mlp_late)
     go(gain_steps)
     go(mixer_late)
-    go(gain_steps)
     for _ in extra_steps:
         go(gain_steps)
     mixer_out = final_mixer(spot, finish(mixer_early), mixer_count, chans, 1, layers, None)

time: 597 us -> 578 us (0.968)
  waiting for transfers between devices: 198 us -> 169 us
  starting transfers between devices: 104 us -> 112 us
    ppermute x94 -> x95, waiting for transfers between devices: 198 us -> 169 us  [swap(): lax.ppermute(values, axis, [(i, i ^ mask) for i in range(lax.axis_size(ax...]
    ppermute x94 -> x95, starting transfers between devices: 104 us -> 112 us  [swap(): lax.ppermute(values, axis, [(i, i ^ mask) for i in range(lax.axis_size(ax...]
    unnamed x140 -> x142, local copies, waits for them, and re-layouts: 18.9 us -> 20.7 us
  transfers between devices with their start and end apart: 94 -> 95, of which waited for: 33 -> 29; matrix products, arithmetic and copies ran while one was open for 17% -> 19% of each run, Pallas kernels for 20% -> 21%
where the time goes in v5:
time: 578 us; the launch traced here: 568 us
  waiting for transfers between devices  169 us (29%)
  Pallas kernels  155 us (27%)
  starting transfers between devices  112 us (19%)
  other arithmetic  81.8 us (14%)
  local copies, waits for them, and re-layouts  46 us (8%)
    ppermute x95, waiting for transfers between devices, swap(): lax.ppermute(values, axis, [(i, i ^ mask) for i in range(lax.axis_size(ax...  169 us
    ppermute x95, starting transfers between devices, swap(): lax.ppermute(values, axis, [(i, i ^ mask) for i in range(lax.axis_size(ax...  112 us
    pallas_call x2, Pallas kernels, mixer_back(): pl.pallas_call(functools.partial(mixer_back_kernel, plan, routes, plan[0]...  41.4 us
    pallas_call x1, Pallas kernels, mlp_turn(): pl.pallas_call(functools.partial(mlp_turn_kernel, plan, routes, plan[0][3...  32 us
    pallas_call x2, Pallas kernels, mixer_forward(): pl.pallas_call(functools.partial(mixer_forward_kernel, plan, sizes), grid...  25.6 us
    convert_element_type x20, other arithmetic, added(): return sum((value.astype(F32) for value in values)).astype(BF16)  24.7 us
    pallas_call x1, Pallas kernels, mlp_back(): pl.pallas_call(functools.partial(mlp_back_kernel, plan, routes, plan[0][3...  22.2 us
    unnamed x142, local copies, waits for them, and re-layouts  20.7 us
  transfers between devices with their start and end apart: 95, of which 29 were waited for; matrix products, arithmetic and copies ran while one was open for 19% of the time, Pallas kernels for 21%

profile of v5, /device:TPU:0, one launch (start us, length us, event | category | flops | bytes accessed | tf_op | source)
XLA Modules:
  0.0 567.7 jit_solution(10819981068792351076)
XLA Ops:
  16.2 5.6 fusion.58
  44.8 8.5 %collective-permute-done.1 = bf16[2,192,512]{2,1,0:T(8,128)(2,1)S(1)} collective-permute-done((bf16[2,192,512]{2,1,0:T(8,128)(2,1)S(1)}, bf16[2,192,512]{2,1,0:T(8,128)(2,1)S(1)}, u32[]{:S(2)}, u32[]{:S(2)}) %collective-permute-start.1) | collective-permute-done | bytes 393248 | tf_op jit(solution)/shard_map/ppermute | solution.py:42
  53.3 13.1 %collective-permute-start.3 = (bf16[2,192,512]{2,1,0:T(8,128)(2,1)S(1)}, bf16[2,192,512]{2,1,0:T(8,128)(2,1)S(1)}, u32[]{:S(2)}, u32[]{:S(2)}) collective-permute-start(bf16[2,192,512]{2,1,0:T(8,128)(2,1)S(1)} %pad_maximum_fusion.38), channel_id=1, source_target_pairs={{0,1},{1,0},{2,3},{3,2},{4,5},{5,4},{6,7},{7,6},{8,9},{9,8},{10,11... | collective-permute-start | bytes 1179656 | tf_op jit(solution)/shard_map/ppermute | solution.py:42
  82.9 11.1 %collective-permute-done.8 = bf16[2,288,768]{2,1,0:T(8,128)(2,1)} collective-permute-done((bf16[2,288,768]{2,1,0:T(8,128)(2,1)}, bf16[2,288,768]{2,1,0:T(8,128)(2,1)}, u32[]{:S(2)}, u32[]{:S(2)}) %collective-permute-start.8) | collective-permute-done | bytes 884768 | tf_op jit(solution)/shard_map/ppermute | solution.py:42
  103.4 12.7 %mixer_forward.2 = (bf16[2,576,768]{2,1,0:T(8,128)(2,1)}, bf16[2,192,768]{2,1,0:T(8,128)(2,1)S(1)}, f32[768,384]{1,0:T(8,128)}, bf16[768,384]{1,0:T(8,128)(2,1)S(1)}) custom-call(s32[3]{0:T(128)S(1)} %pad_add_fusion.refs_0_, f32[8,768]{1,0:T(8,128)S(1)} %broadcast_in_dim.15.refs_1_, bf16[512,1024]{1,0:T(8,128)(2,1)} %constant.214.refs_2_, ...), custom_call_target="tpu_custom_call" | custom-call | flops 1 | bytes 1 | tf_op jit(solution)/shard_map/mixer_forward/pallas_call | solution.py:597
  120.4 5.6 collective-permute-done.17
  128.6 28.5 %collective-permute-done.22 = bf16[3,64,768]{2,1,0:T(8,128)(2,1)S(1)} collective-permute-done((bf16[3,64,768]{2,1,0:T(8,128)(2,1)S(1)}, bf16[3,64,768]{2,1,0:T(8,128)(2,1)S(1)}, u32[]{:S(2)}, u32[]{:S(2)}) %collective-permute-start.22) | collective-permute-done | bytes 294944 | tf_op jit(solution)/shard_map/ppermute | solution.py:42
  162.9 12.4 %mlp_forward.1 = (bf16[4,768,768]{2,1,0:T(8,128)(2,1)}, f32[768,384]{1,0:T(8,128)S(1)}, bf16[768,384]{1,0:T(8,128)(2,1)S(1)}) custom-call(s32[3]{0:T(128)S(1)} %pad_add_fusion.refs_0_, bf16[768,768]{1,0:T(8,128)(2,1)} %pad_maximum_fusion.8.refs_1_, bf16[1152,768]{1,0:T(8,128)(2,1)} %pad_maximum_fusion.refs_2_.refs_4_, bf16[6,144,768]{2,1,0:T(8,128)(2,1)} %copy-done.3, ...), custom_call_target="tpu_custom_call" | custom-call | flops 1 | bytes 1 | tf_op jit(solution)/shard_map/mlp_forward/pallas_call | solution.py:178
  188.1 5.7 collective-permute-start.35
  196.2 12.9 %mixer_forward.3 = (bf16[2,576,768]{2,1,0:T(8,128)(2,1)}, bf16[2,192,768]{2,1,0:T(8,128)(2,1)S(1)}, f32[768,384]{1,0:T(8,128)}, bf16[768,384]{1,0:T(8,128)(2,1)S(1)}) custom-call(s32[3]{0:T(128)S(1)} %pad_add_fusion.refs_0_, f32[8,768]{1,0:T(8,128)S(1)} %broadcast_in_dim.15.refs_1_, bf16[512,1024]{1,0:T(8,128)(2,1)} %constant.214.refs_2_, ...), custom_call_target="tpu_custom_call" | custom-call | flops 1 | bytes 1 | tf_op jit(solution)/shard_map/mixer_forward/pallas_call | solution.py:597
  217.3 23.6 %collective-permute-done.37.refs_5_ = bf16[6,144,768]{2,1,0:T(8,128)(2,1)S(1)} collective-permute-done((bf16[6,144,768]{2,1,0:T(8,128)(2,1)}, bf16[6,144,768]{2,1,0:T(8,128)(2,1)S(1)}, u32[]{:S(2)}, u32[]{:S(2)}) %collective-permute-start.37) | collective-permute-done | bytes 1327136 | tf_op jit(solution)/shard_map/ppermute | solution.py:42
  242.0 32.0 %mlp_turn.1 = (f32[768,384]{1,0:T(8,128)}, bf16[768,384]{1,0:T(8,128)(2,1)S(1)}, f32[768,384]{1,0:T(8,128)}, bf16[768,384]{1,0:T(8,128)(2,1)S(1)}, bf16[8,144,76...) custom-call(s32[3]{0:T(128)S(1)} %pad_add_fusion.refs_0_, ...), custom_call_target="tpu_custom_call" | custom-call | flops 1 | bytes 1 | tf_op jit(solution)/shard_map/mlp_turn/pallas_call | solution.py:352
  282.9 20.7 %mixer_back.2 = (f32[768,384]{1,0:T(8,128)}, bf16[768,384]{1,0:T(8,128)(2,1)S(1)}, bf16[8,128,768]{2,1,0:T(8,128)(2,1)}, bf16[8,128,768]{2,1,0:T(8,128)(2,1)}) custom-call(s32[3]{0:T(128)S(1)} %pad_add_fusion.refs_0_, f32[8,768]{1,0:T(8,128)S(1)} %broadcast_in_dim.15.refs_1_, bf16[512,1024]{1,0:T(8,128)(2,1)} %constant.214.refs_2_, ...), custom_call_target="tpu_custom_call" | custom-call | flops 1 | bytes 1 | tf_op jit(solution)/shard_map/mixer_back/pallas_call | solution.py:716
  305.4 10.0 %collective-permute-done.41 = bf16[8,144,768]{2,1,0:T(8,128)(2,1)} collective-permute-done((bf16[8,144,768]{2,1,0:T(8,128)(2,1)}, bf16[8,144,768]{2,1,0:T(8,128)(2,1)}, u32[]{:S(2)}, u32[]{:S(2)}) %collective-permute-start.41) | collective-permute-done | bytes 1769504 | tf_op jit(solution)/shard_map/ppermute | solution.py:42
  325.7 22.2 %mlp_back.1 = (f32[768,384]{1,0:T(8,128)S(1)}, bf16[768,384]{1,0:T(8,128)(2,1)S(1)}, bf16[8,144,768]{2,1,0:T(8,128)(2,1)}, bf16[8,144,768]{2,1,0:T(8,128)(2,1)},...) custom-call(s32[3]{0:T(128)S(1)} %pad_add_fusion.refs_0_, bf16[768,768]{1,0:T(8,128)(2,1)} %pad_maximum_fusion.8.refs_1_, ...), custom_call_target="tpu_custom_call" | custom-call | flops 10871635968 | bytes 18874368 | tf_op jit(solution)/shard_map/mlp_back/pallas_call | solution.py:277
  364.4 20.7 %mixer_back.3 = (f32[768,384]{1,0:T(8,128)}, bf16[768,384]{1,0:T(8,128)(2,1)S(1)}, bf16[8,128,768]{2,1,0:T(8,128)(2,1)}, bf16[8,128,768]{2,1,0:T(8,128)(2,1)}) custom-call(s32[3]{0:T(128)S(1)} %pad_add_fusion.refs_0_, f32[8,768]{1,0:T(8,128)S(1)} %broadcast_in_dim.15.refs_1_, bf16[512,1024]{1,0:T(8,128)(2,1)} %constant.214.refs_2_, ...), custom_call_target="tpu_custom_call" | custom-call | flops 1 | bytes 1 | tf_op jit(solution)/shard_map/mixer_back/pallas_call | solution.py:716
  385.1 12.0 %collective-permute-done.55 = bf16[8,144,768]{2,1,0:T(8,128)(2,1)} collective-permute-done((bf16[8,144,768]{2,1,0:T(8,128)(2,1)}, bf16[8,144,768]{2,1,0:T(8,128)(2,1)}, u32[]{:S(2)}, u32[]{:S(2)}) %collective-permute-start.55) | collective-permute-done | bytes 1769504 | tf_op jit(solution)/shard_map/ppermute | solution.py:42
  407.8 6.3 %collective-permute-done.59 = bf16[4,128,768]{2,1,0:T(8,128)(2,1)} collective-permute-done((bf16[4,128,768]{2,1,0:T(8,128)(2,1)}, bf16[4,128,768]{2,1,0:T(8,128)(2,1)}, u32[]{:S(2)}, u32[]{:S(2)}) %collective-permute-start.59) | collective-permute-done | bytes 786464 | tf_op jit(solution)/shard_map/ppermute | solution.py:42
  419.0 13.7 %collective-permute-done.60 = bf16[4,144,768]{2,1,0:T(8,128)(2,1)} collective-permute-done((bf16[4,144,768]{2,1,0:T(8,128)(2,1)}, bf16[4,144,768]{2,1,0:T(8,128)(2,1)}, u32[]{:S(2)}, u32[]{:S(2)}) %collective-permute-start.60) | collective-permute-done | bytes 884768 | tf_op jit(solution)/shard_map/ppermute | solution.py:42
  438.0 5.5 collective-permute-done.57
  455.7 20.9 %collective-permute-done.68 = bf16[2,288,768]{2,1,0:T(8,128)(2,1)S(1)} collective-permute-done((bf16[2,288,768]{2,1,0:T(8,128)(2,1)S(1)}, bf16[2,288,768]{2,1,0:T(8,128)(2,1)S(1)}, u32[]{:S(2)}, u32[]{:S(2)}) %collective-permute-start.68) | collective-permute-done | bytes 884768 | tf_op jit(solution)/shard_map/ppermute | solution.py:42
  489.0 8.5 %collective-permute-start.70 = (bf16[2,192,512]{2,1,0:T(8,128)(2,1)S(1)}, bf16[2,192,512]{2,1,0:T(8,128)(2,1)S(1)}, u32[]{:S(2)}, u32[]{:S(2)}) collective-permute-start(bf16[2,192,512]{2,1,0:T(8,128)(2,1)S(1)} %pad_maximum_fusion.41), channel_id=1, source_target_pairs={{0,1},{1,0},{2,3},{3,2},{4,5},{5,4},{6,7},{7,6},{8,9},{9,8},{10,11... | collective-permute-start | bytes 1179656 | tf_op jit(solution)/shard_map/ppermute | solution.py:42
  515.8 6.6 %final_mlp.2 = (f32[2,768,2,768]{3,2,1,0:T(2,128)}, f32[2,768,768]{2,1,0:T(8,128)}) custom-call(s32[3]{0:T(128)S(1)} %pad_add_fusion.refs_0_, bf16[4,288,768]{2,1,0:T(8,128)(2,1)S(1)} %pad_maximum_fusion.2.refs_1_, bf16[4,288,768]{2,1,0:T(8,128)(2,1)} %copy-done.29), custom_call_target="tpu_custom_call" | custom-call | flops 1 | bytes 1 | tf_op jit(solution)/shard_map/final_mlp/pallas_call | solution.py:799
  541.1 6.6 %final_mlp.3 = (f32[2,768,2,768]{3,2,1,0:T(2,128)}, f32[2,768,768]{2,1,0:T(8,128)}) custom-call(s32[3]{0:T(128)S(1)} %pad_add_fusion.refs_0_, bf16[4,288,768]{2,1,0:T(8,128)(2,1)S(1)} %maximum_maximum_fusion.refs_1_, bf16[4,288,768]{2,1,0:T(8,128)(2,1)} %copy-done.20, ...), custom_call_target="tpu_custom_call", output_to_operand_aliasing={{0}: (3, {}), {1}: (4, {})} | custom-call | flops 1 | bytes 1 | tf_op jit(solution)/shard_map/final_mlp/pallas_call | solution.py:799
  (571 shorter events, 239.3 us)
Async XLA Ops:
  1.4 35.8 %collective-permute-start.6 = (s32[6]{0:T(128)S(1)}, s32[6]{0:T(128)S(1)}, u32[]{:S(2)}, u32[]{:S(2)}) collective-permute-start(s32[6]{0:T(128)S(1)} %pad_add_fusion.1), channel_id=1, source_target_pairs={{0,4},{4,0},{8,12},{12,8},{16,20},{20,16},{24,28},{28,24},{1,5},{5... | collective-permute-start | bytes 80 | tf_op jit(solution)/shard_map/ppermute | solution.py:42
  4.0 33.9 %collective-permute-start = (bf16[2,192,256]{2,1,0:T(8,128)(2,1)}, bf16[2,192,256]{2,1,0:T(8,128)(2,1)}, u32[]{:S(2)}, u32[]{:S(2)}) collective-permute-start(bf16[2,192,256]{2,1,0:T(8,128)(2,1)} %get-tuple-element.435), channel_id=1, source_target_pairs={{0,4},{4,0},{8,12},{12,8},{16,20},{20,16},{24,28},{28,24},{1,5},{5... | collective-permute-start | bytes 589832 | tf_op jit(solution)/shard_map/ppermute | solution.py:42
  7.7 34.9 %collective-permute-start.2 = (bf16[1,128,768]{2,1,0:T(8,128)(2,1)}, bf16[1,128,768]{2,1,0:T(8,128)(2,1)}, u32[]{:S(2)}, u32[]{:S(2)}) collective-permute-start(bf16[1,128,768]{2,1,0:T(8,128)(2,1)} %maximum_bitcast_fusion.2), channel_id=1, source_target_pairs={{0,3},{1,2},{2,1},{3,0},{4,7},{5,6},{6,5},{7,4},{8,11},{9,10},{10,... | collective-permute-start | bytes 589832 | tf_op jit(solution)/shard_map/ppermute | solution.py:42
  13.5 102.6 %collective-permute-start.13 = (bf16[1,128,768]{2,1,0:T(8,128)(2,1)}, bf16[1,128,768]{2,1,0:T(8,128)(2,1)}, u32[]{:S(2)}, u32[]{:S(2)}) collective-permute-start(bf16[1,128,768]{2,1,0:T(8,128)(2,1)} %maximum_bitcast_fusion.3), channel_id=1, source_target_pairs={{0,3},{1,2},{2,1},{3,0},{4,7},{5,6},{6,5},{7,4},{8,11},{9,10},{10,... | collective-permute-start | bytes 589832 | tf_op jit(solution)/shard_map/ppermute | solution.py:42
  26.3 44.0 %collective-permute-start.4 = (bf16[1,288,768]{2,1,0:T(8,128)(2,1)}, bf16[1,288,768]{2,1,0:T(8,128)(2,1)}, u32[]{:S(2)}, u32[]{:S(2)}) collective-permute-start(bf16[1,288,768]{2,1,0:T(8,128)(2,1)} %maximum_bitcast_fusion), channel_id=1, source_target_pairs={{0,3},{1,2},{2,1},{3,0},{4,7},{5,6},{6,5},{7,4},{8,11},{9,10},{10,... | collective-permute-start | bytes 1327112 | tf_op jit(solution)/shard_map/ppermute | solution.py:42
  119.2 42.5 %collective-permute-start.23 = (bf16[6,144,768]{2,1,0:T(8,128)(2,1)S(1)}, bf16[6,144,768]{2,1,0:T(8,128)(2,1)S(1)}, u32[]{:S(2)}, u32[]{:S(2)}) collective-permute-start(bf16[6,144,768]{2,1,0:T(8,128)(2,1)S(1)} %pad_maximum_fusion.3.refs_3_.refs_5_), channel_id=1, source_target_pairs={{0,16},{4,20},{8,24},{12,28},{16,0},{20,4},{24,8},{28,12},{1,17},{... | collective-permute-start | bytes 3981320 | tf_op jit(solution)/shard_map/ppermute | solution.py:42
  119.8 43.1 %collective-permute-start.24 = (bf16[6,144,768]{2,1,0:T(8,128)(2,1)S(1)}, bf16[6,144,768]{2,1,0:T(8,128)(2,1)}, u32[]{:S(2)}, u32[]{:S(2)}) collective-permute-start(bf16[6,144,768]{2,1,0:T(8,128)(2,1)S(1)} %pad_maximum_fusion.4.refs_5_.refs_7_), channel_id=1, source_target_pairs={{0,8},{4,12},{8,0},{12,4},{16,24},{20,28},{24,16},{28,20},{1,9},{5... | collective-permute-start | bytes 3981320 | tf_op jit(solution)/shard_map/ppermute | solution.py:42
  126.1 31.0 %collective-permute-start.22 = (bf16[3,64,768]{2,1,0:T(8,128)(2,1)S(1)}, bf16[3,64,768]{2,1,0:T(8,128)(2,1)S(1)}, u32[]{:S(2)}, u32[]{:S(2)}) collective-permute-start(bf16[3,64,768]{2,1,0:T(8,128)(2,1)S(1)} %get-tuple-element.408), channel_id=1, source_target_pairs={{0,16},{4,20},{8,24},{12,28},{16,0},{20,4},{24,8},{28,12},{1,17},{... | collective-permute-start | bytes 884744 | tf_op jit(solution)/shard_map/ppermute | solution.py:42
  209.2 31.8 %collective-permute-start.37 = (bf16[6,144,768]{2,1,0:T(8,128)(2,1)}, bf16[6,144,768]{2,1,0:T(8,128)(2,1)S(1)}, u32[]{:S(2)}, u32[]{:S(2)}) collective-permute-start(bf16[6,144,768]{2,1,0:T(8,128)(2,1)} %pad_maximum_fusion.5.refs_4_), channel_id=1, source_target_pairs={{0,16},{4,20},{8,24},{12,28},{16,0},{20,4},{24,8},{28,12},{1,17},{... | collective-permute-start | bytes 3981320 | tf_op jit(solution)/shard_map/ppermute | solution.py:42
  210.0 32.0 %collective-permute-start.38 = (bf16[6,144,768]{2,1,0:T(8,128)(2,1)}, bf16[6,144,768]{2,1,0:T(8,128)(2,1)}, u32[]{:S(2)}, u32[]{:S(2)}) collective-permute-start(bf16[6,144,768]{2,1,0:T(8,128)(2,1)} %pad_maximum_fusion.6.refs_6_), channel_id=1, source_target_pairs={{0,8},{4,12},{8,0},{12,4},{16,24},{20,28},{24,16},{28,20},{1,9},{5... | collective-permute-start | bytes 3981320 | tf_op jit(solution)/shard_map/ppermute | solution.py:42
  274.0 41.3 %collective-permute-start.41 = (bf16[8,144,768]{2,1,0:T(8,128)(2,1)}, bf16[8,144,768]{2,1,0:T(8,128)(2,1)}, u32[]{:S(2)}, u32[]{:S(2)}) collective-permute-start(bf16[8,144,768]{2,1,0:T(8,128)(2,1)} %get-tuple-element.172), channel_id=1, source_target_pairs={{0,8},{4,12},{8,0},{12,4},{16,24},{20,28},{24,16},{28,20},{1,9},{5... | collective-permute-start | bytes 5308424 | tf_op jit(solution)/shard_map/ppermute | solution.py:42
  275.7 42.9 %collective-permute-start.44 = (bf16[8,144,768]{2,1,0:T(8,128)(2,1)}, bf16[8,144,768]{2,1,0:T(8,128)(2,1)}, u32[]{:S(2)}, u32[]{:S(2)}) collective-permute-start(bf16[8,144,768]{2,1,0:T(8,128)(2,1)} %get-tuple-element.173), channel_id=1, source_target_pairs={{0,16},{4,20},{8,24},{12,28},{16,0},{20,4},{24,8},{28,12},{1,17},{... | collective-permute-start | bytes 5308424 | tf_op jit(solution)/shard_map/ppermute | solution.py:42
  305.4 46.1 %collective-permute-start.52 = (bf16[8,128,768]{2,1,0:T(8,128)(2,1)}, bf16[8,128,768]{2,1,0:T(8,128)(2,1)}, u32[]{:S(2)}, u32[]{:S(2)}) collective-permute-start(bf16[8,128,768]{2,1,0:T(8,128)(2,1)} %get-tuple-element.180), channel_id=1, source_target_pairs={{0,1},{1,0},{2,3},{3,2},{4,5},{5,4},{6,7},{7,6},{8,9},{9,8},{10,11... | collective-permute-start | bytes 4718600 | tf_op jit(solution)/shard_map/ppermute | solution.py:42
  355.6 41.7 %collective-permute-start.51 = (bf16[8,144,768]{2,1,0:T(8,128)(2,1)}, bf16[8,144,768]{2,1,0:T(8,128)(2,1)}, u32[]{:S(2)}, u32[]{:S(2)}) collective-permute-start(bf16[8,144,768]{2,1,0:T(8,128)(2,1)} %get-tuple-element.193), channel_id=1, source_target_pairs={{0,8},{4,12},{8,0},{12,4},{16,24},{20,28},{24,16},{28,20},{1,9},{5... | collective-permute-start | bytes 5308424 | tf_op jit(solution)/shard_map/ppermute | solution.py:42
  356.0 41.1 %collective-permute-start.55 = (bf16[8,144,768]{2,1,0:T(8,128)(2,1)}, bf16[8,144,768]{2,1,0:T(8,128)(2,1)}, u32[]{:S(2)}, u32[]{:S(2)}) collective-permute-start(bf16[8,144,768]{2,1,0:T(8,128)(2,1)} %get-tuple-element.196), channel_id=1, source_target_pairs={{0,16},{4,20},{8,24},{12,28},{16,0},{20,4},{24,8},{28,12},{1,17},{... | collective-permute-start | bytes 5308424 | tf_op jit(solution)/shard_map/ppermute | solution.py:42
  359.8 46.1 %collective-permute-start.45 = (bf16[2,192,384]{2,1,0:T(8,128)(2,1)}, bf16[2,192,384]{2,1,0:T(8,128)(2,1)S(1)}, u32[]{:S(2)}, u32[]{:S(2)}) collective-permute-start(bf16[2,192,384]{2,1,0:T(8,128)(2,1)} %pad_maximum_fusion.46), channel_id=1, source_target_pairs={{0,1},{1,0},{2,3},{3,2},{4,5},{5,4},{6,7},{7,6},{8,9},{9,8},{10,11... | collective-permute-start | bytes 884744 | tf_op jit(solution)/shard_map/ppermute | solution.py:42
  359.9 43.8 %collective-permute-start.50 = (bf16[2,288,768]{2,1,0:T(8,128)(2,1)S(1)}, bf16[2,288,768]{2,1,0:T(8,128)(2,1)S(1)}, u32[]{:S(2)}, u32[]{:S(2)}) collective-permute-start(bf16[2,288,768]{2,1,0:T(8,128)(2,1)S(1)} %pad_maximum_fusion.16), channel_id=1, source_target_pairs={{0,1},{1,0},{2,3},{3,2},{4,5},{5,4},{6,7},{7,6},{8,9},{9,8},{10,11... | collective-permute-start | bytes 2654216 | tf_op jit(solution)/shard_map/ppermute | solution.py:42
  361.9 52.2 %collective-permute-start.59 = (bf16[4,128,768]{2,1,0:T(8,128)(2,1)}, bf16[4,128,768]{2,1,0:T(8,128)(2,1)}, u32[]{:S(2)}, u32[]{:S(2)}) collective-permute-start(bf16[4,128,768]{2,1,0:T(8,128)(2,1)} %slice.588), channel_id=1, source_target_pairs={{0,8},{4,12},{8,0},{12,4},{16,24},{20,28},{24,16},{28,20},{1,9},{5... | collective-permute-start | bytes 2359304 | tf_op jit(solution)/shard_map/ppermute | solution.py:42
  397.1 51.3 %collective-permute-start.62 = (bf16[8,128,768]{2,1,0:T(8,128)(2,1)}, bf16[8,128,768]{2,1,0:T(8,128)(2,1)}, u32[]{:S(2)}, u32[]{:S(2)}) collective-permute-start(bf16[8,128,768]{2,1,0:T(8,128)(2,1)} %get-tuple-element.202), channel_id=1, source_target_pairs={{0,1},{1,0},{2,3},{3,2},{4,5},{5,4},{6,7},{7,6},{8,9},{9,8},{10,11... | collective-permute-start | bytes 4718600 | tf_op jit(solution)/shard_map/ppermute | solution.py:42
  400.0 32.7 %collective-permute-start.60 = (bf16[4,144,768]{2,1,0:T(8,128)(2,1)}, bf16[4,144,768]{2,1,0:T(8,128)(2,1)}, u32[]{:S(2)}, u32[]{:S(2)}) collective-permute-start(bf16[4,144,768]{2,1,0:T(8,128)(2,1)} %add_convert_fusion.8), channel_id=1, source_target_pairs={{0,8},{4,12},{8,0},{12,4},{16,24},{20,28},{24,16},{28,20},{1,9},{5... | collective-permute-start | bytes 2654216 | tf_op jit(solution)/shard_map/ppermute | solution.py:42
  414.1 32.1 %collective-permute-start.56 = (bf16[2,192,256]{2,1,0:T(8,128)(2,1)}, bf16[2,192,256]{2,1,0:T(8,128)(2,1)}, u32[]{:S(2)}, u32[]{:S(2)}) collective-permute-start(bf16[2,192,256]{2,1,0:T(8,128)(2,1)} %get-tuple-element.425), channel_id=1, source_target_pairs={{0,4},{4,0},{8,12},{12,8},{16,20},{20,16},{24,28},{28,24},{1,5},{5... | collective-permute-start | bytes 589832 | tf_op jit(solution)/shard_map/ppermute | solution.py:42
  437.9 38.8 %collective-permute-start.68 = (bf16[2,288,768]{2,1,0:T(8,128)(2,1)S(1)}, bf16[2,288,768]{2,1,0:T(8,128)(2,1)S(1)}, u32[]{:S(2)}, u32[]{:S(2)}) collective-permute-start(bf16[2,288,768]{2,1,0:T(8,128)(2,1)S(1)} %fusion.16), channel_id=1, source_target_pairs={{0,1},{1,0},{2,3},{3,2},{4,5},{5,4},{6,7},{7,6},{8,9},{9,8},{10,11... | collective-permute-start | bytes 2654216 | tf_op jit(solution)/shard_map/ppermute | solution.py:42
  444.6 32.3 %collective-permute-start.67 = (bf16[1,288,768]{2,1,0:T(8,128)(2,1)S(1)}, bf16[1,288,768]{2,1,0:T(8,128)(2,1)S(1)}, u32[]{:S(2)}, u32[]{:S(2)}) collective-permute-start(bf16[1,288,768]{2,1,0:T(8,128)(2,1)S(1)} %add_convert_fusion.17), channel_id=1, source_target_pairs={{0,8},{4,12},{8,0},{12,4},{16,24},{20,28},{24,16},{28,20},{1,9},{5... | collective-permute-start | bytes 1327112 | tf_op jit(solution)/shard_map/ppermute | solution.py:42
  452.1 33.5 %collective-permute-start.63 = (bf16[2,192,512]{2,1,0:T(8,128)(2,1)S(1)}, bf16[2,192,512]{2,1,0:T(8,128)(2,1)S(1)}, u32[]{:S(2)}, u32[]{:S(2)}) collective-permute-start(bf16[2,192,512]{2,1,0:T(8,128)(2,1)S(1)} %pad_maximum_fusion.40), channel_id=1, source_target_pairs={{0,3},{1,2},{2,1},{3,0},{4,7},{5,6},{6,5},{7,4},{8,11},{9,10},{10,... | collective-permute-start | bytes 1179656 | tf_op jit(solution)/shard_map/ppermute | solution.py:42
  (136 other events, 1386.5 us)
